TPU v7x, 32 devices: a whole 2x2x4 slice. The times are simulated.
32 devices in a mesh: grp: 2 (over y), mom: 16 (over z, x, core).
Axes of the slice: x: 2, y: 2, z: 4, core: 2. Of those that a mesh axis runs over, the one named last changes fastest.
Arguments:
- lesser: bfloat16 [4, 1, 64, 256, 512], P('grp', None, 'mom'), may hold values from -6 to 6
- greater: bfloat16 [4, 1, 64, 256, 512], P('grp', None, 'mom'), may hold values from -6 to 6
- coupling: float32 [4, 4, 64], replicated, may hold values from 0.002 to 0.2
- occupation: float32 [4], replicated, may hold values from 0.1 to 2
- shift: int32 [4], replicated, may hold values from 1 to 2, as said below
- region_map: int32 [1], replicated, may hold values from 0 to 3
Outputs:
- lesser_self: bfloat16 [4, 1, 64, 256, 512], P('grp', None, 'mom')
- greater_self: bfloat16 [4, 1, 64, 256, 512], P('grp', None, 'mom')
Inputs may be any that keep to these rules, and one draw needn't show every extreme that they name: Some mode has shift 2.
All inputs are finite; a program needn't handle non-finite values.
Results may differ from a plain program's by a relative error of at most 0.0053.
Values may be sent and summed in bfloat16 or wider, within the bound.
No kernel may reach another device: no remote copies, remote signals or barrier semaphores. Data moves between devices by JAX's collectives and lax.ppermute only.
A program may use at most 128 MiB of HBM per device.

v0:
```python
import math

import jax
import jax.numpy as jnp
from jax import lax
from jax.sharding import PartitionSpec as P

SMAX = 2


def with_halo(shard, sides, width):
    for axis, dim in sides:
        size, length = (lax.axis_size(axis), shard.shape[dim])
        up = [(i, (i + 1) % size) for i in range(size - 1)]
        down = [(j, i) for i, j in up]
        last = lax.slice_in_dim(shard, length - width, length, axis=dim)
        first = lax.slice_in_dim(shard, 0, width, axis=dim)
        before = lax.ppermute(last, axis, up)
        after = lax.ppermute(first, axis, down)
        shard = jnp.concatenate([before, shard, after], axis=dim)
    return shard


def dft_basis(points):
    row_index = lax.broadcasted_iota(jnp.int32, (points, points), 0)
    col_index = lax.broadcasted_iota(jnp.int32, (points, points), 1)
    angles = (row_index * col_index % points).astype(jnp.float32) * (2.0 * math.pi / points)
    return jnp.concatenate([jnp.cos(angles), jnp.sin(angles)], axis=0)


def coupling_spectrum(coupling, region_map, basis):
    regions = coupling.shape[0]
    points = coupling.shape[2]
    onehot = (region_map[:, None] == jnp.arange(regions, dtype=jnp.int32)[None, :]).astype(
        jnp.float32
    )
    chosen = jnp.einsum("br,rmq->bmq", onehot, coupling, precision=lax.Precision.HIGHEST)
    spectrum = jnp.einsum("pq,bmq->bmp", basis, chosen, precision=lax.Precision.HIGHEST)
    return (spectrum[:, :, :points], -spectrum[:, :, points:])


def forward(stacked, basis_low):
    points = stacked.shape[3]
    columns = stacked.shape[5] // 2
    mixture = jnp.einsum(
        "pk,aebkxw->aebpxw", basis_low, stacked, preferred_element_type=jnp.float32
    )
    cosine = mixture[:, :, :, :points]
    sine = mixture[:, :, :, points:]
    return (
        cosine[..., :columns] + sine[..., columns:],
        cosine[..., columns:] - sine[..., :columns],
    )


def combine(hat_real, hat_imag, spec_real, spec_imag, occupation, shift, energies):
    out_shape = (2, energies) + hat_real.shape[2:]
    sigma_real = jnp.zeros(out_shape, jnp.float32)
    sigma_imag = jnp.zeros(out_shape, jnp.float32)
    points = spec_real.shape[2]
    for phonon in range(occupation.shape[0]):
        offset = shift[phonon]
        filling = occupation[phonon]
        lower_real = lax.dynamic_slice_in_dim(hat_real, SMAX - offset, energies, 1)
        lower_imag = lax.dynamic_slice_in_dim(hat_imag, SMAX - offset, energies, 1)
        upper_real = lax.dynamic_slice_in_dim(hat_real, SMAX + offset, energies, 1)
        upper_imag = lax.dynamic_slice_in_dim(hat_imag, SMAX + offset, energies, 1)
        weight_low = jnp.stack([filling, filling + 1.0]).reshape(2, 1, 1, 1, 1, 1)
        weight_high = jnp.stack([filling + 1.0, filling]).reshape(2, 1, 1, 1, 1, 1)
        mixed_real = weight_low * lower_real + weight_high * upper_real
        mixed_imag = weight_low * lower_imag + weight_high * upper_imag
        factor_real = spec_real[:, phonon, :].reshape(1, 1, -1, points, 1, 1)
        factor_imag = spec_imag[:, phonon, :].reshape(1, 1, -1, points, 1, 1)
        sigma_real = sigma_real + factor_real * mixed_real - factor_imag * mixed_imag
        sigma_imag = sigma_imag + factor_real * mixed_imag + factor_imag * mixed_real
    return (sigma_real, sigma_imag)


def inverse(sigma_real, sigma_imag, basis_low):
    points = sigma_real.shape[3]
    columns = sigma_real.shape[5]
    spectral = jnp.concatenate([sigma_real, sigma_imag], axis=-1).astype(jnp.bfloat16)
    mixture = jnp.einsum(
        "pk,aebkxw->aebpxw", basis_low, spectral, preferred_element_type=jnp.float32
    )
    cosine = mixture[:, :, :, :points]
    sine = mixture[:, :, :, points:]
    real_part = cosine[..., :columns] - sine[..., columns:]
    imag_part = cosine[..., columns:] + sine[..., :columns]
    return (jnp.concatenate([real_part, imag_part], axis=-1) * (1.0 / points)).astype(jnp.bfloat16)


def on_device(lesser, greater, coupling, occupation, shift, region_map):
    stacked = jnp.stack([lesser, greater])
    widened = with_halo(stacked, (("grp", 1),), SMAX)
    regrouped = lax.all_to_all(widened, "mom", split_axis=4, concat_axis=3, tiled=True)
    points = regrouped.shape[3]
    basis = dft_basis(points)
    basis_low = basis.astype(jnp.bfloat16)
    spec_real, spec_imag = coupling_spectrum(coupling, region_map, basis)
    hat_real, hat_imag = forward(regrouped, basis_low)
    sigma_real, sigma_imag = combine(
        hat_real, hat_imag, spec_real, spec_imag, occupation, shift, lesser.shape[0]
    )
    result = inverse(sigma_real, sigma_imag, basis_low)
    returned = lax.all_to_all(result, "mom", split_axis=3, concat_axis=4, tiled=True)
    return (returned[0], returned[1])


def solution(mesh):
    return jax.shard_map(
        on_device,
        mesh=mesh,
        in_specs=(
            P("grp", None, "mom", None, None),
            P("grp", None, "mom", None, None),
            P(),
            P(),
            P(),
            P(),
        ),
        out_specs=(P("grp", None, "mom", None, None), P("grp", None, "mom", None, None)),
        check_vma=False,
    )
```

profile of v0, /device:TPU:0, one launch (start us, length us, event | category | flops | bytes accessed | tf_op | source)
XLA Modules:
  0.0 636.4 jit_solution(203095934510335000)
XLA Ops:
  0.6 0.0 copy-start
  0.6 5.9 copy_bitcast_fusion.1
  6.6 2.7 pad_maximum_fusion.1
  9.3 1.3 collective-permute-start.1
  10.6 5.4 collective-permute-start
  16.0 88.1 %collective-permute-done.1 = bf16[2,2,1,4,256,512]{5,3,1,2,0,4:T(4,128)(2,1)S(1)} collective-permute-done((bf16[2,2,1,4,256,512]{5,3,1,2,0,4:T(4,128)(2,1)S(1)}, bf16[2,2,1,4,256,512]{5,3,1,2,0,4:T(4,128)(2,1)S(1)}, u32[]{:S(2)}, u32[]{:S(2)}) %collective-permute-start.1) | collective-permute-done | bytes 4194336 | tf_op jit(solution)/shard_map/ppermute | solution.py:19
  104.1 1.4 collective-permute-done
  105.6 10.7 %pad_maximum_fusion = bf16[2,6,1,4,256,512]{5,3,1,2,0,4:T(4,128)(2,1)} fusion(bf16[2,2,1,4,256,512]{5,3,1,2,0,4:T(4,128)(2,1)S(1)} %collective-permute-done.1, bf16[1,2,1,4,256,512]{5,3,1,2,0,4:T(4,128)(2,1)S(1)} %get-tuple-element.26, bf16[1,2,1,4,256,512]{5,3,1,2,0,4:T(4,128)(2,1)S(1)} %get-tuple-element.27, ...), kind=kLoop, calls=%fused_computation.3 | loop fusion | flops 18874368 | bytes 25165824 | tf_op jit(solution)/shard_map/concatenate | solution.py:20
  116.3 0.0 copy-start.3
  116.3 0.0 copy-start.4
  116.3 6.9 %all-to-all-start = ((bf16[2,6,1,4,256,512]{5,3,1,2,0,4:T(4,128)(2,1)}), bf16[2,6,1,4,256,512]{5,3,1,2,0,4:T(4,128)(2,1)}, u32[]{:S(2)}, u32[]{:S(2)}) async-start(bf16[2,6,1,4,256,512]{5,3,1,2,0,4:T(4,128)(2,1)} %pad_maximum_fusion), calls=%async_computation | async-start | bytes 25165824 | tf_op jit(solution)/shard_map/all_to_all | solution.py:96
  123.2 0.0 copy-done.3
  123.2 0.7 fusion.27
  134.7 0.0 copy-done.4
  134.7 0.6 fusion.26
  137.7 0.6 pad_maximum_fusion.4
  138.3 0.6 pad_maximum_fusion.6
  138.9 0.6 pad_maximum_fusion.8
  139.6 0.7 pad_maximum_fusion.10
  140.3 0.1 fusion.14
  140.4 0.1 fusion.16
  140.5 0.0 copy-done
  140.5 0.1 fusion.17
  140.6 0.2 convolution_bitcast_fusion.2
  140.9 0.1 slice_negate_fusion
  141.0 206.0 %all-to-all-done = bf16[2,6,1,4,256,512]{5,3,1,2,0,4:T(4,128)(2,1)} async-done(((bf16[2,6,1,4,256,512]{5,3,1,2,0,4:T(4,128)(2,1)}), bf16[2,6,1,4,256,512]{5,3,1,2,0,4:T(4,128)(2,1)}, u32[]{:S(2)}, u32[]{:S(2)}) %all-to-all-start) | async-done | bytes 12582944 | tf_op jit(solution)/shard_map/all_to_all | solution.py:96
  347.0 11.6 %copy.25 = bf16[2,6,1,4,16,16,512]{6,3,4,5,1,0,2:T(4,128)(2,1)} copy(bf16[2,6,1,4,16,16,512]{6,3,1,0,5,4,2:T(4,128)(2,1)} %bitcast.8) | data formatting | bytes 25165824 | tf_op jit(solution)/shard_map/all_to_all | solution.py:96
  358.5 18.1 %reshape.171 = bf16[2,6,64,16,512]{4,2,3,1,0:T(8,128)(2,1)} reshape(bf16[2,6,1,16,4,16,512]{6,4,3,5,1,0,2:T(4,128)(2,1)} %bitcast.77) | data formatting | bytes 25165824 | tf_op jit(solution)/shard_map/reshape.7
  376.6 21.9 %convolution_bitcast_fusion = f32[2,6,1,128,16,512]{5,3,4,1,0,2:T(8,128)} fusion(bf16[2,6,64,16,512]{4,2,3,1,0:T(8,128)(2,1)} %reshape.171, bf16[128,64]{0,1:T(8,128)(2,1)S(1)} %fusion.16), kind=kOutput, calls=%fused_computation | convolution fusion | flops 1610612736 | bytes 62930944 | tf_op jit(solution)/shard_map/pk,aebkxw->aebpxw/dot_general | solution.py:45
  398.6 27.6 %slice_subtract_fusion = (f32[2,6,1,64,16,256]{5,3,4,1,0,2:T(8,128)}, f32[2,6,1,64,16,256]{5,3,4,1,0,2:T(8,128)}) fusion(f32[2,6,1,128,16,512]{5,3,4,1,0,2:T(8,128)} %convolution_bitcast_fusion), kind=kLoop, calls=%fused_computation.1 | loop fusion | flops 6291456 | bytes 75497472 | tf_op jit(solution)/shard_map/sub | solution.py:52
  426.2 0.0 copy-start.2
  426.2 24.2 %fusion.5 = bf16[2,2,64,16,256]{4,2,3,1,0:T(8,128)(2,1)S(1)} fusion(f32[64]{0:T(128)S(1)} %get-tuple-element.13, f32[64]{0:T(128)S(1)} %get-tuple-element.9, f32[64]{0:T(128)S(1)} %get-tuple-element.14, f32[64]{0:T(128)S(1)} %get-tuple-element.10, f32[64]{0:T(128)S(1)} %get-tuple-element.15, f32[64]{0:T(128)S(1)} %get-tuple-element.11, ...), kind=kLoop, calls=%fused_computation.27 | loop fusion | flops 41943040 | bytes 69208160 | tf_op jit(solution)/shard_map/concatenate | solution.py:82
  450.4 0.0 copy-done.2
  450.4 13.2 %fusion.4 = bf16[2,2,64,16,256]{4,2,3,1,0:T(8,128)(2,1)S(1)} fusion(f32[64]{0:T(128)S(1)} %get-tuple-element.13, f32[64]{0:T(128)S(1)} %get-tuple-element.9, f32[64]{0:T(128)S(1)} %get-tuple-element.14, f32[64]{0:T(128)S(1)} %get-tuple-element.10, f32[64]{0:T(128)S(1)} %get-tuple-element.15, f32[64]{0:T(128)S(1)} %get-tuple-element.11, ...), kind=kLoop, calls=%fused_computation.26 | loop fusion | flops 41943040 | bytes 69208160 | tf_op jit(solution)/shard_map/concatenate | solution.py:82
  463.6 8.2 %convolution_bitcast_fusion.1 = f32[2,2,1,128,16,512]{5,3,4,1,0,2:T(8,128)} fusion(bf16[2,2,64,16,256]{4,2,3,1,0:T(8,128)(2,1)S(1)} %fusion.5, bf16[2,2,64,16,256]{4,2,3,1,0:T(8,128)(2,1)S(1)} %fusion.4, bf16[128,64]{0,1:T(8,128)(2,1)S(1)} %fusion.16), kind=kOutput, calls=%fused_computation.7 | convolution fusion | flops 545259520 | bytes 20987904 | tf_op jit(solution)/shard_map/pk,aebkxw->aebpxw/dot_general | solution.py:83
  471.8 10.2 %slice_subtract_fusion.1 = (f32[2,2,1,64,16,256]{5,3,4,1,0,2:T(8,128)S(1)}, f32[2,2,1,64,16,256]{5,3,4,1,0,2:T(8,128)}) fusion(f32[2,2,1,128,16,512]{5,3,4,1,0,2:T(8,128)} %convolution_bitcast_fusion.1), kind=kLoop, calls=%fused_computation.9 | loop fusion | flops 2097152 | bytes 25165824 | tf_op jit(solution)/shard_map/sub | solution.py:88
  482.0 2.8 fusion
  484.8 2.3 copy.14
  487.2 145.4 %all_to_all.30 = bf16[2,2,1,64,16,512]{5,4,1,0,2,3:T(8,128)(2,1)S(1)} all-to-all(bf16[2,2,1,64,16,512]{5,4,1,0,2,3:T(8,128)(2,1)S(1)} %copy.14), channel_id=1, replica_groups=mesh['grp'=2,'mom'=16] {'mom'}, dimensions={3} | all-to-all | bytes 8388608 | tf_op jit(solution)/shard_map/all_to_all | solution.py:106
  632.6 0.8 fusion.25
  633.4 0.0 copy-start.1
  633.4 1.5 copy.15
  634.9 1.5 copy.16
  636.4 0.0 copy-done.1
  (2 shorter events, 0.0 us)
Async XLA Ops:
  0.6 139.9 %copy-start = (f32[4,4,64]{2,1,0:T(4,128)S(1)}, f32[4,4,64]{2,1,0:T(4,128)}, u32[]{:S(2)}) copy-start(f32[4,4,64]{2,1,0:T(4,128)} %param.8) | copy-start | bytes 12292
  9.3 94.8 %collective-permute-start.1 = (bf16[2,2,1,4,256,512]{5,3,1,2,0,4:T(4,128)(2,1)S(1)}, bf16[2,2,1,4,256,512]{5,3,1,2,0,4:T(4,128)(2,1)S(1)}, u32[]{:S(2)}, u32[]{:S(2)}) collective-permute-start(bf16[2,2,1,4,256,512]{5,3,1,2,0,4:T(4,128)(2,1)S(1)} %pad_maximum_fusion.1), channel_id=1, source_target_pairs={{16,0},{17,1},{18,2},{19,3},{20,4},{21,5},{22,6},{23,7},{24,8},{25... | collective-permute-start | bytes 12582920 | tf_op jit(solution)/shard_map/ppermute | solution.py:19
  10.6 95.0 %collective-permute-start = (bf16[2,2,1,4,256,512]{5,3,1,2,0,4:T(4,128)(2,1)S(1)}, bf16[2,2,1,4,256,512]{5,3,1,2,0,4:T(4,128)(2,1)S(1)}, u32[]{:S(2)}, u32[]{:S(2)}) collective-permute-start(bf16[2,2,1,4,256,512]{5,3,1,2,0,4:T(4,128)(2,1)S(1)} %pad_maximum_fusion.1), channel_id=1, source_target_pairs={{0,16},{1,17},{2,18},{3,19},{4,20},{5,21},{6,22},{7,23},{8,24},{9,... | collective-permute-start | bytes 12582920 | tf_op jit(solution)/shard_map/ppermute | solution.py:18
  116.3 6.9 %copy-start.3 = (s32[4]{0:T(128)S(1)}, s32[4]{0:T(128)}, u32[]{:S(2)}) copy-start(s32[4]{0:T(128)} %param.10) | copy-start | bytes 52
  116.3 18.4 %copy-start.4 = (f32[4]{0:T(128)S(1)}, f32[4]{0:T(128)}, u32[]{:S(2)}) copy-start(f32[4]{0:T(128)} %param.9) | copy-start | bytes 52
  116.3 230.7 %all-to-all-start = ((bf16[2,6,1,4,256,512]{5,3,1,2,0,4:T(4,128)(2,1)}), bf16[2,6,1,4,256,512]{5,3,1,2,0,4:T(4,128)(2,1)}, u32[]{:S(2)}, u32[]{:S(2)}) async-start(bf16[2,6,1,4,256,512]{5,3,1,2,0,4:T(4,128)(2,1)} %pad_maximum_fusion), calls=%async_computation | async-start | bytes 25165824 | tf_op jit(solution)/shard_map/all_to_all | solution.py:96
  426.2 24.2 %copy-start.2 = (f32[2,6,1,64,16,256]{5,3,4,1,0,2:T(8,128)S(1)}, f32[2,6,1,64,16,256]{5,3,4,1,0,2:T(8,128)}, u32[]{:S(2)}) copy-start(f32[2,6,1,64,16,256]{5,3,4,1,0,2:T(8,128)} %get-tuple-element.2) | copy-start | bytes 37748740
  633.4 3.0 copy-start.1
where the time goes:
time: 638 us; the launch traced here: 636 us
  waiting for transfers between devices  296 us (46%)
  blocking collectives  145 us (23%)
  other arithmetic  94.3 us (15%)
  local copies, waits for them, and re-layouts  43.1 us (7%)
  matrix products  30.5 us (5%)
  between operations  13.9 us (2%)
  starting transfers between devices  13.6 us (2%)
    all_to_all x1, waiting for transfers between devices, on_device(): lax.all_to_all(widened, 'mom', split_axis=4, concat_axis=3, tiled=True)  206 us
    all_to_all x1, blocking collectives, on_device(): lax.all_to_all(result, 'mom', split_axis=3, concat_axis=4, tiled=True)  145 us
    ppermute x1, waiting for transfers between devices, with_halo(): after = lax.ppermute(first, axis, down)  88.1 us
    concatenate x2, other arithmetic, inverse(): jnp.concatenate([sigma_real, sigma_imag], axis=-1).astype(jnp.bfloat16)  37.4 us
    sub x1, other arithmetic, forward(): cosine[..., columns:] - sine[..., :columns]  27.6 us
    dot_general x1, matrix products, forward(): jnp.einsum('pk,aebkxw->aebpxw', basis_low, stacked, preferred_element_typ...  21.9 us
    another operation x1, local copies, waits for them, and re-layouts  18.1 us
  transfers between devices with their start and end apart: 3, of which 3 were waited for; matrix products, arithmetic and copies ran while one was open for 1% of the time, Pallas kernels for 0%

commit v1 on v0

--- a/solution.py
+++ b/solution.py
@@ -1,11 +1,191 @@
+import functools
 import math
 
 import jax
 import jax.numpy as jnp
+import numpy as np
 from jax import lax
+from jax.experimental import pallas as pl
+from jax.experimental.pallas import tpu as pltpu
 from jax.sharding import PartitionSpec as P
 
 SMAX = 2
+TILE = 16
+VMEM_BYTES = 40 * 1024 * 1024
+APART = 1 << 16
+
+
+def permutation(energies, momenta, rows):
+    inner = energies * momenta
+    size = inner * rows
+    matrix = np.zeros((size, size), np.float32)
+    for state in range(inner):
+        for row in range(rows):
+            matrix[row * inner + state, state * rows + row] = 1.0
+    return matrix
+
+
+def pack_kernel(perm_ref, lesser_ref, greater_ref, out_ref):
+    for side, ref in enumerate((lesser_ref, greater_ref)):
+        for piece in range(out_ref.shape[1]):
+            rows = out_ref.shape[2] // (ref.shape[0] * ref.shape[2])
+            block = ref[:, :, :, piece * rows : (piece + 1) * rows, :]
+            block = block.reshape(out_ref.shape[2], out_ref.shape[3])
+            moved = jnp.dot(perm_ref[...], block, preferred_element_type=jnp.float32)
+            out_ref[side, piece] = moved.astype(out_ref.dtype)
+
+
+def unpack_kernel(perm_ref, in_ref, lesser_ref, greater_ref):
+    for side, ref in enumerate((lesser_ref, greater_ref)):
+        for piece in range(in_ref.shape[1]):
+            rows = in_ref.shape[2] // (ref.shape[0] * ref.shape[2])
+            moved = jnp.dot(
+                perm_ref[...], in_ref[side, piece], preferred_element_type=jnp.float32
+            )
+            moved = moved.astype(ref.dtype).reshape(
+                ref.shape[0], 1, ref.shape[2], rows, ref.shape[4]
+            )
+            ref[:, :, :, piece * rows : (piece + 1) * rows, :] = moved
+
+
+def mix_kernel(matrix_ref, in_ref, out_ref):
+    devices, rows, columns = in_ref.shape
+    block = in_ref[...].reshape(devices * rows, columns)
+    mixed = jnp.dot(matrix_ref[...], block, preferred_element_type=jnp.float32)
+    out_ref[...] = mixed.astype(out_ref.dtype).reshape(devices, rows, columns)
+
+
+def build_kernel(
+    region_ref, side_ref, shift_ref, occupation_ref, coupling_ref, pick_ref, down_ref, across_ref, out_ref
+):
+    points = pick_ref.shape[1]
+    modes = coupling_ref.shape[1]
+    chosen = coupling_ref[region_ref[0]]
+    greater = side_ref[0].astype(jnp.float32)
+    apart = down_ref[...] - across_ref[...]
+    total = jnp.zeros(out_ref.shape, jnp.float32)
+    for step in range(-SMAX, SMAX + 1):
+        if step == 0:
+            continue
+        row = jnp.zeros((1, 2 * points), jnp.float32)
+        for mode in range(modes):
+            filling = occupation_ref[mode] + (greater if step > 0 else 1.0 - greater)
+            weight = jnp.where(shift_ref[mode] == abs(step), filling, 0.0)
+            row = row + weight * chosen[mode : mode + 1, :]
+        wide = jnp.broadcast_to(row, (points, 2 * points))
+        turned = pltpu.roll(wide, 0, 1, stride=1, stride_axis=0)[:, :points]
+        half = jnp.dot(
+            pick_ref[...], turned.astype(jnp.bfloat16), preferred_element_type=jnp.float32
+        ).astype(jnp.bfloat16)
+        full = lax.dot_general(
+            pick_ref[...], half, (((1,), (1,)), ((), ())), preferred_element_type=jnp.float32
+        )
+        total = jnp.where(apart == step, full, total)
+    out_ref[...] = total.astype(out_ref.dtype)
+
+
+def params():
+    return pltpu.CompilerParams(vmem_limit_bytes=VMEM_BYTES)
+
+
+def build(coupling, occupation, shift, region_map, side, groups, shares, energies, momenta, fold):
+    devices = groups * shares
+    points = shares * momenta
+    group, share, row, energy, momentum = np.unravel_index(
+        np.arange(devices * fold * energies * momenta), (groups, shares, fold, energies, momenta)
+    )
+    code = (row * APART + group * energies + energy).astype(np.int32)
+    pick = (share * momenta + momentum)[:, None] == np.arange(points)[None, :]
+    size = code.size
+    scalars = pl.BlockSpec(memory_space=pltpu.SMEM)
+    vectors = pl.BlockSpec(memory_space=pltpu.VMEM)
+    return pl.pallas_call(
+        build_kernel,
+        out_shape=jax.ShapeDtypeStruct((size, size), jnp.bfloat16),
+        in_specs=[scalars] * 4 + [vectors] * 4,
+        out_specs=vectors,
+        compiler_params=params(),
+        name="build",
+    )(
+        region_map,
+        side.reshape(1),
+        shift,
+        occupation,
+        jnp.concatenate([coupling, coupling], axis=2),
+        jnp.asarray(pick, jnp.bfloat16),
+        jnp.asarray(code[:, None]),
+        jnp.asarray(code[None, :]),
+    )
+
+
+def pack(lesser, greater, pieces, rows, batch):
+    energies, _, momenta, _, columns = lesser.shape
+    size = energies * momenta * rows
+    perm = jnp.asarray(permutation(energies, momenta, rows), jnp.bfloat16)
+    slab = pl.BlockSpec((energies, 1, momenta, batch * rows, columns), lambda i: (0, 0, 0, i, 0))
+    return pl.pallas_call(
+        pack_kernel,
+        grid=(pieces // batch,),
+        out_shape=jax.ShapeDtypeStruct((2, pieces, size, columns), lesser.dtype),
+        in_specs=[pl.BlockSpec((size, size), lambda i: (0, 0)), slab, slab],
+        out_specs=pl.BlockSpec((2, batch, size, columns), lambda i: (0, i, 0, 0)),
+        compiler_params=params(),
+        name="pack",
+    )(perm, lesser, greater)
+
+
+def unpack(packed, shape, pieces, rows, batch):
+    energies, _, momenta, _, columns = shape
+    size = energies * momenta * rows
+    perm = jnp.asarray(permutation(energies, momenta, rows).T, jnp.bfloat16)
+    slab = pl.BlockSpec((energies, 1, momenta, batch * rows, columns), lambda i: (0, 0, 0, i, 0))
+    out = jax.ShapeDtypeStruct(shape, packed.dtype)
+    return pl.pallas_call(
+        unpack_kernel,
+        grid=(pieces // batch,),
+        out_shape=(out, out),
+        in_specs=[
+            pl.BlockSpec((size, size), lambda i: (0, 0)),
+            pl.BlockSpec((2, batch, size, columns), lambda i: (0, i, 0, 0)),
+        ],
+        out_specs=(slab, slab),
+        compiler_params=params(),
+        name="unpack",
+    )(perm, packed)
+
+
+def mix(matrix, received):
+    devices, size, columns = received.shape
+    block = pl.BlockSpec((devices, TILE, columns), lambda i: (0, i, 0))
+    return pl.pallas_call(
+        mix_kernel,
+        grid=(size // TILE,),
+        out_shape=jax.ShapeDtypeStruct(received.shape, received.dtype),
+        in_specs=[pl.BlockSpec(matrix.shape, lambda i: (0, 0)), block],
+        out_specs=block,
+        compiler_params=params(),
+        name="mix",
+    )(matrix, received)
+
+
+def by_rows(lesser, greater, coupling, occupation, shift, region_map, groups, shares):
+    energies, _, momenta, height, columns = lesser.shape
+    devices = groups * shares
+    pieces = devices // 2
+    rows = height // pieces
+    batch = 2 if pieces % 2 == 0 else 1
+    side = (lax.axis_index(("grp", "mom")) // pieces).astype(jnp.int32)
+    fold = TILE // (energies * momenta)
+    matrix = build(
+        coupling, occupation, shift, region_map, side, groups, shares, energies, momenta, fold
+    )
+    sent = pack(lesser, greater, pieces, rows, batch)
+    sent = sent.reshape((devices,) + sent.shape[2:])
+    received = lax.all_to_all(sent, ("grp", "mom"), split_axis=0, concat_axis=0, tiled=True)
+    mixed = mix(matrix, received)
+    returned = lax.all_to_all(mixed, ("grp", "mom"), split_axis=0, concat_axis=0, tiled=True)
+    returned = returned.reshape((2, pieces) + returned.shape[1:])
+    return unpack(returned, lesser.shape, pieces, rows, batch)
 
 
 def with_halo(shard, sides, width):
@@ -90,7 +270,7 @@
     return (jnp.concatenate([real_part, imag_part], axis=-1) * (1.0 / points)).astype(jnp.bfloat16)
 
 
-def on_device(lesser, greater, coupling, occupation, shift, region_map):
+def by_groups(lesser, greater, coupling, occupation, shift, region_map):
     stacked = jnp.stack([lesser, greater])
     widened = with_halo(stacked, (("grp", 1),), SMAX)
     regrouped = lax.all_to_all(widened, "mom", split_axis=4, concat_axis=3, tiled=True)
@@ -107,9 +287,27 @@
     return (returned[0], returned[1])
 
 
+def on_device(groups, shares, lesser, greater, coupling, occupation, shift, region_map):
+    energies, blocks, momenta, height, columns = lesser.shape
+    devices = groups * shares
+    states = energies * momenta
+    whole_tiles = (
+        blocks == 1
+        and devices % 2 == 0
+        and height % (TILE * (devices // 2)) == 0
+        and TILE % states == 0
+        and columns % 128 == 0
+    )
+    if whole_tiles:
+        return by_rows(
+            lesser, greater, coupling, occupation, shift, region_map, groups, shares
+        )
+    return by_groups(lesser, greater, coupling, occupation, shift, region_map)
+
+
 def solution(mesh):
     return jax.shard_map(
-        on_device,
+        functools.partial(on_device, mesh.shape["grp"], mesh.shape["mom"]),
         mesh=mesh,
         in_specs=(
             P("grp", None, "mom", None, None),

time: 638 us -> 220 us (0.34)
  waiting for transfers between devices: 296 us -> 92.4 us
  other arithmetic: 94.3 us -> 0.08 us
  blocking collectives: 145 us -> 96.4 us
  local copies, waits for them, and re-layouts: 43.1 us -> 5.92 us
  matrix products: 30.5 us -> 0 us
  Pallas kernels: 0 us -> 16.3 us
  between operations: 13.9 us -> 1.4 us
    all_to_all x1, waiting for transfers between devices: 206 us -> 92.4 us  [by_rows(): lax.all_to_all(sent, ('grp', 'mom'), split_axis=0, concat_axis=0, tiled=T...]
    ppermute x2 -> x0, waiting for transfers between devices: 89.6 us -> none  [the longest x1 88.1 us: with_halo(): after = lax.ppermute(first, axis, down)]
    all_to_all x1, blocking collectives: 145 us -> 96.4 us  [by_rows(): lax.all_to_all(mixed, ('grp', 'mom'), split_axis=0, concat_axis=0, tiled=...]
    concatenate x3 -> x1, other arithmetic: 48.1 us -> 0.08 us  [build(): jnp.concatenate([coupling, coupling], axis=2)]
    sub x2 -> x0, other arithmetic: 37.8 us -> none  [the longest x1 27.6 us: forward(): cosine[..., columns:] - sine[..., :columns]]
    dot_general x4 -> x0, matrix products: 30.5 us -> none  [the longest x1 21.9 us: forward(): jnp.einsum('pk,aebkxw->aebpxw', basis_low, stacked, preferred_element_typ...]
    another operation x2 -> x0, local copies, waits for them, and re-layouts: 24.1 us -> none
    pallas_call x0 -> x4, Pallas kernels: none -> 16.3 us  [the longest x1 6.65 us: mix(): pl.pallas_call(mix_kernel, grid=(size // TILE,), out_shape=jax.ShapeDtype...]
  transfers between devices with their start and end apart: 3 -> 1, of which waited for: 3 -> 1; matrix products, arithmetic and copies ran while one was open for 1% -> 0% of each run, Pallas kernels for 0% -> 1%
where the time goes in v1:
time: 220 us
  blocking collectives  96.4 us (44%)
  waiting for transfers between devices  92.4 us (42%)
  Pallas kernels  16.3 us (7%)
  starting transfers between devices  7.44 us (3%)
  local copies, waits for them, and re-layouts  5.92 us (3%)
    all_to_all x1, blocking collectives, by_rows(): lax.all_to_all(mixed, ('grp', 'mom'), split_axis=0, concat_axis=0, tiled=...  96.4 us
    all_to_all x1, waiting for transfers between devices, by_rows(): lax.all_to_all(sent, ('grp', 'mom'), split_axis=0, concat_axis=0, tiled=T...  92.4 us
    all_to_all x1, starting transfers between devices, by_rows(): lax.all_to_all(sent, ('grp', 'mom'), split_axis=0, concat_axis=0, tiled=T...  7.44 us
    pallas_call x1, Pallas kernels, mix(): pl.pallas_call(mix_kernel, grid=(size // TILE,), out_shape=jax.ShapeDtype...  6.65 us
    unnamed x22, local copies, waits for them, and re-layouts  5.92 us
    pallas_call x1, Pallas kernels, unpack(): pl.pallas_call(unpack_kernel, grid=(pieces // batch,), out_shape=(out, ou...  4.78 us
  transfers between devices with their start and end apart: 1, of which 1 were waited for; matrix products, arithmetic and copies ran while one was open for 0% of the time, Pallas kernels for 1%

profile of v1, /device:TPU:0, one launch (start us, length us, event | category | flops | bytes accessed | tf_op | source)
XLA Modules:
  0.0 219.9 jit_solution(9324697131156057224)
XLA Ops:
  0.6 0.0 copy-start.1
  0.6 1.6 copy-done.1
  2.2 0.0 copy-start.2
  2.2 1.6 copy-done.2
  3.8 0.0 copy-start.6
  3.8 0.8 copy-done.6
  4.6 2.8 %pack.1 = bf16[2,16,128,512]{3,2,1,0:T(8,128)(2,1)S(1)} custom-call(bf16[128,128]{1,0:T(8,128)(2,1)S(1)} %copy-done.6, bf16[2,1,4,256,512]{4,3,2,1,0:T(8,128)(2,1)S(1)} %copy-done.1, bf16[2,1,4,256,512]{4,3,2,1,0:T(8,128)(2,1)S(1)} %copy-done.2), custom_call_target="tpu_custom_call" | custom-call | tf_op jit(solution)/shard_map/pack/pallas_call | solution.py:126
  7.4 0.0 copy-start
  7.4 2.0 copy-done
  9.3 0.0 copy-start.10
  9.3 0.0 copy-start.3
  9.4 0.0 copy-start.4
  9.4 0.0 copy-start.7
  9.4 0.0 copy-start.8
  9.4 0.0 copy-start.9
  9.4 7.4 %all-to-all-start = ((bf16[32,128,512]{2,1,0:T(8,128)(2,1)}), bf16[32,128,512]{2,1,0:T(8,128)(2,1)}, u32[]{:S(2)}, u32[]{:S(2)}) async-start(bf16[32,128,512]{2,1,0:T(8,128)(2,1)} %bitcast.3), calls=%async_computation | async-start | bytes 8388608 | tf_op jit(solution)/shard_map/all_to_all | solution.py:184
  17.5 0.0 copy-done.10
  17.5 0.1 pad_maximum_fusion.coupling_ref
  17.6 0.0 copy-done.3
  17.6 0.0 copy-done.4
  17.6 0.0 copy-done.7
  17.6 0.0 copy-done.8
  17.6 0.0 copy-done.9
  17.6 2.0 build.1.matrix_ref
  19.7 92.4 %all-to-all-done.in_ref = bf16[32,128,512]{2,1,0:T(8,128)(2,1)} async-done(((bf16[32,128,512]{2,1,0:T(8,128)(2,1)}), bf16[32,128,512]{2,1,0:T(8,128)(2,1)}, u32[]{:S(2)}, u32[]{:S(2)}) %all-to-all-start) | async-done | bytes 4194336 | tf_op jit(solution)/shard_map/all_to_all | solution.py:184
  112.0 6.7 %mix.1 = bf16[32,128,512]{2,1,0:T(8,128)(2,1)S(1)} custom-call(bf16[512,512]{1,0:T(8,128)(2,1)S(1)} %build.1.matrix_ref, bf16[32,128,512]{2,1,0:T(8,128)(2,1)} %all-to-all-done.in_ref), custom_call_target="tpu_custom_call" | custom-call | tf_op jit(solution)/shard_map/mix/pallas_call | solution.py:160
  118.7 0.0 copy-start.5
  118.7 96.4 %all_to_all.10 = bf16[32,128,512]{2,1,0:T(8,128)(2,1)S(1)} all-to-all(bf16[32,128,512]{2,1,0:T(8,128)(2,1)S(1)} %mix.1), channel_id=1, replica_groups=mesh['grp'=2,'mom'=16] {'grp','mom'}, dimensions={0} | all-to-all | bytes 8388608 | tf_op jit(solution)/shard_map/all_to_all | solution.py:186
  215.1 0.0 copy-done.5
  215.1 4.8 %unpack.1 = (bf16[2,1,4,256,512]{4,3,2,1,0:T(8,128)(2,1)}, bf16[2,1,4,256,512]{4,3,2,1,0:T(8,128)(2,1)}) custom-call(bf16[128,128]{1,0:T(8,128)(2,1)S(1)} %copy-done.5, bf16[2,16,128,512]{3,2,1,0:T(8,128)(2,1)S(1)} %bitcast.4), custom_call_target="tpu_custom_call" | custom-call | tf_op jit(solution)/shard_map/unpack/pallas_call | solution.py:143
Async XLA Ops:
  0.6 1.6 copy-start.1
  2.2 1.6 copy-start.2
  3.8 0.8 copy-start.6
  7.4 2.0 copy-start
  9.3 8.1 %copy-start.10 = (f32[4,4,64]{2,1,0:T(4,128)S(1)}, f32[4,4,64]{2,1,0:T(4,128)}, u32[]{:S(2)}) copy-start(f32[4,4,64]{2,1,0:T(4,128)} %param.13) | copy-start | bytes 12292
  9.3 8.2 %copy-start.3 = (s32[512,1]{1,0:T(8,128)S(1)}, s32[512,1]{1,0:T(8,128)}, u32[]{:S(2)}) copy-start(s32[512,1]{1,0:T(8,128)} %constant.37.clone.down_ref) | copy-start | bytes 6148
  9.4 8.2 %copy-start.4 = (bf16[512,64]{1,0:T(8,128)(2,1)S(1)}, bf16[512,64]{1,0:T(8,128)(2,1)}, u32[]{:S(2)}) copy-start(bf16[512,64]{1,0:T(8,128)(2,1)} %constant.36.clone.pick_ref) | copy-start | bytes 196612
  9.4 8.2 %copy-start.7 = (s32[1,512]{1,0:T(1,128)S(1)}, s32[1,512]{1,0:T(1,128)}, u32[]{:S(2)}) copy-start(s32[1,512]{1,0:T(1,128)} %constant.38.clone.across_ref) | copy-start | bytes 6148
  9.4 8.2 %copy-start.8 = (s32[4]{0:T(128)S(1)}, s32[4]{0:T(128)}, u32[]{:S(2)}) copy-start(s32[4]{0:T(128)} %shift_ref.1) | copy-start | bytes 52
  9.4 8.2 %copy-start.9 = (f32[4]{0:T(128)S(1)}, f32[4]{0:T(128)}, u32[]{:S(2)}) copy-start(f32[4]{0:T(128)} %occupation_ref.1) | copy-start | bytes 52
  9.4 102.6 %all-to-all-start = ((bf16[32,128,512]{2,1,0:T(8,128)(2,1)}), bf16[32,128,512]{2,1,0:T(8,128)(2,1)}, u32[]{:S(2)}, u32[]{:S(2)}) async-start(bf16[32,128,512]{2,1,0:T(8,128)(2,1)} %bitcast.3), calls=%async_computation | async-start | bytes 8388608 | tf_op jit(solution)/shard_map/all_to_all | solution.py:184
  118.7 96.5 %copy-start.5 = (bf16[128,128]{1,0:T(8,128)(2,1)S(1)}, bf16[128,128]{1,0:T(8,128)(2,1)}, u32[]{:S(2)}) copy-start(bf16[128,128]{1,0:T(8,128)(2,1)} %constant.40.clone.perm_ref) | copy-start | bytes 98308

commit v2 on v1

--- a/solution.py
+++ b/solution.py
@@ -11,7 +11,7 @@
 
 SMAX = 2
 TILE = 16
-VMEM_BYTES = 40 * 1024 * 1024
+VMEM_BYTES = 60 * 1024 * 1024
 APART = 1 << 16
 
 
@@ -35,8 +35,8 @@
             out_ref[side, piece] = moved.astype(out_ref.dtype)
 
 
-def unpack_kernel(perm_ref, in_ref, lesser_ref, greater_ref):
-    for side, ref in enumerate((lesser_ref, greater_ref)):
+def unpack_kernel(perm_ref, in_ref, *refs):
+    for side, ref in enumerate(refs[-2:]):
         for piece in range(in_ref.shape[1]):
             rows = in_ref.shape[2] // (ref.shape[0] * ref.shape[2])
             moved = jnp.dot(
@@ -50,9 +50,12 @@
 
 def mix_kernel(matrix_ref, in_ref, out_ref):
     devices, rows, columns = in_ref.shape
-    block = in_ref[...].reshape(devices * rows, columns)
-    mixed = jnp.dot(matrix_ref[...], block, preferred_element_type=jnp.float32)
-    out_ref[...] = mixed.astype(out_ref.dtype).reshape(devices, rows, columns)
+    for start in range(0, rows, TILE):
+        block = in_ref[:, start : start + TILE, :].reshape(devices * TILE, columns)
+        mixed = jnp.dot(matrix_ref[...], block, preferred_element_type=jnp.float32)
+        out_ref[:, start : start + TILE, :] = mixed.astype(out_ref.dtype).reshape(
+            devices, TILE, columns
+        )
 
 
 def build_kernel(
@@ -118,27 +121,32 @@
     )
 
 
-def pack(lesser, greater, pieces, rows, batch):
-    energies, _, momenta, _, columns = lesser.shape
+def slab_spec(shape, rows, width, chunk):
+    energies, _, momenta, _, _ = shape
+    return pl.BlockSpec((energies, 1, momenta, rows, width), lambda i: (0, 0, 0, i, chunk))
+
+
+def pack(lesser, greater, pieces, rows, batch, width, chunk):
+    energies, _, momenta, _, _ = lesser.shape
     size = energies * momenta * rows
     perm = jnp.asarray(permutation(energies, momenta, rows), jnp.bfloat16)
-    slab = pl.BlockSpec((energies, 1, momenta, batch * rows, columns), lambda i: (0, 0, 0, i, 0))
+    slab = slab_spec(lesser.shape, batch * rows, width, chunk)
     return pl.pallas_call(
         pack_kernel,
         grid=(pieces // batch,),
-        out_shape=jax.ShapeDtypeStruct((2, pieces, size, columns), lesser.dtype),
+        out_shape=jax.ShapeDtypeStruct((2, pieces, size, width), lesser.dtype),
         in_specs=[pl.BlockSpec((size, size), lambda i: (0, 0)), slab, slab],
-        out_specs=pl.BlockSpec((2, batch, size, columns), lambda i: (0, i, 0, 0)),
+        out_specs=pl.BlockSpec((2, batch, size, width), lambda i: (0, i, 0, 0)),
         compiler_params=params(),
         name="pack",
     )(perm, lesser, greater)
 
 
-def unpack(packed, shape, pieces, rows, batch):
-    energies, _, momenta, _, columns = shape
+def unpack(packed, filled, shape, pieces, rows, batch, width, chunk):
+    energies, _, momenta, _, _ = shape
     size = energies * momenta * rows
     perm = jnp.asarray(permutation(energies, momenta, rows).T, jnp.bfloat16)
-    slab = pl.BlockSpec((energies, 1, momenta, batch * rows, columns), lambda i: (0, 0, 0, i, 0))
+    slab = slab_spec(shape, batch * rows, width, chunk)
     out = jax.ShapeDtypeStruct(shape, packed.dtype)
     return pl.pallas_call(
         unpack_kernel,
@@ -146,20 +154,22 @@
         out_shape=(out, out),
         in_specs=[
             pl.BlockSpec((size, size), lambda i: (0, 0)),
-            pl.BlockSpec((2, batch, size, columns), lambda i: (0, i, 0, 0)),
-        ],
+            pl.BlockSpec((2, batch, size, width), lambda i: (0, i, 0, 0)),
+        ]
+        + [pl.BlockSpec(memory_space=pl.ANY)] * len(filled),
         out_specs=(slab, slab),
+        input_output_aliases={2 + side: side for side in range(len(filled))},
         compiler_params=params(),
         name="unpack",
-    )(perm, packed)
-
-
-def mix(matrix, received):
-    devices, size, columns = received.shape
-    block = pl.BlockSpec((devices, TILE, columns), lambda i: (0, i, 0))
+    )(perm, packed, *filled)
+
+
+def mix(matrix, received, tall):
+    devices, size, width = received.shape
+    block = pl.BlockSpec((devices, tall, width), lambda i: (0, i, 0))
     return pl.pallas_call(
         mix_kernel,
-        grid=(size // TILE,),
+        grid=(size // tall,),
         out_shape=jax.ShapeDtypeStruct(received.shape, received.dtype),
         in_specs=[pl.BlockSpec(matrix.shape, lambda i: (0, 0)), block],
         out_specs=block,
@@ -168,24 +178,34 @@
     )(matrix, received)
 
 
+def exchange(array):
+    return lax.all_to_all(array, ("grp", "mom"), split_axis=0, concat_axis=0, tiled=True)
+
+
 def by_rows(lesser, greater, coupling, occupation, shift, region_map, groups, shares):
     energies, _, momenta, height, columns = lesser.shape
     devices = groups * shares
     pieces = devices // 2
     rows = height // pieces
-    batch = 2 if pieces % 2 == 0 else 1
-    side = (lax.axis_index(("grp", "mom")) // pieces).astype(jnp.int32)
+    batch = math.gcd(4, pieces)
+    chunks = 2 if columns % 256 == 0 else 1
+    width = columns // chunks
+    place = lax.axis_index("grp") * shares + lax.axis_index("mom")
+    side = lax.div(place, jnp.int32(pieces))
     fold = TILE // (energies * momenta)
     matrix = build(
         coupling, occupation, shift, region_map, side, groups, shares, energies, momenta, fold
     )
-    sent = pack(lesser, greater, pieces, rows, batch)
-    sent = sent.reshape((devices,) + sent.shape[2:])
-    received = lax.all_to_all(sent, ("grp", "mom"), split_axis=0, concat_axis=0, tiled=True)
-    mixed = mix(matrix, received)
-    returned = lax.all_to_all(mixed, ("grp", "mom"), split_axis=0, concat_axis=0, tiled=True)
-    returned = returned.reshape((2, pieces) + returned.shape[1:])
-    return unpack(returned, lesser.shape, pieces, rows, batch)
+    received = []
+    for chunk in range(chunks):
+        sent = pack(lesser, greater, pieces, rows, batch, width, chunk)
+        received.append(exchange(sent.reshape((devices,) + sent.shape[2:])))
+    returned = [exchange(mix(matrix, part, 2 * TILE)) for part in received]
+    filled = ()
+    for chunk, part in enumerate(returned):
+        part = part.reshape((2, pieces) + part.shape[1:])
+        filled = unpack(part, filled, lesser.shape, pieces, rows, batch, width, chunk)
+    return filled
 
 
 def with_halo(shard, sides, width):

time: 220 us -> 229 us (1.041)
  blocking collectives: 96.4 us -> 0 us
  waiting for transfers between devices: 92.4 us -> 176 us
  Pallas kernels: 16.3 us -> 30.2 us
  starting transfers between devices: 7.44 us -> 16.2 us
    all_to_all x1 -> x0, blocking collectives: 96.4 us -> none  [by_rows(): lax.all_to_all(mixed, ('grp', 'mom'), split_axis=0, concat_axis=0, tiled=...]
    all_to_all x1 -> x4, waiting for transfers between devices: 92.4 us -> 176 us  [exchange(): lax.all_to_all(array, ('grp', 'mom'), split_axis=0, concat_axis=0, tiled=...]
    all_to_all x1 -> x4, starting transfers between devices: 7.44 us -> 16.2 us  [exchange(): lax.all_to_all(array, ('grp', 'mom'), split_axis=0, concat_axis=0, tiled=...]
    pallas_call x1 -> x2, Pallas kernels: 2.81 us -> 8.6 us  [pack(): pl.pallas_call(pack_kernel, grid=(pieces // batch,), out_shape=jax.ShapeD...]
    pallas_call x1 -> x2, Pallas kernels: 4.78 us -> 8.55 us  [unpack(): pl.pallas_call(unpack_kernel, grid=(pieces // batch,), out_shape=(out, ou...]
    pallas_call x1 -> x2, Pallas kernels: 6.65 us -> 9.67 us  [mix(): pl.pallas_call(mix_kernel, grid=(size // tall,), out_shape=jax.ShapeDtype...]
    unnamed x22 -> x8, local copies, waits for them, and re-layouts: 5.92 us -> 3.98 us
  transfers between devices with their start and end apart: 1 -> 4, of which waited for: 1 -> 4; matrix products, arithmetic and copies ran while one was open for 0% -> 0% of each run, Pallas kernels for 1% -> 9%
where the time goes in v2:
time: 229 us; the launch traced here: 228 us
  waiting for transfers between devices  176 us (77%)
  Pallas kernels  30.2 us (13%)
  starting transfers between devices  16.2 us (7%)
  local copies, waits for them, and re-layouts  3.98 us (2%)
    all_to_all x4, waiting for transfers between devices, exchange(): lax.all_to_all(array, ('grp', 'mom'), split_axis=0, concat_axis=0, tiled=...  176 us
    all_to_all x4, starting transfers between devices, exchange(): lax.all_to_all(array, ('grp', 'mom'), split_axis=0, concat_axis=0, tiled=...  16.2 us
    pallas_call x2, Pallas kernels, mix(): pl.pallas_call(mix_kernel, grid=(size // tall,), out_shape=jax.ShapeDtype...  9.67 us
    pallas_call x2, Pallas kernels, pack(): pl.pallas_call(pack_kernel, grid=(pieces // batch,), out_shape=jax.ShapeD...  8.6 us
    pallas_call x2, Pallas kernels, unpack(): pl.pallas_call(unpack_kernel, grid=(pieces // batch,), out_shape=(out, ou...  8.55 us
  transfers between devices with their start and end apart: 4, of which 4 were waited for; matrix products, arithmetic and copies ran while one was open for 0% of the time, Pallas kernels for 9%

profile of v2, /device:TPU:0, one launch (start us, length us, event | category | flops | bytes accessed | tf_op | source)
XLA Modules:
  0.0 228.3 jit_solution(732942963038986681)
XLA Ops:
  0.6 4.3 %pack.3 = bf16[2,16,128,256]{3,2,1,0:T(8,128)(2,1)} custom-call(bf16[128,128]{1,0:T(8,128)(2,1)} %constant.28.clone.perm_ref, bf16[2,1,4,256,512]{4,3,2,1,0:T(8,128)(2,1)} %lesser_ref.3, bf16[2,1,4,256,512]{4,3,2,1,0:T(8,128)(2,1)} %greater_ref.3), custom_call_target="tpu_custom_call" | custom-call | tf_op jit(solution)/shard_map/pack/pallas_call | solution.py:134
  4.9 7.3 %all-to-all-start.2 = ((bf16[32,128,256]{2,1,0:T(8,128)(2,1)}), bf16[32,128,256]{2,1,0:T(8,128)(2,1)S(1)}, u32[]{:S(2)}, u32[]{:S(2)}) async-start(bf16[32,128,256]{2,1,0:T(8,128)(2,1)} %bitcast.7), calls=%async_computation.2 | async-start | bytes 4194304 | tf_op jit(solution)/shard_map/all_to_all | solution.py:182
  12.2 4.3 %pack.2 = bf16[2,16,128,256]{3,2,1,0:T(8,128)(2,1)} custom-call(bf16[128,128]{1,0:T(8,128)(2,1)} %constant.28.clone.perm_ref, bf16[2,1,4,256,512]{4,3,2,1,0:T(8,128)(2,1)} %lesser_ref.3, bf16[2,1,4,256,512]{4,3,2,1,0:T(8,128)(2,1)} %greater_ref.3), custom_call_target="tpu_custom_call" | custom-call | tf_op jit(solution)/shard_map/pack/pallas_call | solution.py:134
  16.5 45.4 %all-to-all-done.2.in_ref = bf16[32,128,256]{2,1,0:T(8,128)(2,1)S(1)} async-done(((bf16[32,128,256]{2,1,0:T(8,128)(2,1)}), bf16[32,128,256]{2,1,0:T(8,128)(2,1)S(1)}, u32[]{:S(2)}, u32[]{:S(2)}) %all-to-all-start.2) | async-done | bytes 2097184 | tf_op jit(solution)/shard_map/all_to_all | solution.py:182
  61.9 0.0 copy-start.1
  61.9 0.0 copy-start.3
  61.9 1.3 copy-done.1
  63.3 3.5 %all-to-all-start = ((bf16[32,128,256]{2,1,0:T(8,128)(2,1)}), bf16[32,128,256]{2,1,0:T(8,128)(2,1)}, u32[]{:S(2)}, u32[]{:S(2)}) async-start(bf16[32,128,256]{2,1,0:T(8,128)(2,1)} %bitcast.5), calls=%async_computation | async-start | bytes 4194304 | tf_op jit(solution)/shard_map/all_to_all | solution.py:182
  67.4 0.0 copy-done.3
  67.4 0.7 pad_maximum_fusion.coupling_ref
  68.1 3.3 %build.1.matrix_ref = bf16[512,512]{1,0:T(8,128)(2,1)} custom-call(s32[1]{0:T(128)S(6)} %copy.19.region_ref, s32[1]{0:T(128)} %bitcast.side_ref, s32[4]{0:T(128)} %shift_ref.1, f32[4]{0:T(128)} %occupation_ref.1, f32[4,4,128]{2,1,0:T(4,128)} %pad_maximum_fusion.coupling_ref, bf16[512,64]{1,0:T(8,128)(2,1)} %constant.25.clone.pick_ref, ...), custom_call_target="tpu_custom_call" | custom-call | tf_op jit(solution)/shard_map/build/pallas_call | solution.py:105
  71.4 4.8 %mix.3 = bf16[32,128,256]{2,1,0:T(8,128)(2,1)} custom-call(bf16[512,512]{1,0:T(8,128)(2,1)} %build.1.matrix_ref, bf16[32,128,256]{2,1,0:T(8,128)(2,1)} %copy-done.1), custom_call_target="tpu_custom_call" | custom-call | tf_op jit(solution)/shard_map/mix/pallas_call | solution.py:170
  76.2 40.2 %all-to-all-done.in_ref = bf16[32,128,256]{2,1,0:T(8,128)(2,1)} async-done(((bf16[32,128,256]{2,1,0:T(8,128)(2,1)}), bf16[32,128,256]{2,1,0:T(8,128)(2,1)}, u32[]{:S(2)}, u32[]{:S(2)}) %all-to-all-start) | async-done | bytes 2097184 | tf_op jit(solution)/shard_map/all_to_all | solution.py:182
  116.4 2.7 %all-to-all-start.3 = ((bf16[32,128,256]{2,1,0:T(8,128)(2,1)}), bf16[32,128,256]{2,1,0:T(8,128)(2,1)S(1)}, u32[]{:S(2)}, u32[]{:S(2)}) async-start(bf16[32,128,256]{2,1,0:T(8,128)(2,1)} %mix.3), calls=%async_computation.3 | async-start | bytes 4194304 | tf_op jit(solution)/shard_map/all_to_all | solution.py:182
  119.2 4.9 %mix.2 = bf16[32,128,256]{2,1,0:T(8,128)(2,1)} custom-call(bf16[512,512]{1,0:T(8,128)(2,1)} %build.1.matrix_ref, bf16[32,128,256]{2,1,0:T(8,128)(2,1)} %all-to-all-done.in_ref), custom_call_target="tpu_custom_call" | custom-call | tf_op jit(solution)/shard_map/mix/pallas_call | solution.py:170
  124.1 44.8 %all-to-all-done.3 = bf16[32,128,256]{2,1,0:T(8,128)(2,1)S(1)} async-done(((bf16[32,128,256]{2,1,0:T(8,128)(2,1)}), bf16[32,128,256]{2,1,0:T(8,128)(2,1)S(1)}, u32[]{:S(2)}, u32[]{:S(2)}) %all-to-all-start.3) | async-done | bytes 2097184 | tf_op jit(solution)/shard_map/all_to_all | solution.py:182
  168.9 0.0 copy-start.2
  168.9 1.3 copy-done.2
  170.2 2.7 %all-to-all-start.1 = ((bf16[32,128,256]{2,1,0:T(8,128)(2,1)}), bf16[32,128,256]{2,1,0:T(8,128)(2,1)S(1)}, u32[]{:S(2)}, u32[]{:S(2)}) async-start(bf16[32,128,256]{2,1,0:T(8,128)(2,1)} %mix.2), calls=%async_computation.1 | async-start | bytes 4194304 | tf_op jit(solution)/shard_map/all_to_all | solution.py:182
  172.9 4.3 %unpack.2 = (bf16[2,1,4,256,512]{4,3,2,1,0:T(8,128)(2,1)}, bf16[2,1,4,256,512]{4,3,2,1,0:T(8,128)(2,1)}) custom-call(bf16[128,128]{1,0:T(8,128)(2,1)} %constant.29.clone.perm_ref, bf16[2,16,128,256]{3,2,1,0:T(8,128)(2,1)} %bitcast.8), custom_call_target="tpu_custom_call" | custom-call | tf_op jit(solution)/shard_map/unpack/pallas_call | solution.py:151
  177.2 45.4 %all-to-all-done.1 = bf16[32,128,256]{2,1,0:T(8,128)(2,1)S(1)} async-done(((bf16[32,128,256]{2,1,0:T(8,128)(2,1)}), bf16[32,128,256]{2,1,0:T(8,128)(2,1)S(1)}, u32[]{:S(2)}, u32[]{:S(2)}) %all-to-all-start.1) | async-done | bytes 2097184 | tf_op jit(solution)/shard_map/all_to_all | solution.py:182
  222.7 0.0 copy-start
  222.7 1.3 copy-done
  224.0 4.3 %unpack.3 = (bf16[2,1,4,256,512]{4,3,2,1,0:T(8,128)(2,1)}, bf16[2,1,4,256,512]{4,3,2,1,0:T(8,128)(2,1)}) custom-call(bf16[128,128]{1,0:T(8,128)(2,1)} %constant.29.clone.perm_ref, bf16[2,16,128,256]{3,2,1,0:T(8,128)(2,1)} %bitcast.6, bf16[2,1,4,256,512]{4,3,2,1,0:T(8,128)(2,1)} %get-tuple-element.4.refs_0_, ...), custom_call_target="tpu_custom_call", output_to_operand_aliasing={{0}: (2, {}), {1}: (3, {})} | custom-call | tf_op jit(solution)/shard_map/unpack/pallas_call | solution.py:151
Async XLA Ops:
  4.9 57.0 %all-to-all-start.2 = ((bf16[32,128,256]{2,1,0:T(8,128)(2,1)}), bf16[32,128,256]{2,1,0:T(8,128)(2,1)S(1)}, u32[]{:S(2)}, u32[]{:S(2)}) async-start(bf16[32,128,256]{2,1,0:T(8,128)(2,1)} %bitcast.7), calls=%async_computation.2 | async-start | bytes 4194304 | tf_op jit(solution)/shard_map/all_to_all | solution.py:182
  61.9 1.3 copy-start.1
  61.9 5.5 %copy-start.3 = (f32[4,4,64]{2,1,0:T(4,128)S(1)}, f32[4,4,64]{2,1,0:T(4,128)}, u32[]{:S(2)}) copy-start(f32[4,4,64]{2,1,0:T(4,128)} %param.15) | copy-start | bytes 12292
  63.3 53.2 %all-to-all-start = ((bf16[32,128,256]{2,1,0:T(8,128)(2,1)}), bf16[32,128,256]{2,1,0:T(8,128)(2,1)}, u32[]{:S(2)}, u32[]{:S(2)}) async-start(bf16[32,128,256]{2,1,0:T(8,128)(2,1)} %bitcast.5), calls=%async_computation | async-start | bytes 4194304 | tf_op jit(solution)/shard_map/all_to_all | solution.py:182
  116.4 52.4 %all-to-all-start.3 = ((bf16[32,128,256]{2,1,0:T(8,128)(2,1)}), bf16[32,128,256]{2,1,0:T(8,128)(2,1)S(1)}, u32[]{:S(2)}, u32[]{:S(2)}) async-start(bf16[32,128,256]{2,1,0:T(8,128)(2,1)} %mix.3), calls=%async_computation.3 | async-start | bytes 4194304 | tf_op jit(solution)/shard_map/all_to_all | solution.py:182
  168.9 1.3 copy-start.2
  170.2 52.4 %all-to-all-start.1 = ((bf16[32,128,256]{2,1,0:T(8,128)(2,1)}), bf16[32,128,256]{2,1,0:T(8,128)(2,1)S(1)}, u32[]{:S(2)}, u32[]{:S(2)}) async-start(bf16[32,128,256]{2,1,0:T(8,128)(2,1)} %mix.2), calls=%async_computation.1 | async-start | bytes 4194304 | tf_op jit(solution)/shard_map/all_to_all | solution.py:182
  222.7 1.3 copy-start

commit v3 on v0

--- a/solution.py
+++ b/solution.py
@@ -1,11 +1,264 @@
+import functools
 import math
 
 import jax
 import jax.numpy as jnp
+import numpy as np
 from jax import lax
+from jax.experimental import pallas as pl
+from jax.experimental.pallas import tpu as pltpu
 from jax.sharding import PartitionSpec as P
 
 SMAX = 2
+TILE = 16
+VMEM_BYTES = 48 * 1024 * 1024
+APART = 1 << 16
+AXES = ("grp", "mom")
+
+
+def permutation(energies, momenta, rows):
+    inner = energies * momenta
+    size = inner * rows
+    matrix = np.zeros((size, size), np.float32)
+    for state in range(inner):
+        for row in range(rows):
+            matrix[row * inner + state, state * rows + row] = 1.0
+    return matrix
+
+
+def place_of(place_ref, pieces, far):
+    place = place_ref[0]
+    half = pieces // 2
+    block = lax.rem(place, jnp.int32(pieces))
+    low = lax.rem(block, jnp.int32(half))
+    high = lax.div(block, jnp.int32(half))
+    return lax.div(place, jnp.int32(pieces)), low, (1 - high if far else high) * half
+
+
+def pack_kernel(pieces, far, place_ref, perm_ref, lesser_ref, greater_ref, *refs):
+    half = pieces // 2
+    outs, held, arrived = refs[: 2 * half], refs[-2], refs[-1]
+    rows = held.shape[4]
+    size, width = outs[0].shape
+    side, low, base = place_of(place_ref, pieces, far)
+    copies = []
+    for step in range(half):
+        start = pl.multiple_of((base + (low ^ step)) * rows, rows)
+        for which, ref in enumerate((lesser_ref, greater_ref)):
+            copy = pltpu.make_async_copy(
+                ref.at[:, 0, :, pl.ds(start, rows), :],
+                held.at[step, which],
+                arrived.at[step, which],
+            )
+            copy.start()
+            copies.append(copy)
+    for step in range(half):
+        moved = []
+        for which in range(2):
+            copies[2 * step + which].wait()
+            block = held[step, which].reshape(size, width)
+            moved.append(jnp.dot(perm_ref[...], block, preferred_element_type=jnp.float32))
+        outs[step][...] = jnp.where(side == 0, moved[0], moved[1]).astype(outs[0].dtype)
+        outs[half + step][...] = jnp.where(side == 0, moved[1], moved[0]).astype(outs[0].dtype)
+
+
+def unpack_kernel(pieces, far, place_ref, perm_ref, *refs):
+    half = pieces // 2
+    ins, held, sent = refs[: 2 * half], refs[-2], refs[-1]
+    outs = refs[-4:-2]
+    rows = held.shape[4]
+    side, low, base = place_of(place_ref, pieces, far)
+    copies = []
+    for step in range(half):
+        own = jnp.dot(perm_ref[...], ins[step][...], preferred_element_type=jnp.float32)
+        other = jnp.dot(perm_ref[...], ins[half + step][...], preferred_element_type=jnp.float32)
+        start = pl.multiple_of((base + (low ^ step)) * rows, rows)
+        for which, ref in enumerate(outs):
+            moved = jnp.where(side == which, own, other).astype(held.dtype)
+            held[step, which] = moved.reshape(held.shape[2:])
+            copy = pltpu.make_async_copy(
+                held.at[step, which],
+                ref.at[:, 0, :, pl.ds(start, rows), :],
+                sent.at[step, which],
+            )
+            copy.start()
+            copies.append(copy)
+    for copy in copies:
+        copy.wait()
+
+
+def mix_kernel(count, matrix_ref, *refs):
+    ins, outs = refs[:count], refs[count:]
+    size, width = ins[0].shape
+    for start in range(0, size, TILE):
+        block = jnp.concatenate([ref[start : start + TILE, :] for ref in ins], axis=0)
+        mixed = jnp.dot(matrix_ref[...], block, preferred_element_type=jnp.float32)
+        mixed = mixed.astype(outs[0].dtype)
+        for slot, ref in enumerate(outs):
+            ref[start : start + TILE, :] = mixed[slot * TILE : (slot + 1) * TILE, :]
+
+
+def build_kernel(
+    shares, momenta, energies, pieces,
+    place_ref, region_ref, shift_ref, occupation_ref, coupling_ref, down_ref, across_ref, *out_refs
+):
+    points = shares * momenta
+    modes = coupling_ref.shape[1]
+    place = place_ref[0]
+    greater = lax.div(place, jnp.int32(pieces)).astype(jnp.float32)
+    chosen = coupling_ref[region_ref[0]]
+    bits = shares.bit_length() - 1
+
+    def code_of(slot, own):
+        return own + ((slot ^ place) >> bits) * energies
+
+    size = down_ref.shape[0]
+    momentum = ((down_ref[:, 0:1] ^ place) & (shares - 1)) * momenta + down_ref[:, 2:3]
+    pick = momentum == lax.broadcasted_iota(jnp.int32, (size, points), 1)
+    pick = jnp.where(pick, 1.0, 0.0).astype(jnp.bfloat16)
+    down = code_of(down_ref[:, 0:1], down_ref[:, 1:2])
+    across = code_of(across_ref[0:1, :], across_ref[1:2, :])
+    apart = down - across
+    total = jnp.zeros((size, size), jnp.float32)
+    for step in range(-SMAX, SMAX + 1):
+        if step == 0:
+            continue
+        row = jnp.zeros((1, 2 * points), jnp.float32)
+        for mode in range(modes):
+            filling = occupation_ref[mode] + (greater if step > 0 else 1.0 - greater)
+            weight = jnp.where(shift_ref[mode] == abs(step), filling, 0.0)
+            row = row + weight * chosen[mode : mode + 1, :]
+        wide = jnp.broadcast_to(row, (points, 2 * points))
+        turned = pltpu.roll(wide, 0, 1, stride=1, stride_axis=0)[:, :points]
+        half = jnp.dot(
+            pick, turned.astype(jnp.bfloat16), preferred_element_type=jnp.float32
+        ).astype(jnp.bfloat16)
+        full = lax.dot_general(
+            pick, half, (((1,), (1,)), ((), ())), preferred_element_type=jnp.float32
+        )
+        total = jnp.where(apart == step, full, total)
+    first = out_refs[0].shape[0]
+    out_refs[0][...] = total[:first].astype(out_refs[0].dtype)
+    out_refs[1][...] = total[first:].astype(out_refs[1].dtype)
+
+
+def params():
+    return pltpu.CompilerParams(vmem_limit_bytes=VMEM_BYTES)
+
+
+SCALARS = pl.BlockSpec(memory_space=pltpu.SMEM)
+VECTORS = pl.BlockSpec(memory_space=pltpu.VMEM)
+WHERE_IT_LIES = pl.BlockSpec(memory_space=pl.ANY)
+
+
+def build(place, coupling, occupation, shift, region_map, slots, shares, energies, momenta, pieces):
+    fold = TILE // (energies * momenta)
+    slot, row, energy, momentum = np.meshgrid(
+        np.asarray(slots), np.arange(fold), np.arange(energies), np.arange(momenta), indexing="ij"
+    )
+    static = [slot.ravel(), (row * APART + energy).ravel(), momentum.ravel()]
+    down = np.stack(static, axis=1).astype(np.int32)
+    size = down.shape[0]
+    part = jax.ShapeDtypeStruct((size // 2, size), jnp.bfloat16)
+    return pl.pallas_call(
+        functools.partial(build_kernel, shares, momenta, energies, pieces),
+        out_shape=(part, part),
+        in_specs=[SCALARS] * 4 + [VECTORS] * 3,
+        out_specs=(VECTORS, VECTORS),
+        compiler_params=params(),
+        name="build",
+    )(
+        place,
+        region_map,
+        shift,
+        occupation,
+        jnp.concatenate([coupling, coupling], axis=2),
+        jnp.asarray(down),
+        jnp.asarray(down.T),
+    )
+
+
+def pack(place, lesser, greater, pieces, rows, far):
+    energies, _, momenta, _, columns = lesser.shape
+    size = energies * momenta * rows
+    half = pieces // 2
+    perm = jnp.asarray(permutation(energies, momenta, rows), jnp.bfloat16)
+    piece = jax.ShapeDtypeStruct((size, columns), lesser.dtype)
+    return pl.pallas_call(
+        functools.partial(pack_kernel, pieces, far),
+        out_shape=(piece,) * (2 * half),
+        in_specs=[SCALARS, VECTORS, WHERE_IT_LIES, WHERE_IT_LIES],
+        out_specs=(VECTORS,) * (2 * half),
+        scratch_shapes=[
+            pltpu.VMEM((half, 2, energies, momenta, rows, columns), lesser.dtype),
+            pltpu.SemaphoreType.DMA((half, 2)),
+        ],
+        compiler_params=params(),
+        name="pack",
+    )(place, perm, lesser, greater)
+
+
+def unpack(place, parts, filled, shape, pieces, rows, far):
+    energies, _, momenta, _, columns = shape
+    half = pieces // 2
+    perm = jnp.asarray(permutation(energies, momenta, rows).T, jnp.bfloat16)
+    out = jax.ShapeDtypeStruct(shape, parts[0].dtype)
+    return pl.pallas_call(
+        functools.partial(unpack_kernel, pieces, far),
+        out_shape=(out, out),
+        in_specs=[SCALARS, VECTORS] + [VECTORS] * len(parts) + [WHERE_IT_LIES] * len(filled),
+        out_specs=(WHERE_IT_LIES, WHERE_IT_LIES),
+        scratch_shapes=[
+            pltpu.VMEM((half, 2, energies, momenta, rows, columns), parts[0].dtype),
+            pltpu.SemaphoreType.DMA((half, 2)),
+        ],
+        input_output_aliases={2 + len(parts) + side: side for side in range(len(filled))},
+        compiler_params=params(),
+        name="unpack",
+    )(place, perm, *parts, *filled)
+
+
+def mix(matrix, parts):
+    piece = jax.ShapeDtypeStruct(parts[0].shape, parts[0].dtype)
+    count = matrix.shape[0] // TILE
+    return pl.pallas_call(
+        functools.partial(mix_kernel, len(parts)),
+        out_shape=(piece,) * count,
+        in_specs=[VECTORS] * (1 + len(parts)),
+        out_specs=(VECTORS,) * count,
+        compiler_params=params(),
+        name="mix",
+    )(matrix, *parts)
+
+
+def exchange(parts, slots, devices):
+    return [
+        part
+        if slot == 0
+        else lax.ppermute(part, AXES, [(device, device ^ slot) for device in range(devices)])
+        for part, slot in zip(parts, slots)
+    ]
+
+
+def by_rows(lesser, greater, coupling, occupation, shift, region_map, groups, shares):
+    energies, _, momenta, height, _ = lesser.shape
+    devices = groups * shares
+    pieces = devices // 2
+    half = pieces // 2
+    rows = height // pieces
+    far = [side * pieces + half + step for side in range(2) for step in range(half)]
+    near = [side * pieces + step for side in range(2) for step in range(half)]
+    place = (lax.axis_index("grp") * shares + lax.axis_index("mom")).astype(jnp.int32).reshape(1)
+    far_in = exchange(pack(place, lesser, greater, pieces, rows, True), far, devices)
+    near_in = exchange(pack(place, lesser, greater, pieces, rows, False), near, devices)
+    far_matrix, near_matrix = build(
+        place, coupling, occupation, shift, region_map, far + near, shares, energies, momenta, pieces
+    )
+    received = far_in + near_in
+    far_out = exchange(mix(far_matrix, received), far, devices)
+    near_out = exchange(mix(near_matrix, received), near, devices)
+    filled = unpack(place, far_out, (), lesser.shape, pieces, rows, True)
+    return unpack(place, near_out, filled, lesser.shape, pieces, rows, False)
 
 
 def with_halo(shard, sides, width):
@@ -90,7 +343,7 @@
     return (jnp.concatenate([real_part, imag_part], axis=-1) * (1.0 / points)).astype(jnp.bfloat16)
 
 
-def on_device(lesser, greater, coupling, occupation, shift, region_map):
+def by_groups(lesser, greater, coupling, occupation, shift, region_map):
     stacked = jnp.stack([lesser, greater])
     widened = with_halo(stacked, (("grp", 1),), SMAX)
     regrouped = lax.all_to_all(widened, "mom", split_axis=4, concat_axis=3, tiled=True)
@@ -107,9 +360,28 @@
     return (returned[0], returned[1])
 
 
+def on_device(groups, shares, lesser, greater, coupling, occupation, shift, region_map):
+    energies, blocks, momenta, height, columns = lesser.shape
+    devices = groups * shares
+    states = energies * momenta
+    whole_tiles = (
+        blocks == 1
+        and devices >= 4
+        and devices & (devices - 1) == 0
+        and height % (TILE * (devices // 2)) == 0
+        and TILE % states == 0
+        and columns % 128 == 0
+    )
+    if whole_tiles:
+        return by_rows(
+            lesser, greater, coupling, occupation, shift, region_map, groups, shares
+        )
+    return by_groups(lesser, greater, coupling, occupation, shift, region_map)
+
+
 def solution(mesh):
     return jax.shard_map(
-        on_device,
+        functools.partial(on_device, mesh.shape["grp"], mesh.shape["mom"]),
         mesh=mesh,
         in_specs=(
             P("grp", None, "mom", None, None),

time: 638 us -> 269 us (0.42)
  waiting for transfers between devices: 296 us -> 87.7 us
  blocking collectives: 145 us -> 0 us
  starting transfers between devices: 13.6 us -> 158 us
  other arithmetic: 94.3 us -> 0.08 us
  local copies, waits for them, and re-layouts: 43.1 us -> 3.07 us
  matrix products: 30.5 us -> 0 us
  Pallas kernels: 0 us -> 17.2 us
  between operations: 13.9 us -> 1.53 us
    all_to_all x1 -> x0, waiting for transfers between devices: 206 us -> none  [on_device(): lax.all_to_all(widened, 'mom', split_axis=4, concat_axis=3, tiled=True)]
    ppermute x2 -> x62, starting transfers between devices: 6.7 us -> 158 us  [exchange(): lax.ppermute(part, AXES, [(device, device ^ slot) for device in range(dev...]
    all_to_all x1 -> x0, blocking collectives: 145 us -> none  [on_device(): lax.all_to_all(result, 'mom', split_axis=3, concat_axis=4, tiled=True)]
    concatenate x3 -> x1, other arithmetic: 48.1 us -> 0.08 us  [build(): jnp.concatenate([coupling, coupling], axis=2)]
    sub x2 -> x0, other arithmetic: 37.8 us -> none  [the longest x1 27.6 us: forward(): cosine[..., columns:] - sine[..., :columns]]
    dot_general x4 -> x0, matrix products: 30.5 us -> none  [the longest x1 21.9 us: forward(): jnp.einsum('pk,aebkxw->aebpxw', basis_low, stacked, preferred_element_typ...]
    another operation x2 -> x0, local copies, waits for them, and re-layouts: 24.1 us -> none
    pallas_call x0 -> x7, Pallas kernels: none -> 17.2 us  [the longest x2 7.35 us: pack(): pl.pallas_call(functools.partial(pack_kernel, pieces, far), out_shape=(pi...]
  transfers between devices with their start and end apart: 3 -> 62, of which waited for: 3 -> 18; matrix products, arithmetic and copies ran while one was open for 1% -> 0% of each run, Pallas kernels for 0% -> 4%
where the time goes in v3:
time: 269 us; the launch traced here: 268 us
  starting transfers between devices  158 us (59%)
  waiting for transfers between devices  87.7 us (33%)
  Pallas kernels  17.2 us (6%)
  local copies, waits for them, and re-layouts  3.07 us (1%)
    ppermute x62, starting transfers between devices, exchange(): lax.ppermute(part, AXES, [(device, device ^ slot) for device in range(dev...  158 us
    ppermute x62, waiting for transfers between devices, exchange(): lax.ppermute(part, AXES, [(device, device ^ slot) for device in range(dev...  87.7 us
    pallas_call x2, Pallas kernels, pack(): pl.pallas_call(functools.partial(pack_kernel, pieces, far), out_shape=(pi...  7.35 us
  transfers between devices with their start and end apart: 62, of which 18 were waited for; matrix products, arithmetic and copies ran while one was open for 0% of the time, Pallas kernels for 4%

profile of v3, /device:TPU:0, one launch (start us, length us, event | category | flops | bytes accessed | tf_op | source)
XLA Modules:
  0.0 267.8 jit_solution(18079937957848737778)
XLA Ops:
  3.0 3.7 %pack.3 = (bf16[128,512]{1,0:T(8,128)(2,1)S(1)}, bf16[128,512]{1,0:T(8,128)(2,1)S(1)}, bf16[128,512]{1,0:T(8,128)(2,1)S(1)}, bf16[128,512]{1,0:T(8,128)(2,1)S(1)...) custom-call(s32[1]{0:T(128)} %bitcast.place_ref, ...), custom_call_target="tpu_custom_call" | custom-call | tf_op jit(solution)/shard_map/pack/pallas_call | solution.py:187
  7.2 2.6 collective-permute-start.17
  11.7 2.6 collective-permute-start.21
  18.5 2.3 collective-permute-start.25
  20.9 2.1 collective-permute-done.21.refs_22_
  23.1 3.7 %pack.2 = (bf16[128,512]{1,0:T(8,128)(2,1)S(1)}, bf16[128,512]{1,0:T(8,128)(2,1)S(1)}, bf16[128,512]{1,0:T(8,128)(2,1)S(1)}, bf16[128,512]{1,0:T(8,128)(2,1)S(1)...) custom-call(s32[1]{0:T(128)} %bitcast.place_ref, ...), custom_call_target="tpu_custom_call" | custom-call | tf_op jit(solution)/shard_map/pack/pallas_call | solution.py:187
  26.8 2.7 collective-permute-start.27
  30.6 5.1 %collective-permute-done.24.refs_25_ = bf16[128,512]{1,0:T(8,128)(2,1)S(1)} collective-permute-done((bf16[128,512]{1,0:T(8,128)(2,1)S(1)}, bf16[128,512]{1,0:T(8,128)(2,1)S(1)}, u32[]{:S(2)}, u32[]{:S(2)}) %collective-permute-start.24) | collective-permute-done | bytes 131104 | tf_op jit(solution)/shard_map/ppermute | solution.py:238
  35.7 3.9 %collective-permute-start.29 = (bf16[128,512]{1,0:T(8,128)(2,1)S(1)}, bf16[128,512]{1,0:T(8,128)(2,1)S(1)}, u32[]{:S(2)}, u32[]{:S(2)}) collective-permute-start(bf16[128,512]{1,0:T(8,128)(2,1)S(1)} %get-tuple-element.101), channel_id=1, source_target_pairs={{0,22},{1,23},{2,20},{3,21},{4,18},{5,19},{6,16},{7,17},{8,30},{9,... | collective-permute-start | bytes 393224 | tf_op jit(solution)/shard_map/ppermute | solution.py:238
  39.6 2.6 collective-permute-start
  42.3 3.0 %collective-permute-start.2 = (bf16[128,512]{1,0:T(8,128)(2,1)S(1)}, bf16[128,512]{1,0:T(8,128)(2,1)S(1)}, u32[]{:S(2)}, u32[]{:S(2)}) collective-permute-start(bf16[128,512]{1,0:T(8,128)(2,1)S(1)} %get-tuple-element.73), channel_id=1, source_target_pairs={{0,10},{1,11},{2,8},{3,9},{4,14},{5,15},{6,12},{7,13},{8,2},{9,3},... | collective-permute-start | bytes 393224 | tf_op jit(solution)/shard_map/ppermute | solution.py:238
  45.9 5.1 %collective-permute-done.30.refs_31_ = bf16[128,512]{1,0:T(8,128)(2,1)S(1)} collective-permute-done((bf16[128,512]{1,0:T(8,128)(2,1)S(1)}, bf16[128,512]{1,0:T(8,128)(2,1)S(1)}, u32[]{:S(2)}, u32[]{:S(2)}) %collective-permute-start.30) | collective-permute-done | bytes 131104 | tf_op jit(solution)/shard_map/ppermute | solution.py:238
  51.0 3.3 %collective-permute-start.5 = (bf16[128,512]{1,0:T(8,128)(2,1)S(1)}, bf16[128,512]{1,0:T(8,128)(2,1)S(1)}, u32[]{:S(2)}, u32[]{:S(2)}) collective-permute-start(bf16[128,512]{1,0:T(8,128)(2,1)S(1)} %get-tuple-element.76), channel_id=1, source_target_pairs={{0,13},{1,12},{2,15},{3,14},{4,9},{5,8},{6,11},{7,10},{8,5},{9,4},... | collective-permute-start | bytes 393224 | tf_op jit(solution)/shard_map/ppermute | solution.py:238
  54.3 11.6 %collective-permute-done.1.refs_1_ = bf16[128,512]{1,0:T(8,128)(2,1)S(1)} collective-permute-done((bf16[128,512]{1,0:T(8,128)(2,1)S(1)}, bf16[128,512]{1,0:T(8,128)(2,1)S(1)}, u32[]{:S(2)}, u32[]{:S(2)}) %collective-permute-start.1) | collective-permute-done | bytes 131104 | tf_op jit(solution)/shard_map/ppermute | solution.py:238
  70.8 3.4 %collective-permute-done.3.refs_3_ = bf16[128,512]{1,0:T(8,128)(2,1)S(1)} collective-permute-done((bf16[128,512]{1,0:T(8,128)(2,1)S(1)}, bf16[128,512]{1,0:T(8,128)(2,1)S(1)}, u32[]{:S(2)}, u32[]{:S(2)}) %collective-permute-start.3) | collective-permute-done | bytes 131104 | tf_op jit(solution)/shard_map/ppermute | solution.py:238
  75.1 3.8 %collective-permute-start.9 = (bf16[128,512]{1,0:T(8,128)(2,1)S(1)}, bf16[128,512]{1,0:T(8,128)(2,1)S(1)}, u32[]{:S(2)}, u32[]{:S(2)}) collective-permute-start(bf16[128,512]{1,0:T(8,128)(2,1)S(1)} %get-tuple-element.80), channel_id=1, source_target_pairs={{0,25},{1,24},{2,27},{3,26},{4,29},{5,28},{6,31},{7,30},{8,17},{9,... | collective-permute-start | bytes 393224 | tf_op jit(solution)/shard_map/ppermute | solution.py:238
  78.9 13.9 %collective-permute-start.10 = (bf16[128,512]{1,0:T(8,128)(2,1)S(1)}, bf16[128,512]{1,0:T(8,128)(2,1)S(1)}, u32[]{:S(2)}, u32[]{:S(2)}) collective-permute-start(bf16[128,512]{1,0:T(8,128)(2,1)S(1)} %get-tuple-element.81), channel_id=1, source_target_pairs={{0,26},{1,27},{2,24},{3,25},{4,30},{5,31},{6,28},{7,29},{8,18},{9,... | collective-permute-start | bytes 393224 | tf_op jit(solution)/shard_map/ppermute | solution.py:238
  92.8 2.3 collective-permute-start.11
  95.1 3.1 %collective-permute-start.12 = (bf16[128,512]{1,0:T(8,128)(2,1)S(1)}, bf16[128,512]{1,0:T(8,128)(2,1)S(1)}, u32[]{:S(2)}, u32[]{:S(2)}) collective-permute-start(bf16[128,512]{1,0:T(8,128)(2,1)S(1)} %get-tuple-element.83), channel_id=1, source_target_pairs={{0,28},{1,29},{2,30},{3,31},{4,24},{5,25},{6,26},{7,27},{8,20},{9,... | collective-permute-start | bytes 393224 | tf_op jit(solution)/shard_map/ppermute | solution.py:238
  98.2 7.2 %collective-permute-done.8.refs_8_ = bf16[128,512]{1,0:T(8,128)(2,1)S(1)} collective-permute-done((bf16[128,512]{1,0:T(8,128)(2,1)S(1)}, bf16[128,512]{1,0:T(8,128)(2,1)S(1)}, u32[]{:S(2)}, u32[]{:S(2)}) %collective-permute-start.8) | collective-permute-done | bytes 131104 | tf_op jit(solution)/shard_map/ppermute | solution.py:238
  105.3 3.1 %collective-permute-done.9.refs_9_ = bf16[128,512]{1,0:T(8,128)(2,1)S(1)} collective-permute-done((bf16[128,512]{1,0:T(8,128)(2,1)S(1)}, bf16[128,512]{1,0:T(8,128)(2,1)S(1)}, u32[]{:S(2)}, u32[]{:S(2)}) %collective-permute-start.9) | collective-permute-done | bytes 131104 | tf_op jit(solution)/shard_map/ppermute | solution.py:238
  108.4 8.8 %collective-permute-start.14 = (bf16[128,512]{1,0:T(8,128)(2,1)S(1)}, bf16[128,512]{1,0:T(8,128)(2,1)S(1)}, u32[]{:S(2)}, u32[]{:S(2)}) collective-permute-start(bf16[128,512]{1,0:T(8,128)(2,1)S(1)} %get-tuple-element.85), channel_id=1, source_target_pairs={{0,30},{1,31},{2,28},{3,29},{4,26},{5,27},{6,24},{7,25},{8,22},{9,... | collective-permute-start | bytes 393224 | tf_op jit(solution)/shard_map/ppermute | solution.py:238
  117.2 4.2 %collective-permute-done.10.refs_10_ = bf16[128,512]{1,0:T(8,128)(2,1)S(1)} collective-permute-done((bf16[128,512]{1,0:T(8,128)(2,1)S(1)}, bf16[128,512]{1,0:T(8,128)(2,1)S(1)}, u32[]{:S(2)}, u32[]{:S(2)}) %collective-permute-start.10) | collective-permute-done | bytes 131104 | tf_op jit(solution)/shard_map/ppermute | solution.py:238
  125.1 5.5 %collective-permute-done.15.refs_15_ = bf16[128,512]{1,0:T(8,128)(2,1)S(1)} collective-permute-done((bf16[128,512]{1,0:T(8,128)(2,1)S(1)}, bf16[128,512]{1,0:T(8,128)(2,1)S(1)}, u32[]{:S(2)}, u32[]{:S(2)}) %collective-permute-start.15) | collective-permute-done | bytes 131104 | tf_op jit(solution)/shard_map/ppermute | solution.py:238
  130.6 2.2 mix.3
  132.8 9.7 %collective-permute-start.46 = (bf16[128,512]{1,0:T(8,128)(2,1)S(1)}, bf16[128,512]{1,0:T(8,128)(2,1)S(1)}, u32[]{:S(2)}, u32[]{:S(2)}) collective-permute-start(bf16[128,512]{1,0:T(8,128)(2,1)S(1)} %get-tuple-element.120), channel_id=1, source_target_pairs={{0,8},{1,9},{2,10},{3,11},{4,12},{5,13},{6,14},{7,15},{8,0},{9,1},... | collective-permute-start | bytes 393224 | tf_op jit(solution)/shard_map/ppermute | solution.py:238
  142.8 3.1 %collective-permute-start.49 = (bf16[128,512]{1,0:T(8,128)(2,1)S(1)}, bf16[128,512]{1,0:T(8,128)(2,1)S(1)}, u32[]{:S(2)}, u32[]{:S(2)}) collective-permute-start(bf16[128,512]{1,0:T(8,128)(2,1)S(1)} %get-tuple-element.123), channel_id=1, source_target_pairs={{0,11},{1,10},{2,9},{3,8},{4,15},{5,14},{6,13},{7,12},{8,3},{9,2},... | collective-permute-start | bytes 393224 | tf_op jit(solution)/shard_map/ppermute | solution.py:238
  146.7 14.2 %collective-permute-done.46.refs_0_ = bf16[128,512]{1,0:T(8,128)(2,1)S(1)} collective-permute-done((bf16[128,512]{1,0:T(8,128)(2,1)S(1)}, bf16[128,512]{1,0:T(8,128)(2,1)S(1)}, u32[]{:S(2)}, u32[]{:S(2)}) %collective-permute-start.46) | collective-permute-done | bytes 131104 | tf_op jit(solution)/shard_map/ppermute | solution.py:238
  162.7 3.0 %collective-permute-done.48.refs_2_ = bf16[128,512]{1,0:T(8,128)(2,1)S(1)} collective-permute-done((bf16[128,512]{1,0:T(8,128)(2,1)S(1)}, bf16[128,512]{1,0:T(8,128)(2,1)S(1)}, u32[]{:S(2)}, u32[]{:S(2)}) %collective-permute-start.48) | collective-permute-done | bytes 131104 | tf_op jit(solution)/shard_map/ppermute | solution.py:238
  165.7 7.3 %collective-permute-start.53 = (bf16[128,512]{1,0:T(8,128)(2,1)S(1)}, bf16[128,512]{1,0:T(8,128)(2,1)S(1)}, u32[]{:S(2)}, u32[]{:S(2)}) collective-permute-start(bf16[128,512]{1,0:T(8,128)(2,1)S(1)} %get-tuple-element.127), channel_id=1, source_target_pairs={{0,15},{1,14},{2,13},{3,12},{4,11},{5,10},{6,9},{7,8},{8,7},{9,6},... | collective-permute-start | bytes 393224 | tf_op jit(solution)/shard_map/ppermute | solution.py:238
  173.0 6.6 %collective-permute-start.55 = (bf16[128,512]{1,0:T(8,128)(2,1)S(1)}, bf16[128,512]{1,0:T(8,128)(2,1)S(1)}, u32[]{:S(2)}, u32[]{:S(2)}) collective-permute-start(bf16[128,512]{1,0:T(8,128)(2,1)S(1)} %get-tuple-element.129), channel_id=1, source_target_pairs={{0,25},{1,24},{2,27},{3,26},{4,29},{5,28},{6,31},{7,30},{8,17},{9,... | collective-permute-start | bytes 393224 | tf_op jit(solution)/shard_map/ppermute | solution.py:238
  179.6 8.9 %collective-permute-start.56 = (bf16[128,512]{1,0:T(8,128)(2,1)S(1)}, bf16[128,512]{1,0:T(8,128)(2,1)S(1)}, u32[]{:S(2)}, u32[]{:S(2)}) collective-permute-start(bf16[128,512]{1,0:T(8,128)(2,1)S(1)} %get-tuple-element.130), channel_id=1, source_target_pairs={{0,26},{1,27},{2,24},{3,25},{4,30},{5,31},{6,28},{7,29},{8,18},{9,... | collective-permute-start | bytes 393224 | tf_op jit(solution)/shard_map/ppermute | solution.py:238
  188.5 2.7 %collective-permute-start.57 = (bf16[128,512]{1,0:T(8,128)(2,1)S(1)}, bf16[128,512]{1,0:T(8,128)(2,1)S(1)}, u32[]{:S(2)}, u32[]{:S(2)}) collective-permute-start(bf16[128,512]{1,0:T(8,128)(2,1)S(1)} %get-tuple-element.131), channel_id=1, source_target_pairs={{0,27},{1,26},{2,25},{3,24},{4,31},{5,30},{6,29},{7,28},{8,19},{9,... | collective-permute-start | bytes 393224 | tf_op jit(solution)/shard_map/ppermute | solution.py:238
  191.2 9.7 %collective-permute-start.58 = (bf16[128,512]{1,0:T(8,128)(2,1)S(1)}, bf16[128,512]{1,0:T(8,128)(2,1)S(1)}, u32[]{:S(2)}, u32[]{:S(2)}) collective-permute-start(bf16[128,512]{1,0:T(8,128)(2,1)S(1)} %get-tuple-element.132), channel_id=1, source_target_pairs={{0,28},{1,29},{2,30},{3,31},{4,24},{5,25},{6,26},{7,27},{8,20},{9,... | collective-permute-start | bytes 393224 | tf_op jit(solution)/shard_map/ppermute | solution.py:238
  200.9 3.0 %collective-permute-start.59 = (bf16[128,512]{1,0:T(8,128)(2,1)S(1)}, bf16[128,512]{1,0:T(8,128)(2,1)S(1)}, u32[]{:S(2)}, u32[]{:S(2)}) collective-permute-start(bf16[128,512]{1,0:T(8,128)(2,1)S(1)} %get-tuple-element.133), channel_id=1, source_target_pairs={{0,29},{1,28},{2,31},{3,30},{4,25},{5,24},{6,27},{7,26},{8,21},{9,... | collective-permute-start | bytes 393224 | tf_op jit(solution)/shard_map/ppermute | solution.py:238
  203.9 3.8 %collective-permute-start.60 = (bf16[128,512]{1,0:T(8,128)(2,1)S(1)}, bf16[128,512]{1,0:T(8,128)(2,1)S(1)}, u32[]{:S(2)}, u32[]{:S(2)}) collective-permute-start(bf16[128,512]{1,0:T(8,128)(2,1)S(1)} %get-tuple-element.134), channel_id=1, source_target_pairs={{0,30},{1,31},{2,28},{3,29},{4,26},{5,27},{6,24},{7,25},{8,22},{9,... | collective-permute-start | bytes 393224 | tf_op jit(solution)/shard_map/ppermute | solution.py:238
  207.7 8.6 %collective-permute-done.56.refs_10_ = bf16[128,512]{1,0:T(8,128)(2,1)S(1)} collective-permute-done((bf16[128,512]{1,0:T(8,128)(2,1)S(1)}, bf16[128,512]{1,0:T(8,128)(2,1)S(1)}, u32[]{:S(2)}, u32[]{:S(2)}) %collective-permute-start.56) | collective-permute-done | bytes 131104 | tf_op jit(solution)/shard_map/ppermute | solution.py:238
  216.3 4.9 %collective-permute-start.61 = (bf16[128,512]{1,0:T(8,128)(2,1)S(1)}, bf16[128,512]{1,0:T(8,128)(2,1)S(1)}, u32[]{:S(2)}, u32[]{:S(2)}) collective-permute-start(bf16[128,512]{1,0:T(8,128)(2,1)S(1)} %get-tuple-element.135), channel_id=1, source_target_pairs={{0,31},{1,30},{2,29},{3,28},{4,27},{5,26},{6,25},{7,24},{8,23},{9,... | collective-permute-start | bytes 393224 | tf_op jit(solution)/shard_map/ppermute | solution.py:238
  221.2 2.2 mix.2
  225.4 6.1 %collective-permute-start.34 = (bf16[128,512]{1,0:T(8,128)(2,1)S(1)}, bf16[128,512]{1,0:T(8,128)(2,1)S(1)}, u32[]{:S(2)}, u32[]{:S(2)}) collective-permute-start(bf16[128,512]{1,0:T(8,128)(2,1)S(1)} %get-tuple-element.107), channel_id=1, source_target_pairs={{0,4},{1,5},{2,6},{3,7},{4,0},{5,1},{6,2},{7,3},{8,12},{9,13},{10,... | collective-permute-start | bytes 393224 | tf_op jit(solution)/shard_map/ppermute | solution.py:238
  231.6 2.5 collective-permute-start.35
  234.1 2.7 collective-permute-start.37
  236.8 2.5 collective-permute-start.38
  239.3 4.2 %collective-permute-start.40 = (bf16[128,512]{1,0:T(8,128)(2,1)S(1)}, bf16[128,512]{1,0:T(8,128)(2,1)S(1)}, u32[]{:S(2)}, u32[]{:S(2)}) collective-permute-start(bf16[128,512]{1,0:T(8,128)(2,1)S(1)} %get-tuple-element.113), channel_id=1, source_target_pairs={{0,18},{1,19},{2,16},{3,17},{4,22},{5,23},{6,20},{7,21},{8,26},{9,... | collective-permute-start | bytes 393224 | tf_op jit(solution)/shard_map/ppermute | solution.py:238
  244.8 5.1 %collective-permute-start.42 = (bf16[128,512]{1,0:T(8,128)(2,1)S(1)}, bf16[128,512]{1,0:T(8,128)(2,1)S(1)}, u32[]{:S(2)}, u32[]{:S(2)}) collective-permute-start(bf16[128,512]{1,0:T(8,128)(2,1)S(1)} %get-tuple-element.115), channel_id=1, source_target_pairs={{0,20},{1,21},{2,22},{3,23},{4,16},{5,17},{6,18},{7,19},{8,28},{9,... | collective-permute-start | bytes 393224 | tf_op jit(solution)/shard_map/ppermute | solution.py:238
  250.0 6.4 %collective-permute-done.39.refs_9_ = bf16[128,512]{1,0:T(8,128)(2,1)S(1)} collective-permute-done((bf16[128,512]{1,0:T(8,128)(2,1)S(1)}, bf16[128,512]{1,0:T(8,128)(2,1)S(1)}, u32[]{:S(2)}, u32[]{:S(2)}) %collective-permute-start.39) | collective-permute-done | bytes 131104 | tf_op jit(solution)/shard_map/ppermute | solution.py:238
  256.4 3.0 %collective-permute-start.44 = (bf16[128,512]{1,0:T(8,128)(2,1)S(1)}, bf16[128,512]{1,0:T(8,128)(2,1)S(1)}, u32[]{:S(2)}, u32[]{:S(2)}) collective-permute-start(bf16[128,512]{1,0:T(8,128)(2,1)S(1)} %get-tuple-element.117), channel_id=1, source_target_pairs={{0,22},{1,23},{2,20},{3,21},{4,18},{5,19},{6,16},{7,17},{8,30},{9,... | collective-permute-start | bytes 393224 | tf_op jit(solution)/shard_map/ppermute | solution.py:238
  262.3 2.2 collective-permute-done.44.refs_14_
  (106 shorter events, 32.3 us)
Async XLA Ops:
  11.7 11.3 %collective-permute-start.21 = (bf16[128,512]{1,0:T(8,128)(2,1)S(1)}, bf16[128,512]{1,0:T(8,128)(2,1)S(1)}, u32[]{:S(2)}, u32[]{:S(2)}) collective-permute-start(bf16[128,512]{1,0:T(8,128)(2,1)S(1)} %get-tuple-element.93), channel_id=1, source_target_pairs={{0,6},{1,7},{2,4},{3,5},{4,2},{5,3},{6,0},{7,1},{8,14},{9,15},{10,... | collective-permute-start | bytes 393224 | tf_op jit(solution)/shard_map/ppermute | solution.py:238
  14.3 12.5 %collective-permute-start.22 = (bf16[128,512]{1,0:T(8,128)(2,1)S(1)}, bf16[128,512]{1,0:T(8,128)(2,1)S(1)}, u32[]{:S(2)}, u32[]{:S(2)}) collective-permute-start(bf16[128,512]{1,0:T(8,128)(2,1)S(1)} %get-tuple-element.94), channel_id=1, source_target_pairs={{0,7},{1,6},{2,5},{3,4},{4,3},{5,2},{6,1},{7,0},{8,15},{9,14},{10,... | collective-permute-start | bytes 393224 | tf_op jit(solution)/shard_map/ppermute | solution.py:238
  16.4 13.0 %collective-permute-start.23 = (bf16[128,512]{1,0:T(8,128)(2,1)S(1)}, bf16[128,512]{1,0:T(8,128)(2,1)S(1)}, u32[]{:S(2)}, u32[]{:S(2)}) collective-permute-start(bf16[128,512]{1,0:T(8,128)(2,1)S(1)} %get-tuple-element.95), channel_id=1, source_target_pairs={{0,16},{1,17},{2,18},{3,19},{4,20},{5,21},{6,22},{7,23},{8,24},{9,... | collective-permute-start | bytes 393224 | tf_op jit(solution)/shard_map/ppermute | solution.py:238
  18.0 17.7 %collective-permute-start.24 = (bf16[128,512]{1,0:T(8,128)(2,1)S(1)}, bf16[128,512]{1,0:T(8,128)(2,1)S(1)}, u32[]{:S(2)}, u32[]{:S(2)}) collective-permute-start(bf16[128,512]{1,0:T(8,128)(2,1)S(1)} %get-tuple-element.96), channel_id=1, source_target_pairs={{0,17},{1,16},{2,19},{3,18},{4,21},{5,20},{6,23},{7,22},{8,25},{9,... | collective-permute-start | bytes 393224 | tf_op jit(solution)/shard_map/ppermute | solution.py:238
  18.5 21.1 %collective-permute-start.25 = (bf16[128,512]{1,0:T(8,128)(2,1)S(1)}, bf16[128,512]{1,0:T(8,128)(2,1)S(1)}, u32[]{:S(2)}, u32[]{:S(2)}) collective-permute-start(bf16[128,512]{1,0:T(8,128)(2,1)S(1)} %get-tuple-element.97), channel_id=1, source_target_pairs={{0,18},{1,19},{2,16},{3,17},{4,22},{5,23},{6,20},{7,21},{8,26},{9,... | collective-permute-start | bytes 393224 | tf_op jit(solution)/shard_map/ppermute | solution.py:238
  23.0 16.7 %collective-permute-start.26 = (bf16[128,512]{1,0:T(8,128)(2,1)S(1)}, bf16[128,512]{1,0:T(8,128)(2,1)S(1)}, u32[]{:S(2)}, u32[]{:S(2)}) collective-permute-start(bf16[128,512]{1,0:T(8,128)(2,1)S(1)} %get-tuple-element.98), channel_id=1, source_target_pairs={{0,19},{1,18},{2,17},{3,16},{4,23},{5,22},{6,21},{7,20},{8,27},{9,... | collective-permute-start | bytes 393224 | tf_op jit(solution)/shard_map/ppermute | solution.py:238
  26.8 15.5 %collective-permute-start.27 = (bf16[128,512]{1,0:T(8,128)(2,1)S(1)}, bf16[128,512]{1,0:T(8,128)(2,1)S(1)}, u32[]{:S(2)}, u32[]{:S(2)}) collective-permute-start(bf16[128,512]{1,0:T(8,128)(2,1)S(1)} %get-tuple-element.99), channel_id=1, source_target_pairs={{0,20},{1,21},{2,22},{3,23},{4,16},{5,17},{6,18},{7,19},{8,28},{9,... | collective-permute-start | bytes 393224 | tf_op jit(solution)/shard_map/ppermute | solution.py:238
  29.4 12.8 %collective-permute-start.28 = (bf16[128,512]{1,0:T(8,128)(2,1)S(1)}, bf16[128,512]{1,0:T(8,128)(2,1)S(1)}, u32[]{:S(2)}, u32[]{:S(2)}) collective-permute-start(bf16[128,512]{1,0:T(8,128)(2,1)S(1)} %get-tuple-element.100), channel_id=1, source_target_pairs={{0,21},{1,20},{2,23},{3,22},{4,17},{5,16},{6,19},{7,18},{8,29},{9,... | collective-permute-start | bytes 393224 | tf_op jit(solution)/shard_map/ppermute | solution.py:238
  39.6 11.4 %collective-permute-start.30 = (bf16[128,512]{1,0:T(8,128)(2,1)S(1)}, bf16[128,512]{1,0:T(8,128)(2,1)S(1)}, u32[]{:S(2)}, u32[]{:S(2)}) collective-permute-start(bf16[128,512]{1,0:T(8,128)(2,1)S(1)} %get-tuple-element.102), channel_id=1, source_target_pairs={{0,23},{1,22},{2,21},{3,20},{4,19},{5,18},{6,17},{7,16},{8,31},{9,... | collective-permute-start | bytes 393224 | tf_op jit(solution)/shard_map/ppermute | solution.py:238
  39.6 11.4 %collective-permute-start = (bf16[128,512]{1,0:T(8,128)(2,1)S(1)}, bf16[128,512]{1,0:T(8,128)(2,1)S(1)}, u32[]{:S(2)}, u32[]{:S(2)}) collective-permute-start(bf16[128,512]{1,0:T(8,128)(2,1)S(1)} %get-tuple-element.71), channel_id=1, source_target_pairs={{0,8},{1,9},{2,10},{3,11},{4,12},{5,13},{6,14},{7,15},{8,0},{9,1},... | collective-permute-start | bytes 393224 | tf_op jit(solution)/shard_map/ppermute | solution.py:238
  42.3 23.5 %collective-permute-start.1 = (bf16[128,512]{1,0:T(8,128)(2,1)S(1)}, bf16[128,512]{1,0:T(8,128)(2,1)S(1)}, u32[]{:S(2)}, u32[]{:S(2)}) collective-permute-start(bf16[128,512]{1,0:T(8,128)(2,1)S(1)} %get-tuple-element.72), channel_id=1, source_target_pairs={{0,9},{1,8},{2,11},{3,10},{4,13},{5,12},{6,15},{7,14},{8,1},{9,0},... | collective-permute-start | bytes 393224 | tf_op jit(solution)/shard_map/ppermute | solution.py:238
  42.3 26.8 %collective-permute-start.2 = (bf16[128,512]{1,0:T(8,128)(2,1)S(1)}, bf16[128,512]{1,0:T(8,128)(2,1)S(1)}, u32[]{:S(2)}, u32[]{:S(2)}) collective-permute-start(bf16[128,512]{1,0:T(8,128)(2,1)S(1)} %get-tuple-element.73), channel_id=1, source_target_pairs={{0,10},{1,11},{2,8},{3,9},{4,14},{5,15},{6,12},{7,13},{8,2},{9,3},... | collective-permute-start | bytes 393224 | tf_op jit(solution)/shard_map/ppermute | solution.py:238
  45.3 28.9 %collective-permute-start.3 = (bf16[128,512]{1,0:T(8,128)(2,1)S(1)}, bf16[128,512]{1,0:T(8,128)(2,1)S(1)}, u32[]{:S(2)}, u32[]{:S(2)}) collective-permute-start(bf16[128,512]{1,0:T(8,128)(2,1)S(1)} %get-tuple-element.74), channel_id=1, source_target_pairs={{0,11},{1,10},{2,9},{3,8},{4,15},{5,14},{6,13},{7,12},{8,3},{9,2},... | collective-permute-start | bytes 393224 | tf_op jit(solution)/shard_map/ppermute | solution.py:238
  51.0 24.1 %collective-permute-start.4 = (bf16[128,512]{1,0:T(8,128)(2,1)S(1)}, bf16[128,512]{1,0:T(8,128)(2,1)S(1)}, u32[]{:S(2)}, u32[]{:S(2)}) collective-permute-start(bf16[128,512]{1,0:T(8,128)(2,1)S(1)} %get-tuple-element.75), channel_id=1, source_target_pairs={{0,12},{1,13},{2,14},{3,15},{4,8},{5,9},{6,10},{7,11},{8,4},{9,5},... | collective-permute-start | bytes 393224 | tf_op jit(solution)/shard_map/ppermute | solution.py:238
  51.0 27.9 %collective-permute-start.5 = (bf16[128,512]{1,0:T(8,128)(2,1)S(1)}, bf16[128,512]{1,0:T(8,128)(2,1)S(1)}, u32[]{:S(2)}, u32[]{:S(2)}) collective-permute-start(bf16[128,512]{1,0:T(8,128)(2,1)S(1)} %get-tuple-element.76), channel_id=1, source_target_pairs={{0,13},{1,12},{2,15},{3,14},{4,9},{5,8},{6,11},{7,10},{8,5},{9,4},... | collective-permute-start | bytes 393224 | tf_op jit(solution)/shard_map/ppermute | solution.py:238
  65.8 27.0 %collective-permute-start.6 = (bf16[128,512]{1,0:T(8,128)(2,1)S(1)}, bf16[128,512]{1,0:T(8,128)(2,1)S(1)}, u32[]{:S(2)}, u32[]{:S(2)}) collective-permute-start(bf16[128,512]{1,0:T(8,128)(2,1)S(1)} %get-tuple-element.77), channel_id=1, source_target_pairs={{0,14},{1,15},{2,12},{3,13},{4,10},{5,11},{6,8},{7,9},{8,6},{9,7},... | collective-permute-start | bytes 393224 | tf_op jit(solution)/shard_map/ppermute | solution.py:238
  69.1 26.0 %collective-permute-start.7 = (bf16[128,512]{1,0:T(8,128)(2,1)S(1)}, bf16[128,512]{1,0:T(8,128)(2,1)S(1)}, u32[]{:S(2)}, u32[]{:S(2)}) collective-permute-start(bf16[128,512]{1,0:T(8,128)(2,1)S(1)} %get-tuple-element.78), channel_id=1, source_target_pairs={{0,15},{1,14},{2,13},{3,12},{4,11},{5,10},{6,9},{7,8},{8,7},{9,6},... | collective-permute-start | bytes 393224 | tf_op jit(solution)/shard_map/ppermute | solution.py:238
  74.2 31.1 %collective-permute-start.8 = (bf16[128,512]{1,0:T(8,128)(2,1)S(1)}, bf16[128,512]{1,0:T(8,128)(2,1)S(1)}, u32[]{:S(2)}, u32[]{:S(2)}) collective-permute-start(bf16[128,512]{1,0:T(8,128)(2,1)S(1)} %get-tuple-element.79), channel_id=1, source_target_pairs={{0,24},{1,25},{2,26},{3,27},{4,28},{5,29},{6,30},{7,31},{8,16},{9,... | collective-permute-start | bytes 393224 | tf_op jit(solution)/shard_map/ppermute | solution.py:238
  75.1 33.3 %collective-permute-start.9 = (bf16[128,512]{1,0:T(8,128)(2,1)S(1)}, bf16[128,512]{1,0:T(8,128)(2,1)S(1)}, u32[]{:S(2)}, u32[]{:S(2)}) collective-permute-start(bf16[128,512]{1,0:T(8,128)(2,1)S(1)} %get-tuple-element.80), channel_id=1, source_target_pairs={{0,25},{1,24},{2,27},{3,26},{4,29},{5,28},{6,31},{7,30},{8,17},{9,... | collective-permute-start | bytes 393224 | tf_op jit(solution)/shard_map/ppermute | solution.py:238
  78.9 42.5 %collective-permute-start.10 = (bf16[128,512]{1,0:T(8,128)(2,1)S(1)}, bf16[128,512]{1,0:T(8,128)(2,1)S(1)}, u32[]{:S(2)}, u32[]{:S(2)}) collective-permute-start(bf16[128,512]{1,0:T(8,128)(2,1)S(1)} %get-tuple-element.81), channel_id=1, source_target_pairs={{0,26},{1,27},{2,24},{3,25},{4,30},{5,31},{6,28},{7,29},{8,18},{9,... | collective-permute-start | bytes 393224 | tf_op jit(solution)/shard_map/ppermute | solution.py:238
  92.8 32.2 %collective-permute-start.11 = (bf16[128,512]{1,0:T(8,128)(2,1)S(1)}, bf16[128,512]{1,0:T(8,128)(2,1)S(1)}, u32[]{:S(2)}, u32[]{:S(2)}) collective-permute-start(bf16[128,512]{1,0:T(8,128)(2,1)S(1)} %get-tuple-element.82), channel_id=1, source_target_pairs={{0,27},{1,26},{2,25},{3,24},{4,31},{5,30},{6,29},{7,28},{8,19},{9,... | collective-permute-start | bytes 393224 | tf_op jit(solution)/shard_map/ppermute | solution.py:238
  95.1 30.0 %collective-permute-start.12 = (bf16[128,512]{1,0:T(8,128)(2,1)S(1)}, bf16[128,512]{1,0:T(8,128)(2,1)S(1)}, u32[]{:S(2)}, u32[]{:S(2)}) collective-permute-start(bf16[128,512]{1,0:T(8,128)(2,1)S(1)} %get-tuple-element.83), channel_id=1, source_target_pairs={{0,28},{1,29},{2,30},{3,31},{4,24},{5,25},{6,26},{7,27},{8,20},{9,... | collective-permute-start | bytes 393224 | tf_op jit(solution)/shard_map/ppermute | solution.py:238
  105.3 19.7 %collective-permute-start.13 = (bf16[128,512]{1,0:T(8,128)(2,1)S(1)}, bf16[128,512]{1,0:T(8,128)(2,1)S(1)}, u32[]{:S(2)}, u32[]{:S(2)}) collective-permute-start(bf16[128,512]{1,0:T(8,128)(2,1)S(1)} %get-tuple-element.84), channel_id=1, source_target_pairs={{0,29},{1,28},{2,31},{3,30},{4,25},{5,24},{6,27},{7,26},{8,21},{9,... | collective-permute-start | bytes 393224 | tf_op jit(solution)/shard_map/ppermute | solution.py:238
  108.4 16.7 %collective-permute-start.14 = (bf16[128,512]{1,0:T(8,128)(2,1)S(1)}, bf16[128,512]{1,0:T(8,128)(2,1)S(1)}, u32[]{:S(2)}, u32[]{:S(2)}) collective-permute-start(bf16[128,512]{1,0:T(8,128)(2,1)S(1)} %get-tuple-element.85), channel_id=1, source_target_pairs={{0,30},{1,31},{2,28},{3,29},{4,26},{5,27},{6,24},{7,25},{8,22},{9,... | collective-permute-start | bytes 393224 | tf_op jit(solution)/shard_map/ppermute | solution.py:238
  132.8 28.0 %collective-permute-start.46 = (bf16[128,512]{1,0:T(8,128)(2,1)S(1)}, bf16[128,512]{1,0:T(8,128)(2,1)S(1)}, u32[]{:S(2)}, u32[]{:S(2)}) collective-permute-start(bf16[128,512]{1,0:T(8,128)(2,1)S(1)} %get-tuple-element.120), channel_id=1, source_target_pairs={{0,8},{1,9},{2,10},{3,11},{4,12},{5,13},{6,14},{7,15},{8,0},{9,1},... | collective-permute-start | bytes 393224 | tf_op jit(solution)/shard_map/ppermute | solution.py:238
  142.5 20.2 %collective-permute-start.47 = (bf16[128,512]{1,0:T(8,128)(2,1)S(1)}, bf16[128,512]{1,0:T(8,128)(2,1)S(1)}, u32[]{:S(2)}, u32[]{:S(2)}) collective-permute-start(bf16[128,512]{1,0:T(8,128)(2,1)S(1)} %get-tuple-element.121), channel_id=1, source_target_pairs={{0,9},{1,8},{2,11},{3,10},{4,13},{5,12},{6,15},{7,14},{8,1},{9,0},... | collective-permute-start | bytes 393224 | tf_op jit(solution)/shard_map/ppermute | solution.py:238
  142.5 23.1 %collective-permute-start.48 = (bf16[128,512]{1,0:T(8,128)(2,1)S(1)}, bf16[128,512]{1,0:T(8,128)(2,1)S(1)}, u32[]{:S(2)}, u32[]{:S(2)}) collective-permute-start(bf16[128,512]{1,0:T(8,128)(2,1)S(1)} %get-tuple-element.122), channel_id=1, source_target_pairs={{0,10},{1,11},{2,8},{3,9},{4,14},{5,15},{6,12},{7,13},{8,2},{9,3},... | collective-permute-start | bytes 393224 | tf_op jit(solution)/shard_map/ppermute | solution.py:238
  142.8 30.2 %collective-permute-start.49 = (bf16[128,512]{1,0:T(8,128)(2,1)S(1)}, bf16[128,512]{1,0:T(8,128)(2,1)S(1)}, u32[]{:S(2)}, u32[]{:S(2)}) collective-permute-start(bf16[128,512]{1,0:T(8,128)(2,1)S(1)} %get-tuple-element.123), channel_id=1, source_target_pairs={{0,11},{1,10},{2,9},{3,8},{4,15},{5,14},{6,13},{7,12},{8,3},{9,2},... | collective-permute-start | bytes 393224 | tf_op jit(solution)/shard_map/ppermute | solution.py:238
  145.9 27.1 %collective-permute-start.50 = (bf16[128,512]{1,0:T(8,128)(2,1)S(1)}, bf16[128,512]{1,0:T(8,128)(2,1)S(1)}, u32[]{:S(2)}, u32[]{:S(2)}) collective-permute-start(bf16[128,512]{1,0:T(8,128)(2,1)S(1)} %get-tuple-element.124), channel_id=1, source_target_pairs={{0,12},{1,13},{2,14},{3,15},{4,8},{5,9},{6,10},{7,11},{8,4},{9,5},... | collective-permute-start | bytes 393224 | tf_op jit(solution)/shard_map/ppermute | solution.py:238
  160.9 18.7 %collective-permute-start.51 = (bf16[128,512]{1,0:T(8,128)(2,1)S(1)}, bf16[128,512]{1,0:T(8,128)(2,1)S(1)}, u32[]{:S(2)}, u32[]{:S(2)}) collective-permute-start(bf16[128,512]{1,0:T(8,128)(2,1)S(1)} %get-tuple-element.125), channel_id=1, source_target_pairs={{0,13},{1,12},{2,15},{3,14},{4,9},{5,8},{6,11},{7,10},{8,5},{9,4},... | collective-permute-start | bytes 393224 | tf_op jit(solution)/shard_map/ppermute | solution.py:238
  162.7 25.8 %collective-permute-start.52 = (bf16[128,512]{1,0:T(8,128)(2,1)S(1)}, bf16[128,512]{1,0:T(8,128)(2,1)S(1)}, u32[]{:S(2)}, u32[]{:S(2)}) collective-permute-start(bf16[128,512]{1,0:T(8,128)(2,1)S(1)} %get-tuple-element.126), channel_id=1, source_target_pairs={{0,14},{1,15},{2,12},{3,13},{4,10},{5,11},{6,8},{7,9},{8,6},{9,7},... | collective-permute-start | bytes 393224 | tf_op jit(solution)/shard_map/ppermute | solution.py:238
  165.7 25.5 %collective-permute-start.53 = (bf16[128,512]{1,0:T(8,128)(2,1)S(1)}, bf16[128,512]{1,0:T(8,128)(2,1)S(1)}, u32[]{:S(2)}, u32[]{:S(2)}) collective-permute-start(bf16[128,512]{1,0:T(8,128)(2,1)S(1)} %get-tuple-element.127), channel_id=1, source_target_pairs={{0,15},{1,14},{2,13},{3,12},{4,11},{5,10},{6,9},{7,8},{8,7},{9,6},... | collective-permute-start | bytes 393224 | tf_op jit(solution)/shard_map/ppermute | solution.py:238
  173.0 27.9 %collective-permute-start.54 = (bf16[128,512]{1,0:T(8,128)(2,1)S(1)}, bf16[128,512]{1,0:T(8,128)(2,1)S(1)}, u32[]{:S(2)}, u32[]{:S(2)}) collective-permute-start(bf16[128,512]{1,0:T(8,128)(2,1)S(1)} %get-tuple-element.128), channel_id=1, source_target_pairs={{0,24},{1,25},{2,26},{3,27},{4,28},{5,29},{6,30},{7,31},{8,16},{9,... | collective-permute-start | bytes 393224 | tf_op jit(solution)/shard_map/ppermute | solution.py:238
  173.0 30.9 %collective-permute-start.55 = (bf16[128,512]{1,0:T(8,128)(2,1)S(1)}, bf16[128,512]{1,0:T(8,128)(2,1)S(1)}, u32[]{:S(2)}, u32[]{:S(2)}) collective-permute-start(bf16[128,512]{1,0:T(8,128)(2,1)S(1)} %get-tuple-element.129), channel_id=1, source_target_pairs={{0,25},{1,24},{2,27},{3,26},{4,29},{5,28},{6,31},{7,30},{8,17},{9,... | collective-permute-start | bytes 393224 | tf_op jit(solution)/shard_map/ppermute | solution.py:238
  179.6 36.7 %collective-permute-start.56 = (bf16[128,512]{1,0:T(8,128)(2,1)S(1)}, bf16[128,512]{1,0:T(8,128)(2,1)S(1)}, u32[]{:S(2)}, u32[]{:S(2)}) collective-permute-start(bf16[128,512]{1,0:T(8,128)(2,1)S(1)} %get-tuple-element.130), channel_id=1, source_target_pairs={{0,26},{1,27},{2,24},{3,25},{4,30},{5,31},{6,28},{7,29},{8,18},{9,... | collective-permute-start | bytes 393224 | tf_op jit(solution)/shard_map/ppermute | solution.py:238
  188.5 35.0 %collective-permute-start.57 = (bf16[128,512]{1,0:T(8,128)(2,1)S(1)}, bf16[128,512]{1,0:T(8,128)(2,1)S(1)}, u32[]{:S(2)}, u32[]{:S(2)}) collective-permute-start(bf16[128,512]{1,0:T(8,128)(2,1)S(1)} %get-tuple-element.131), channel_id=1, source_target_pairs={{0,27},{1,26},{2,25},{3,24},{4,31},{5,30},{6,29},{7,28},{8,19},{9,... | collective-permute-start | bytes 393224 | tf_op jit(solution)/shard_map/ppermute | solution.py:238
  191.2 32.8 %collective-permute-start.58 = (bf16[128,512]{1,0:T(8,128)(2,1)S(1)}, bf16[128,512]{1,0:T(8,128)(2,1)S(1)}, u32[]{:S(2)}, u32[]{:S(2)}) collective-permute-start(bf16[128,512]{1,0:T(8,128)(2,1)S(1)} %get-tuple-element.132), channel_id=1, source_target_pairs={{0,28},{1,29},{2,30},{3,31},{4,24},{5,25},{6,26},{7,27},{8,20},{9,... | collective-permute-start | bytes 393224 | tf_op jit(solution)/shard_map/ppermute | solution.py:238
  200.9 23.1 %collective-permute-start.59 = (bf16[128,512]{1,0:T(8,128)(2,1)S(1)}, bf16[128,512]{1,0:T(8,128)(2,1)S(1)}, u32[]{:S(2)}, u32[]{:S(2)}) collective-permute-start(bf16[128,512]{1,0:T(8,128)(2,1)S(1)} %get-tuple-element.133), channel_id=1, source_target_pairs={{0,29},{1,28},{2,31},{3,30},{4,25},{5,24},{6,27},{7,26},{8,21},{9,... | collective-permute-start | bytes 393224 | tf_op jit(solution)/shard_map/ppermute | solution.py:238
  203.9 21.5 %collective-permute-start.60 = (bf16[128,512]{1,0:T(8,128)(2,1)S(1)}, bf16[128,512]{1,0:T(8,128)(2,1)S(1)}, u32[]{:S(2)}, u32[]{:S(2)}) collective-permute-start(bf16[128,512]{1,0:T(8,128)(2,1)S(1)} %get-tuple-element.134), channel_id=1, source_target_pairs={{0,30},{1,31},{2,28},{3,29},{4,26},{5,27},{6,24},{7,25},{8,22},{9,... | collective-permute-start | bytes 393224 | tf_op jit(solution)/shard_map/ppermute | solution.py:238
  216.3 15.3 %collective-permute-start.61 = (bf16[128,512]{1,0:T(8,128)(2,1)S(1)}, bf16[128,512]{1,0:T(8,128)(2,1)S(1)}, u32[]{:S(2)}, u32[]{:S(2)}) collective-permute-start(bf16[128,512]{1,0:T(8,128)(2,1)S(1)} %get-tuple-element.135), channel_id=1, source_target_pairs={{0,31},{1,30},{2,29},{3,28},{4,27},{5,26},{6,25},{7,24},{8,23},{9,... | collective-permute-start | bytes 393224 | tf_op jit(solution)/shard_map/ppermute | solution.py:238
  224.0 12.8 %collective-permute-start.33 = (bf16[128,512]{1,0:T(8,128)(2,1)S(1)}, bf16[128,512]{1,0:T(8,128)(2,1)S(1)}, u32[]{:S(2)}, u32[]{:S(2)}) collective-permute-start(bf16[128,512]{1,0:T(8,128)(2,1)S(1)} %get-tuple-element.106), channel_id=1, source_target_pairs={{0,3},{1,2},{2,1},{3,0},{4,7},{5,6},{6,5},{7,4},{8,11},{9,10},{10,... | collective-permute-start | bytes 393224 | tf_op jit(solution)/shard_map/ppermute | solution.py:238
  225.4 13.8 %collective-permute-start.34 = (bf16[128,512]{1,0:T(8,128)(2,1)S(1)}, bf16[128,512]{1,0:T(8,128)(2,1)S(1)}, u32[]{:S(2)}, u32[]{:S(2)}) collective-permute-start(bf16[128,512]{1,0:T(8,128)(2,1)S(1)} %get-tuple-element.107), channel_id=1, source_target_pairs={{0,4},{1,5},{2,6},{3,7},{4,0},{5,1},{6,2},{7,3},{8,12},{9,13},{10,... | collective-permute-start | bytes 393224 | tf_op jit(solution)/shard_map/ppermute | solution.py:238
  236.8 13.2 %collective-permute-start.38 = (bf16[128,512]{1,0:T(8,128)(2,1)S(1)}, bf16[128,512]{1,0:T(8,128)(2,1)S(1)}, u32[]{:S(2)}, u32[]{:S(2)}) collective-permute-start(bf16[128,512]{1,0:T(8,128)(2,1)S(1)} %get-tuple-element.111), channel_id=1, source_target_pairs={{0,16},{1,17},{2,18},{3,19},{4,20},{5,21},{6,22},{7,23},{8,24},{9,... | collective-permute-start | bytes 393224 | tf_op jit(solution)/shard_map/ppermute | solution.py:238
  239.3 17.1 %collective-permute-start.39 = (bf16[128,512]{1,0:T(8,128)(2,1)S(1)}, bf16[128,512]{1,0:T(8,128)(2,1)S(1)}, u32[]{:S(2)}, u32[]{:S(2)}) collective-permute-start(bf16[128,512]{1,0:T(8,128)(2,1)S(1)} %get-tuple-element.112), channel_id=1, source_target_pairs={{0,17},{1,16},{2,19},{3,18},{4,21},{5,20},{6,23},{7,22},{8,25},{9,... | collective-permute-start | bytes 393224 | tf_op jit(solution)/shard_map/ppermute | solution.py:238
  239.3 20.1 %collective-permute-start.40 = (bf16[128,512]{1,0:T(8,128)(2,1)S(1)}, bf16[128,512]{1,0:T(8,128)(2,1)S(1)}, u32[]{:S(2)}, u32[]{:S(2)}) collective-permute-start(bf16[128,512]{1,0:T(8,128)(2,1)S(1)} %get-tuple-element.113), channel_id=1, source_target_pairs={{0,18},{1,19},{2,16},{3,17},{4,22},{5,23},{6,20},{7,21},{8,26},{9,... | collective-permute-start | bytes 393224 | tf_op jit(solution)/shard_map/ppermute | solution.py:238
  243.5 18.8 %collective-permute-start.41 = (bf16[128,512]{1,0:T(8,128)(2,1)S(1)}, bf16[128,512]{1,0:T(8,128)(2,1)S(1)}, u32[]{:S(2)}, u32[]{:S(2)}) collective-permute-start(bf16[128,512]{1,0:T(8,128)(2,1)S(1)} %get-tuple-element.114), channel_id=1, source_target_pairs={{0,19},{1,18},{2,17},{3,16},{4,23},{5,22},{6,21},{7,20},{8,27},{9,... | collective-permute-start | bytes 393224 | tf_op jit(solution)/shard_map/ppermute | solution.py:238
  244.8 17.4 %collective-permute-start.42 = (bf16[128,512]{1,0:T(8,128)(2,1)S(1)}, bf16[128,512]{1,0:T(8,128)(2,1)S(1)}, u32[]{:S(2)}, u32[]{:S(2)}) collective-permute-start(bf16[128,512]{1,0:T(8,128)(2,1)S(1)} %get-tuple-element.115), channel_id=1, source_target_pairs={{0,20},{1,21},{2,22},{3,23},{4,16},{5,17},{6,18},{7,19},{8,28},{9,... | collective-permute-start | bytes 393224 | tf_op jit(solution)/shard_map/ppermute | solution.py:238
  250.0 12.3 %collective-permute-start.43 = (bf16[128,512]{1,0:T(8,128)(2,1)S(1)}, bf16[128,512]{1,0:T(8,128)(2,1)S(1)}, u32[]{:S(2)}, u32[]{:S(2)}) collective-permute-start(bf16[128,512]{1,0:T(8,128)(2,1)S(1)} %get-tuple-element.116), channel_id=1, source_target_pairs={{0,21},{1,20},{2,23},{3,22},{4,17},{5,16},{6,19},{7,18},{8,29},{9,... | collective-permute-start | bytes 393224 | tf_op jit(solution)/shard_map/ppermute | solution.py:238
  (25 other events, 741.8 us)

commit v4 on v0

--- a/solution.py
+++ b/solution.py
@@ -1,11 +1,222 @@
+import functools
 import math
 
 import jax
 import jax.numpy as jnp
+import numpy as np
 from jax import lax
+from jax.experimental import pallas as pl
+from jax.experimental.pallas import tpu as pltpu
 from jax.sharding import PartitionSpec as P
 
 SMAX = 2
+TILE = 16
+VMEM_BYTES = 40 * 1024 * 1024
+VMEM_WHOLE = 60 * 1024 * 1024
+APART = 1 << 16
+AXES = ("grp", "mom")
+
+
+def permutation(energies, momenta, rows):
+    inner = energies * momenta
+    size = inner * rows
+    matrix = np.zeros((size, size), np.float32)
+    for state in range(inner):
+        for row in range(rows):
+            matrix[row * inner + state, state * rows + row] = 1.0
+    return matrix
+
+
+def mix_kernel(matrix_ref, in_ref, out_ref):
+    devices, size, width = in_ref.shape
+    for start in range(0, size, TILE):
+        block = in_ref[:, start : start + TILE, :].reshape(devices * TILE, width)
+        mixed = jnp.dot(matrix_ref[...], block, preferred_element_type=jnp.float32)
+        out_ref[:, start : start + TILE, :] = mixed.astype(out_ref.dtype).reshape(
+            devices, TILE, width
+        )
+
+
+def unpack_kernel(perm_ref, in_ref, lesser_ref, greater_ref, held, sent):
+    pieces, rows = held.shape[1], held.shape[4]
+    copies = []
+    for side, ref in enumerate((lesser_ref, greater_ref)):
+        for piece in range(pieces):
+            moved = jnp.dot(
+                perm_ref[...], in_ref[side * pieces + piece], preferred_element_type=jnp.float32
+            )
+            held[side, piece] = moved.astype(held.dtype).reshape(held.shape[2:])
+            copy = pltpu.make_async_copy(
+                held.at[side, piece],
+                ref.at[:, 0, :, piece * rows : (piece + 1) * rows, :],
+                sent.at[side, piece],
+            )
+            copy.start()
+            copies.append(copy)
+    for copy in copies:
+        copy.wait()
+
+
+def pack_kernel(
+    shares, momenta, energies,
+    place_ref, region_ref, shift_ref, occupation_ref, coupling_ref, down_ref, across_ref,
+    perm_ref, lesser_ref, greater_ref, matrix_ref, out_ref, held, arrived, packed, sent,
+):
+    pieces, rows = held.shape[1], held.shape[4]
+    size, width = out_ref.shape[1:]
+    copies = []
+    for side, ref in enumerate((lesser_ref, greater_ref)):
+        for piece in range(pieces):
+            copy = pltpu.make_async_copy(
+                ref.at[:, 0, :, piece * rows : (piece + 1) * rows, :],
+                held.at[side, piece],
+                arrived.at[side, piece],
+            )
+            copy.start()
+            copies.append(copy)
+    build_kernel(
+        shares, momenta, energies, pieces,
+        place_ref, region_ref, shift_ref, occupation_ref, coupling_ref, down_ref, across_ref,
+        matrix_ref,
+    )
+    for side in range(2):
+        for piece in range(pieces):
+            copies[side * pieces + piece].wait()
+            block = held[side, piece].reshape(size, width)
+            moved = jnp.dot(perm_ref[...], block, preferred_element_type=jnp.float32)
+            place = side * pieces + piece
+            packed[place] = moved.astype(packed.dtype)
+            copies.append(pltpu.make_async_copy(packed.at[place], out_ref.at[place], sent.at[place]))
+            copies[-1].start()
+    for copy in copies[2 * pieces :]:
+        copy.wait()
+
+
+def build_kernel(
+    shares, momenta, energies, pieces,
+    place_ref, region_ref, shift_ref, occupation_ref, coupling_ref, down_ref, across_ref, out_ref
+):
+    points = shares * momenta
+    modes = coupling_ref.shape[1]
+    greater = lax.div(place_ref[0], jnp.int32(pieces)).astype(jnp.float32)
+    chosen = coupling_ref[region_ref[0]]
+    size = down_ref.shape[0]
+    pick = down_ref[:, 1:2] == lax.broadcasted_iota(jnp.int32, (size, points), 1)
+    pick = jnp.where(pick, 1.0, 0.0).astype(jnp.bfloat16)
+    apart = down_ref[:, 0:1] - across_ref[0:1, :]
+    total = jnp.zeros((size, size), jnp.float32)
+    for step in range(-SMAX, SMAX + 1):
+        if step == 0:
+            continue
+        row = jnp.zeros((1, points), jnp.float32)
+        for mode in range(modes):
+            filling = occupation_ref[mode] + (greater if step > 0 else 1.0 - greater)
+            weight = jnp.where(shift_ref[mode] == abs(step), filling, 0.0)
+            row = row + weight * chosen[mode : mode + 1, :]
+        wide = jnp.broadcast_to(jnp.concatenate([row, row], axis=1), (points, 2 * points))
+        turned = pltpu.roll(wide, 0, 1, stride=1, stride_axis=0)[:, :points]
+        half = jnp.dot(
+            pick, turned.astype(jnp.bfloat16), preferred_element_type=jnp.float32
+        ).astype(jnp.bfloat16)
+        full = lax.dot_general(
+            pick, half, (((1,), (1,)), ((), ())), preferred_element_type=jnp.float32
+        )
+        total = jnp.where(apart == step, full, total)
+    out_ref[...] = total.astype(out_ref.dtype)
+
+
+def params():
+    return pltpu.CompilerParams(vmem_limit_bytes=VMEM_BYTES)
+
+
+SCALARS = pl.BlockSpec(memory_space=pltpu.SMEM)
+VECTORS = pl.BlockSpec(memory_space=pltpu.VMEM)
+SLABS = pl.BlockSpec(memory_space=pl.ANY)
+
+
+def pack(place, lesser, greater, coupling, occupation, shift, region_map, shares, pieces, rows):
+    energies, _, momenta, _, columns = lesser.shape
+    devices = 2 * pieces
+    size = energies * momenta * rows
+    fold = TILE // (energies * momenta)
+    group, share, row, energy, momentum = np.unravel_index(
+        np.arange(devices * TILE), (devices // shares, shares, fold, energies, momenta)
+    )
+    code = np.stack([row * APART + group * energies + energy, share * momenta + momentum], axis=1)
+    code = code.astype(np.int32)
+    perm = jnp.asarray(permutation(energies, momenta, rows), jnp.bfloat16)
+    return pl.pallas_call(
+        functools.partial(pack_kernel, shares, momenta, energies),
+        out_shape=(
+            jax.ShapeDtypeStruct((devices * TILE, devices * TILE), jnp.bfloat16),
+            jax.ShapeDtypeStruct((devices, size, columns), lesser.dtype),
+        ),
+        in_specs=[SCALARS] * 4 + [VECTORS] * 4 + [SLABS] * 2,
+        out_specs=(VECTORS, SLABS),
+        scratch_shapes=[
+            pltpu.VMEM((2, pieces, energies, momenta, rows, columns), lesser.dtype),
+            pltpu.SemaphoreType.DMA((2, pieces)),
+            pltpu.VMEM((devices, size, columns), lesser.dtype),
+            pltpu.SemaphoreType.DMA((devices,)),
+        ],
+        compiler_params=pltpu.CompilerParams(vmem_limit_bytes=VMEM_WHOLE),
+        name="pack",
+    )(
+        place,
+        region_map,
+        shift,
+        occupation,
+        coupling,
+        jnp.asarray(code),
+        jnp.asarray(code.T),
+        perm,
+        lesser,
+        greater,
+    )
+
+
+def unpack(packed, shape, pieces, rows):
+    energies, _, momenta, _, columns = shape
+    perm = jnp.asarray(permutation(energies, momenta, rows).T, jnp.bfloat16)
+    out = jax.ShapeDtypeStruct(shape, packed.dtype)
+    return pl.pallas_call(
+        unpack_kernel,
+        out_shape=(out, out),
+        in_specs=[VECTORS, VECTORS],
+        out_specs=(SLABS, SLABS),
+        scratch_shapes=[
+            pltpu.VMEM((2, pieces, energies, momenta, rows, columns), packed.dtype),
+            pltpu.SemaphoreType.DMA((2, pieces)),
+        ],
+        compiler_params=params(),
+        name="unpack",
+    )(perm, packed)
+
+
+def mix(matrix, received):
+    return pl.pallas_call(
+        mix_kernel,
+        out_shape=jax.ShapeDtypeStruct(received.shape, received.dtype),
+        in_specs=[VECTORS, VECTORS],
+        out_specs=VECTORS,
+        compiler_params=params(),
+        name="mix",
+    )(matrix, received)
+
+
+def exchange(array):
+    return lax.all_to_all(array, AXES, split_axis=0, concat_axis=0, tiled=True)
+
+
+def by_rows(lesser, greater, coupling, occupation, shift, region_map, groups, shares):
+    pieces = groups * shares // 2
+    rows = lesser.shape[3] // pieces
+    place = (lax.axis_index("grp") * shares + lax.axis_index("mom")).astype(jnp.int32).reshape(1)
+    matrix, sent = pack(
+        place, lesser, greater, coupling, occupation, shift, region_map, shares, pieces, rows
+    )
+    returned = exchange(mix(matrix, exchange(sent)))
+    return unpack(returned, lesser.shape, pieces, rows)
 
 
 def with_halo(shard, sides, width):
@@ -90,7 +301,7 @@
     return (jnp.concatenate([real_part, imag_part], axis=-1) * (1.0 / points)).astype(jnp.bfloat16)
 
 
-def on_device(lesser, greater, coupling, occupation, shift, region_map):
+def by_groups(lesser, greater, coupling, occupation, shift, region_map):
     stacked = jnp.stack([lesser, greater])
     widened = with_halo(stacked, (("grp", 1),), SMAX)
     regrouped = lax.all_to_all(widened, "mom", split_axis=4, concat_axis=3, tiled=True)
@@ -107,9 +318,28 @@
     return (returned[0], returned[1])
 
 
+def on_device(groups, shares, lesser, greater, coupling, occupation, shift, region_map):
+    energies, blocks, momenta, height, columns = lesser.shape
+    devices = groups * shares
+    states = energies * momenta
+    whole_tiles = (
+        blocks == 1
+        and devices >= 4
+        and devices & (devices - 1) == 0
+        and height % (TILE * (devices // 2)) == 0
+        and TILE % states == 0
+        and columns % 128 == 0
+    )
+    if whole_tiles:
+        return by_rows(
+            lesser, greater, coupling, occupation, shift, region_map, groups, shares
+        )
+    return by_groups(lesser, greater, coupling, occupation, shift, region_map)
+
+
 def solution(mesh):
     return jax.shard_map(
-        on_device,
+        functools.partial(on_device, mesh.shape["grp"], mesh.shape["mom"]),
         mesh=mesh,
         in_specs=(
             P("grp", None, "mom", None, None),

time: 638 us -> 215 us (0.34)
  waiting for transfers between devices: 296 us -> 0 us
  other arithmetic: 94.3 us -> 0 us
  blocking collectives: 145 us -> 198 us
  local copies, waits for them, and re-layouts: 43.1 us -> 0.01 us
  matrix products: 30.5 us -> 0 us
  Pallas kernels: 0 us -> 14.9 us
  starting transfers between devices: 13.6 us -> 0 us
  between operations: 13.9 us -> 1.32 us
    all_to_all x1 -> x0, waiting for transfers between devices: 206 us -> none  [on_device(): lax.all_to_all(widened, 'mom', split_axis=4, concat_axis=3, tiled=True)]
    ppermute x2 -> x0, waiting for transfers between devices: 89.6 us -> none  [the longest x1 88.1 us: with_halo(): after = lax.ppermute(first, axis, down)]
    all_to_all x1 -> x2, blocking collectives: 145 us -> 198 us  [exchange(): return lax.all_to_all(array, AXES, split_axis=0, concat_axis=0, tiled=True)]
    concatenate x3 -> x0, other arithmetic: 48.1 us -> none  [the longest x2 37.4 us: inverse(): jnp.concatenate([sigma_real, sigma_imag], axis=-1).astype(jnp.bfloat16)]
    sub x2 -> x0, other arithmetic: 37.8 us -> none  [the longest x1 27.6 us: forward(): cosine[..., columns:] - sine[..., :columns]]
    dot_general x4 -> x0, matrix products: 30.5 us -> none  [the longest x1 21.9 us: forward(): jnp.einsum('pk,aebkxw->aebpxw', basis_low, stacked, preferred_element_typ...]
    another operation x2 -> x0, local copies, waits for them, and re-layouts: 24.1 us -> none
    pallas_call x0 -> x3, Pallas kernels: none -> 14.9 us  [the longest x1 10.1 us: pack(): pl.pallas_call(functools.partial(pack_kernel, shares, momenta, energies),...]
  transfers between devices with their start and end apart: 3 -> 0, of which waited for: 3 -> 0; matrix products, arithmetic and copies ran while one was open for 1% -> 0% of each run, Pallas kernels for 0% -> 0%
where the time goes in v4:
time: 215 us
  blocking collectives  198 us (92%)
  Pallas kernels  14.9 us (7%)
    all_to_all x2, blocking collectives, exchange(): return lax.all_to_all(array, AXES, split_axis=0, concat_axis=0, tiled=True)  198 us
    pallas_call x1, Pallas kernels, pack(): pl.pallas_call(functools.partial(pack_kernel, shares, momenta, energies),...  10.1 us

profile of v4, /device:TPU:0, one launch (start us, length us, event | category | flops | bytes accessed | tf_op | source)
XLA Modules:
  0.0 214.7 jit_solution(15413846862936741080)
XLA Ops:
  1.3 10.1 %pack.1 = (bf16[512,512]{1,0:T(8,128)(2,1)}, bf16[32,128,512]{2,1,0:T(8,128)(2,1)}) custom-call(s32[1]{0:T(128)} %bitcast.place_ref, s32[1]{0:T(128)S(6)} %copy.12.region_ref, s32[4]{0:T(128)} %shift_ref.1, f32[4]{0:T(128)} %occupation_ref.1, f32[4,4,64]{2,1,0:T(4,128)} %coupling_ref.1, s32[512,2]{1,0:T(8,128)} %constant.20.clone.down_ref, ...), custom_call_target="tpu_custom_call" | custom-call | tf_op jit(solution)/shard_map/pack/pallas_call | solution.py:148
  11.4 0.0 copy-start
  11.4 102.0 %all_to_all.10.in_ref = bf16[32,128,512]{2,1,0:T(8,128)(2,1)S(1)} all-to-all(bf16[32,128,512]{2,1,0:T(8,128)(2,1)} %get-tuple-element.5), channel_id=1, replica_groups=mesh['grp'=2,'mom'=16] {'grp','mom'}, dimensions={0} | all-to-all | bytes 8388608 | tf_op jit(solution)/shard_map/all_to_all | solution.py:208
  113.4 0.0 copy-done
  113.4 2.3 %mix.1 = bf16[32,128,512]{2,1,0:T(8,128)(2,1)S(1)} custom-call(bf16[512,512]{1,0:T(8,128)(2,1)S(1)} %copy-done, bf16[32,128,512]{2,1,0:T(8,128)(2,1)S(1)} %all_to_all.10.in_ref), custom_call_target="tpu_custom_call" | custom-call | tf_op jit(solution)/shard_map/mix/pallas_call | solution.py:197
  115.8 0.0 copy-start.1
  115.8 96.4 %all_to_all.11.in_ref = bf16[32,128,512]{2,1,0:T(8,128)(2,1)S(1)} all-to-all(bf16[32,128,512]{2,1,0:T(8,128)(2,1)S(1)} %mix.1), channel_id=1, replica_groups=mesh['grp'=2,'mom'=16] {'grp','mom'}, dimensions={0} | all-to-all | bytes 8388608 | tf_op jit(solution)/shard_map/all_to_all | solution.py:208
  212.2 0.0 copy-done.1
  212.3 2.4 %unpack.1 = (bf16[2,1,4,256,512]{4,3,2,1,0:T(8,128)(2,1)}, bf16[2,1,4,256,512]{4,3,2,1,0:T(8,128)(2,1)}) custom-call(bf16[128,128]{1,0:T(8,128)(2,1)S(1)} %copy-done.1, bf16[32,128,512]{2,1,0:T(8,128)(2,1)S(1)} %all_to_all.11.in_ref), custom_call_target="tpu_custom_call" | custom-call | tf_op jit(solution)/shard_map/unpack/pallas_call | solution.py:182
Async XLA Ops:
  11.4 102.0 %copy-start = (bf16[512,512]{1,0:T(8,128)(2,1)S(1)}, bf16[512,512]{1,0:T(8,128)(2,1)}, u32[]{:S(2)}) copy-start(bf16[512,512]{1,0:T(8,128)(2,1)} %get-tuple-element.4.matrix_ref) | copy-start | bytes 1572868
  115.8 96.5 %copy-start.1 = (bf16[128,128]{1,0:T(8,128)(2,1)S(1)}, bf16[128,128]{1,0:T(8,128)(2,1)}, u32[]{:S(2)}) copy-start(bf16[128,128]{1,0:T(8,128)(2,1)} %constant.22.clone.perm_ref) | copy-start | bytes 98308

commit v5 on v0

--- a/solution.py
+++ b/solution.py
@@ -1,11 +1,338 @@
+import functools
 import math
 
 import jax
 import jax.numpy as jnp
+import numpy as np
 from jax import lax
+from jax.experimental import pallas as pl
+from jax.experimental.pallas import tpu as pltpu
 from jax.sharding import PartitionSpec as P
 
 SMAX = 2
+TILE = 16
+VMEM_BYTES = 60 * 1024 * 1024
+APART = 1 << 16
+
+
+def permutation(energies, momenta, rows):
+    inner = energies * momenta
+    size = inner * rows
+    matrix = np.zeros((size, size), np.float32)
+    for state in range(inner):
+        for row in range(rows):
+            matrix[row * inner + state, state * rows + row] = 1.0
+    return matrix
+
+
+def quarter(place_ref, turn, rows):
+    return pl.ds(pl.multiple_of((place_ref[0] ^ turn) * rows, rows), rows)
+
+
+def cut_kernel(chunk, place_ref, lesser_ref, greater_ref, *refs):
+    outs, sent = refs[-4:-1], refs[-1]
+    rows, width = outs[0].shape[3:]
+    copies = []
+    for turn, out in enumerate(outs, 1):
+        for side, ref in enumerate((lesser_ref, greater_ref)):
+            copies.append(
+                pltpu.make_async_copy(
+                    ref.at[:, 0, :, quarter(place_ref, turn, rows), pl.ds(chunk * width, width)],
+                    out.at[side],
+                    sent.at[turn, side],
+                )
+            )
+            copies[-1].start()
+    for copy in copies:
+        copy.wait()
+
+
+def join_kernel(chunk, place_ref, *refs):
+    turns = len(refs[0:4])
+    ins, sent = refs[:turns], refs[-1]
+    outs = refs[-3:-1]
+    rows, width = ins[0].shape[3:]
+    copies = []
+    for turn, part in enumerate(ins):
+        for side, ref in enumerate(outs):
+            copies.append(
+                pltpu.make_async_copy(
+                    part.at[side],
+                    ref.at[:, 0, :, quarter(place_ref, turn, rows), pl.ds(chunk * width, width)],
+                    sent.at[turn, side],
+                )
+            )
+            copies[-1].start()
+    for copy in copies:
+        copy.wait()
+
+
+def pack_kernel(chunk, place_ref, perm_ref, lesser_ref, greater_ref, *refs):
+    others, (out_ref, held, packed, arrived, sent) = refs[:3], refs[3:]
+    height, width = held.shape[4:]
+    size = packed.shape[2]
+    rows = TILE
+    own = [
+        pltpu.make_async_copy(
+            ref.at[:, 0, :, quarter(place_ref, 0, height), pl.ds(chunk * width, width)],
+            held.at[0, side],
+            arrived.at[0, side],
+        )
+        for side, ref in enumerate((lesser_ref, greater_ref))
+    ]
+    come = [own] + [
+        [pltpu.make_async_copy(part, held.at[turn], arrived.at[turn, 0])]
+        for turn, part in enumerate(others, 1)
+    ]
+    for copies in come:
+        for copy in copies:
+            copy.start()
+    gone = []
+    for turn, copies in enumerate(come):
+        for copy in copies:
+            copy.wait()
+        for side in range(2):
+            for piece in range(height // rows):
+                block = held[turn, side, :, :, piece * rows : (piece + 1) * rows, :]
+                moved = jnp.dot(
+                    perm_ref[...], block.reshape(size, width), preferred_element_type=jnp.float32
+                )
+                packed[side * (height // rows) + piece, turn] = moved.astype(packed.dtype)
+        gone.append(pltpu.make_async_copy(packed.at[:, turn], out_ref.at[:, turn], sent.at[turn]))
+        gone[-1].start()
+    for copy in gone:
+        copy.wait()
+
+
+def unpack_kernel(perm_ref, in_ref, *refs):
+    outs, (held, packed, arrived, sent) = refs[:4], refs[4:]
+    height, width = held.shape[4:]
+    rows = TILE
+    order = list(range(1, len(outs))) + [0]
+    come = {
+        turn: pltpu.make_async_copy(in_ref.at[:, turn], packed.at[:, turn], arrived.at[turn])
+        for turn in order
+    }
+    for turn in order:
+        come[turn].start()
+    gone = []
+    for turn in order:
+        come[turn].wait()
+        for side in range(2):
+            for piece in range(height // rows):
+                moved = jnp.dot(
+                    perm_ref[...],
+                    packed[side * (height // rows) + piece, turn],
+                    preferred_element_type=jnp.float32,
+                )
+                held[turn, side, :, :, piece * rows : (piece + 1) * rows, :] = moved.astype(
+                    held.dtype
+                ).reshape(held.shape[2], held.shape[3], rows, width)
+        gone.append(pltpu.make_async_copy(held.at[turn], outs[turn], sent.at[turn]))
+        gone[-1].start()
+    for copy in gone:
+        copy.wait()
+
+
+def mix_kernel(matrix_ref, in_ref, out_ref):
+    planes, turns, size, width = in_ref.shape
+    for start in range(0, size, 4 * TILE):
+        blocks = [
+            in_ref[:, :, start + step : start + step + TILE, :].reshape(planes * turns * TILE, width)
+            for step in range(0, 4 * TILE, TILE)
+        ]
+        mixed = jnp.dot(
+            matrix_ref[...], jnp.concatenate(blocks, axis=1), preferred_element_type=jnp.float32
+        ).astype(out_ref.dtype)
+        for step in range(4):
+            out_ref[:, :, start + step * TILE : start + (step + 1) * TILE, :] = mixed[
+                :, step * width : (step + 1) * width
+            ].reshape(planes, turns, TILE, width)
+
+
+def build_kernel(
+    points, place_ref, region_ref, shift_ref, occupation_ref, coupling_ref, down_ref, across_ref, out_ref
+):
+    modes = coupling_ref.shape[1]
+    greater = place_ref[1].astype(jnp.float32)
+    chosen = coupling_ref[region_ref[0]]
+    size = down_ref.shape[0]
+    momentum = (down_ref[:, 1:2] ^ place_ref[0]) * down_ref[:, 3:4] + down_ref[:, 2:3]
+    pick = momentum == lax.broadcasted_iota(jnp.int32, (size, points), 1)
+    pick = jnp.where(pick, 1.0, 0.0).astype(jnp.bfloat16)
+    apart = down_ref[:, 0:1] - across_ref[0:1, :]
+    total = jnp.zeros((size, size), jnp.float32)
+    for step in range(-SMAX, SMAX + 1):
+        if step == 0:
+            continue
+        row = jnp.zeros((1, points), jnp.float32)
+        for mode in range(modes):
+            filling = occupation_ref[mode] + (greater if step > 0 else 1.0 - greater)
+            weight = jnp.where(shift_ref[mode] == abs(step), filling, 0.0)
+            row = row + weight * chosen[mode : mode + 1, :]
+        wide = jnp.broadcast_to(jnp.concatenate([row, row], axis=1), (points, 2 * points))
+        turned = pltpu.roll(wide, 0, 1, stride=1, stride_axis=0)[:, :points]
+        half = jnp.dot(
+            pick, turned.astype(jnp.bfloat16), preferred_element_type=jnp.float32
+        ).astype(jnp.bfloat16)
+        full = lax.dot_general(
+            pick, half, (((1,), (1,)), ((), ())), preferred_element_type=jnp.float32
+        )
+        total = jnp.where(apart == step, full, total)
+    out_ref[...] = total.astype(out_ref.dtype)
+
+
+def params():
+    return pltpu.CompilerParams(vmem_limit_bytes=VMEM_BYTES)
+
+
+SCALARS = pl.BlockSpec(memory_space=pltpu.SMEM)
+VECTORS = pl.BlockSpec(memory_space=pltpu.VMEM)
+ANYWHERE = pl.BlockSpec(memory_space=pl.ANY)
+
+
+def build(place, coupling, occupation, shift, region_map, groups, inner, outer, energies, momenta):
+    points = inner * outer * momenta
+    group, share, turn, row, energy, momentum = np.unravel_index(
+        np.arange(groups * inner * outer * TILE),
+        (groups, inner, outer, TILE // (energies * momenta), energies, momenta),
+    )
+    code = np.stack(
+        [
+            row * APART + group * energies + energy,
+            turn,
+            share * momenta + momentum,
+            np.full_like(turn, inner * momenta),
+        ],
+        axis=1,
+    ).astype(np.int32)
+    size = code.shape[0]
+    return pl.pallas_call(
+        functools.partial(build_kernel, points),
+        out_shape=jax.ShapeDtypeStruct((size, size), jnp.bfloat16),
+        in_specs=[SCALARS] * 4 + [VECTORS] * 3,
+        out_specs=VECTORS,
+        compiler_params=params(),
+        name="build",
+    )(
+        place, region_map, shift, occupation, coupling, jnp.asarray(code), jnp.asarray(code[:, :1].T)
+    )
+
+
+def cut(place, lesser, greater, before, chunk, width, height):
+    energies, _, momenta, _, _ = lesser.shape
+    part = jax.ShapeDtypeStruct((2, energies, momenta, height, width), lesser.dtype)
+    return pl.pallas_call(
+        functools.partial(cut_kernel, chunk),
+        out_shape=(part,) * 3,
+        in_specs=[SCALARS, ANYWHERE, ANYWHERE] + [ANYWHERE] * len(before),
+        out_specs=(ANYWHERE,) * 3,
+        scratch_shapes=[pltpu.SemaphoreType.DMA((4, 2))],
+        compiler_params=params(),
+        name="cut",
+    )(place, lesser, greater, *before)
+
+
+def join(place, parts, filled, shape, chunk):
+    out = jax.ShapeDtypeStruct(shape, parts[0].dtype)
+    return pl.pallas_call(
+        functools.partial(join_kernel, chunk),
+        out_shape=(out, out),
+        in_specs=[SCALARS] + [ANYWHERE] * (len(parts) + len(filled)),
+        out_specs=(ANYWHERE, ANYWHERE),
+        scratch_shapes=[pltpu.SemaphoreType.DMA((4, 2))],
+        input_output_aliases={1 + len(parts) + side: side for side in range(len(filled))},
+        compiler_params=params(),
+        name="join",
+    )(place, *parts, *filled)
+
+
+def staging(energies, momenta, height, width, inner, dtype):
+    size = energies * momenta * TILE
+    return [
+        pltpu.VMEM((4, 2, energies, momenta, height, width), dtype),
+        pltpu.VMEM((2 * inner, 4, size, width), dtype),
+    ]
+
+
+def pack(place, lesser, greater, others, chunk, inner):
+    _, energies, momenta, height, width = others[0].shape
+    size = energies * momenta * TILE
+    perm = jnp.asarray(permutation(energies, momenta, TILE), jnp.bfloat16)
+    return pl.pallas_call(
+        functools.partial(pack_kernel, chunk),
+        out_shape=jax.ShapeDtypeStruct((2 * inner, 4, size, width), lesser.dtype),
+        in_specs=[SCALARS, VECTORS] + [ANYWHERE] * 5,
+        out_specs=ANYWHERE,
+        scratch_shapes=staging(energies, momenta, height, width, inner, lesser.dtype)
+        + [pltpu.SemaphoreType.DMA((4, 2)), pltpu.SemaphoreType.DMA((4,))],
+        compiler_params=params(),
+        name="pack",
+    )(place, perm, lesser, greater, *others)
+
+
+def unpack(packed, energies, momenta, height, inner):
+    width = packed.shape[3]
+    perm = jnp.asarray(permutation(energies, momenta, TILE).T, jnp.bfloat16)
+    part = jax.ShapeDtypeStruct((2, energies, momenta, height, width), packed.dtype)
+    return pl.pallas_call(
+        unpack_kernel,
+        out_shape=(part,) * 4,
+        in_specs=[VECTORS, ANYWHERE],
+        out_specs=(ANYWHERE,) * 4,
+        scratch_shapes=staging(energies, momenta, height, width, inner, packed.dtype)
+        + [pltpu.SemaphoreType.DMA((4,)), pltpu.SemaphoreType.DMA((4,))],
+        compiler_params=params(),
+        name="unpack",
+    )(perm, packed)
+
+
+def mix(matrix, received):
+    return pl.pallas_call(
+        mix_kernel,
+        out_shape=jax.ShapeDtypeStruct(received.shape, received.dtype),
+        in_specs=[VECTORS, VECTORS],
+        out_specs=VECTORS,
+        compiler_params=params(),
+        name="mix",
+    )(matrix, received)
+
+
+def in_plane(array):
+    return lax.all_to_all(array, ("grp", "inner"), split_axis=0, concat_axis=0, tiled=True)
+
+
+def across(parts, outer):
+    return [
+        lax.ppermute(part, "outer", [(at, at ^ turn) for at in range(outer)])
+        for turn, part in enumerate(parts, 1)
+    ]
+
+
+def by_rows(lesser, greater, coupling, occupation, shift, region_map, groups, outer, inner):
+    energies, _, momenta, rows, columns = lesser.shape
+    height = rows // outer
+    width = 128
+    chunks = columns // width
+    place = jnp.stack([lax.axis_index("outer"), lax.axis_index("grp")]).astype(jnp.int32)
+    matrix = build(
+        place, coupling, occupation, shift, region_map, groups, inner, outer, energies, momenta
+    )
+    cuts, come = [], []
+    for chunk in range(chunks):
+        before = cuts[-1][:1] if chunk else []
+        if chunk > 1:
+            before = list(before) + come[chunk - 2][:1]
+        cuts.append(cut(place, lesser, greater, before, chunk, width, height))
+        come.append(across(cuts[-1], outer))
+    filled = ()
+    for chunk in range(chunks):
+        received = in_plane(pack(place, lesser, greater, come[chunk], chunk, inner))
+        returned = in_plane(mix(matrix, received))
+        parts = unpack(returned, energies, momenta, height, inner)
+        parts = [parts[0]] + across(parts[1:], outer)
+        filled = join(place, parts, filled, lesser.shape, chunk)
+    return filled
 
 
 def with_halo(shard, sides, width):
@@ -90,10 +417,10 @@
     return (jnp.concatenate([real_part, imag_part], axis=-1) * (1.0 / points)).astype(jnp.bfloat16)
 
 
-def on_device(lesser, greater, coupling, occupation, shift, region_map):
+def by_groups(lesser, greater, coupling, occupation, shift, region_map, momentum):
     stacked = jnp.stack([lesser, greater])
     widened = with_halo(stacked, (("grp", 1),), SMAX)
-    regrouped = lax.all_to_all(widened, "mom", split_axis=4, concat_axis=3, tiled=True)
+    regrouped = lax.all_to_all(widened, momentum, split_axis=4, concat_axis=3, tiled=True)
     points = regrouped.shape[3]
     basis = dft_basis(points)
     basis_low = basis.astype(jnp.bfloat16)
@@ -103,22 +430,40 @@
         hat_real, hat_imag, spec_real, spec_imag, occupation, shift, lesser.shape[0]
     )
     result = inverse(sigma_real, sigma_imag, basis_low)
-    returned = lax.all_to_all(result, "mom", split_axis=3, concat_axis=4, tiled=True)
+    returned = lax.all_to_all(result, momentum, split_axis=3, concat_axis=4, tiled=True)
     return (returned[0], returned[1])
 
 
+def whole_tiles(shape, groups, outer, inner):
+    energies, blocks, momenta, rows, columns = shape
+    return (
+        groups == 2
+        and outer == 4
+        and blocks == 1
+        and rows == TILE * outer * inner
+        and TILE % (energies * momenta) == 0
+        and columns % 128 == 0
+    )
+
+
 def solution(mesh):
+    groups, shares = mesh.shape["grp"], mesh.shape["mom"]
+    outer, inner = 4, shares // 4
+    split = jax.sharding.Mesh(
+        mesh.devices.reshape(groups, outer, inner), ("grp", "outer", "inner")
+    )
+    momentum = ("outer", "inner")
+
+    def on_device(lesser, *rest):
+        if whole_tiles(lesser.shape, groups, outer, inner):
+            return by_rows(lesser, *rest, groups, outer, inner)
+        return by_groups(lesser, *rest, momentum)
+
+    slab = P("grp", None, momentum, None, None)
     return jax.shard_map(
         on_device,
-        mesh=mesh,
-        in_specs=(
-            P("grp", None, "mom", None, None),
-            P("grp", None, "mom", None, None),
-            P(),
-            P(),
-            P(),
-            P(),
-        ),
-        out_specs=(P("grp", None, "mom", None, None), P("grp", None, "mom", None, None)),
+        mesh=split,
+        in_specs=(slab, slab, P(), P(), P(), P()),
+        out_specs=(slab, slab),
         check_vma=False,
     )

time: 638 us -> 526 us (0.82)
  Pallas kernels: 0 us -> 280 us
  waiting for transfers between devices: 296 us -> 145 us
  blocking collectives: 145 us -> 0 us
  other arithmetic: 94.3 us -> 0.58 us
  starting transfers between devices: 13.6 us -> 90.1 us
  local copies, waits for them, and re-layouts: 43.1 us -> 7.68 us
  matrix products: 30.5 us -> 0 us
  between operations: 13.9 us -> 1.88 us
    pallas_call x0 -> x21, Pallas kernels: none -> 280 us  [the longest x4 134 us: join(): pl.pallas_call(functools.partial(join_kernel, chunk), out_shape=(out, out...]
    all_to_all x1 -> x8, waiting for transfers between devices: 206 us -> 45 us  [in_plane(): lax.all_to_all(array, ('grp', 'inner'), split_axis=0, concat_axis=0, tile...]
    all_to_all x1 -> x0, blocking collectives: 145 us -> none  [on_device(): lax.all_to_all(result, 'mom', split_axis=3, concat_axis=4, tiled=True)]
    ppermute x2 -> x24, starting transfers between devices: 6.7 us -> 59.6 us  [across(): lax.ppermute(part, 'outer', [(at, at ^ turn) for at in range(outer)])]
    concatenate x3 -> x0, other arithmetic: 48.1 us -> none  [the longest x2 37.4 us: inverse(): jnp.concatenate([sigma_real, sigma_imag], axis=-1).astype(jnp.bfloat16)]
    sub x2 -> x0, other arithmetic: 37.8 us -> none  [the longest x1 27.6 us: forward(): cosine[..., columns:] - sine[..., :columns]]
    dot_general x4 -> x0, matrix products: 30.5 us -> none  [the longest x1 21.9 us: forward(): jnp.einsum('pk,aebkxw->aebpxw', basis_low, stacked, preferred_element_typ...]
    another operation x2 -> x0, local copies, waits for them, and re-layouts: 24.1 us -> none
  transfers between devices with their start and end apart: 3 -> 32, of which waited for: 3 -> 16; matrix products, arithmetic and copies ran while one was open for 1% -> 0% of each run, Pallas kernels for 0% -> 41%
where the time goes in v5:
time: 526 us; the launch traced here: 525 us
  Pallas kernels  280 us (53%)
  waiting for transfers between devices  145 us (28%)
  starting transfers between devices  90.1 us (17%)
  local copies, waits for them, and re-layouts  7.68 us (1%)
    pallas_call x4, Pallas kernels, join(): pl.pallas_call(functools.partial(join_kernel, chunk), out_shape=(out, out...  134 us
    pallas_call x4, Pallas kernels, cut(): pl.pallas_call(functools.partial(cut_kernel, chunk), out_shape=(part,) *...  103 us
    ppermute x24, waiting for transfers between devices, across(): lax.ppermute(part, 'outer', [(at, at ^ turn) for at in range(outer)])  99.5 us
    ppermute x24, starting transfers between devices, across(): lax.ppermute(part, 'outer', [(at, at ^ turn) for at in range(outer)])  59.6 us
    all_to_all x8, waiting for transfers between devices, in_plane(): lax.all_to_all(array, ('grp', 'inner'), split_axis=0, concat_axis=0, tile...  45 us
    all_to_all x8, starting transfers between devices, in_plane(): lax.all_to_all(array, ('grp', 'inner'), split_axis=0, concat_axis=0, tile...  30.5 us
    pallas_call x4, Pallas kernels, pack(): pl.pallas_call(functools.partial(pack_kernel, chunk), out_shape=jax.Shape...  13.7 us
    pallas_call x4, Pallas kernels, unpack(): pl.pallas_call(unpack_kernel, out_shape=(part,) * 4, in_specs=[VECTORS, A...  13.5 us
  transfers between devices with their start and end apart: 32, of which 16 were waited for; matrix products, arithmetic and copies ran while one was open for 0% of the time, Pallas kernels for 41%

profile of v5, /device:TPU:0, one launch (start us, length us, event | category | flops | bytes accessed | tf_op | source)
XLA Modules:
  0.0 524.8 jit_solution(10188236455212590448)
XLA Ops:
  1.2 25.7 %cut.4 = (bf16[2,2,4,64,128]{4,3,2,1,0:T(8,128)(2,1)}, bf16[2,2,4,64,128]{4,3,2,1,0:T(8,128)(2,1)}, bf16[2,2,4,64,128]{4,3,2,1,0:T(8,128)(2,1)}) custom-call(s32[2]{0:T(128)} %pad_add_fusion.place_ref, bf16[2,1,4,256,512]{4,3,2,1,0:T(8,128)(2,1)} %lesser_ref.15, bf16[2,1,4,256,512]{4,3,2,1,0:T(8,128)(2,1)} %greater_ref.15), custom_call_target="tpu_custom_call" | custom-call | tf_op jit(solution)/shard_map/cut/pallas_call | solution.py:225
  32.6 8.8 %collective-permute-done.refs_1_.refs_0_ = bf16[2,2,4,64,128]{4,3,2,1,0:T(8,128)(2,1)S(1)} collective-permute-done((bf16[2,2,4,64,128]{4,3,2,1,0:T(8,128)(2,1)}, bf16[2,2,4,64,128]{4,3,2,1,0:T(8,128)(2,1)S(1)}, u32[]{:S(2)}, u32[]{:S(2)}) %collective-permute-start) | collective-permute-done | bytes 262176 | tf_op jit(solution)/shard_map/ppermute | solution.py:307
  41.3 10.2 %collective-permute-done.19.refs_1_ = bf16[2,2,4,64,128]{4,3,2,1,0:T(8,128)(2,1)S(1)} collective-permute-done((bf16[2,2,4,64,128]{4,3,2,1,0:T(8,128)(2,1)}, bf16[2,2,4,64,128]{4,3,2,1,0:T(8,128)(2,1)S(1)}, u32[]{:S(2)}, u32[]{:S(2)}) %collective-permute-start.19) | collective-permute-done | bytes 262176 | tf_op jit(solution)/shard_map/ppermute | solution.py:307
  53.0 3.4 pack.7
  56.4 3.7 all-to-all-start.6
  60.1 25.7 %cut.5 = (bf16[2,2,4,64,128]{4,3,2,1,0:T(8,128)(2,1)}, bf16[2,2,4,64,128]{4,3,2,1,0:T(8,128)(2,1)}, bf16[2,2,4,64,128]{4,3,2,1,0:T(8,128)(2,1)}) custom-call(s32[2]{0:T(128)} %pad_add_fusion.place_ref, bf16[2,1,4,256,512]{4,3,2,1,0:T(8,128)(2,1)} %lesser_ref.15, bf16[2,1,4,256,512]{4,3,2,1,0:T(8,128)(2,1)} %greater_ref.15, ...), custom_call_target="tpu_custom_call" | custom-call | tf_op jit(solution)/shard_map/cut/pallas_call | solution.py:225
  85.8 4.1 collective-permute-start.1
  92.4 9.9 %collective-permute-done.1.refs_1_.refs_0_ = bf16[2,2,4,64,128]{4,3,2,1,0:T(8,128)(2,1)S(1)} collective-permute-done((bf16[2,2,4,64,128]{4,3,2,1,0:T(8,128)(2,1)}, bf16[2,2,4,64,128]{4,3,2,1,0:T(8,128)(2,1)S(1)}, u32[]{:S(2)}, u32[]{:S(2)}) %collective-permute-start.1) | collective-permute-done | bytes 262176 | tf_op jit(solution)/shard_map/ppermute | solution.py:307
  102.3 9.1 %collective-permute-done.14.refs_1_ = bf16[2,2,4,64,128]{4,3,2,1,0:T(8,128)(2,1)S(1)} collective-permute-done((bf16[2,2,4,64,128]{4,3,2,1,0:T(8,128)(2,1)}, bf16[2,2,4,64,128]{4,3,2,1,0:T(8,128)(2,1)S(1)}, u32[]{:S(2)}, u32[]{:S(2)}) %collective-permute-start.14) | collective-permute-done | bytes 262176 | tf_op jit(solution)/shard_map/ppermute | solution.py:307
  112.9 3.4 pack.6
  116.4 4.2 all-to-all-start.4
  120.6 25.7 %cut.6 = (bf16[2,2,4,64,128]{4,3,2,1,0:T(8,128)(2,1)}, bf16[2,2,4,64,128]{4,3,2,1,0:T(8,128)(2,1)}, bf16[2,2,4,64,128]{4,3,2,1,0:T(8,128)(2,1)}) custom-call(s32[2]{0:T(128)} %pad_add_fusion.place_ref, bf16[2,1,4,256,512]{4,3,2,1,0:T(8,128)(2,1)} %lesser_ref.15, bf16[2,1,4,256,512]{4,3,2,1,0:T(8,128)(2,1)} %greater_ref.15, ...), custom_call_target="tpu_custom_call" | custom-call | tf_op jit(solution)/shard_map/cut/pallas_call | solution.py:225
  146.2 4.5 collective-permute-start.8
  153.2 4.7 collective-permute-done.8.refs_0_
  157.9 8.3 %collective-permute-done.10.refs_2_ = bf16[2,2,4,64,128]{4,3,2,1,0:T(8,128)(2,1)S(1)} collective-permute-done((bf16[2,2,4,64,128]{4,3,2,1,0:T(8,128)(2,1)}, bf16[2,2,4,64,128]{4,3,2,1,0:T(8,128)(2,1)S(1)}, u32[]{:S(2)}, u32[]{:S(2)}) %collective-permute-start.10) | collective-permute-done | bytes 262176 | tf_op jit(solution)/shard_map/ppermute | solution.py:307
  166.2 9.8 %collective-permute-done.9.refs_1_ = bf16[2,2,4,64,128]{4,3,2,1,0:T(8,128)(2,1)S(1)} collective-permute-done((bf16[2,2,4,64,128]{4,3,2,1,0:T(8,128)(2,1)}, bf16[2,2,4,64,128]{4,3,2,1,0:T(8,128)(2,1)S(1)}, u32[]{:S(2)}, u32[]{:S(2)}) %collective-permute-start.9) | collective-permute-done | bytes 262176 | tf_op jit(solution)/shard_map/ppermute | solution.py:307
  176.8 3.4 pack.5
  180.2 3.9 all-to-all-start.2
  184.1 25.7 %cut.7 = (bf16[2,2,4,64,128]{4,3,2,1,0:T(8,128)(2,1)}, bf16[2,2,4,64,128]{4,3,2,1,0:T(8,128)(2,1)}, bf16[2,2,4,64,128]{4,3,2,1,0:T(8,128)(2,1)}) custom-call(s32[2]{0:T(128)} %pad_add_fusion.place_ref, bf16[2,1,4,256,512]{4,3,2,1,0:T(8,128)(2,1)} %lesser_ref.15, bf16[2,1,4,256,512]{4,3,2,1,0:T(8,128)(2,1)} %greater_ref.15, ...), custom_call_target="tpu_custom_call" | custom-call | tf_op jit(solution)/shard_map/cut/pallas_call | solution.py:225
  214.2 9.8 %collective-permute-done.2.refs_0_ = bf16[2,2,4,64,128]{4,3,2,1,0:T(8,128)(2,1)S(1)} collective-permute-done((bf16[2,2,4,64,128]{4,3,2,1,0:T(8,128)(2,1)}, bf16[2,2,4,64,128]{4,3,2,1,0:T(8,128)(2,1)S(1)}, u32[]{:S(2)}, u32[]{:S(2)}) %collective-permute-start.2) | collective-permute-done | bytes 262176 | tf_op jit(solution)/shard_map/ppermute | solution.py:307
  224.1 7.4 %collective-permute-done.3.refs_1_ = bf16[2,2,4,64,128]{4,3,2,1,0:T(8,128)(2,1)S(1)} collective-permute-done((bf16[2,2,4,64,128]{4,3,2,1,0:T(8,128)(2,1)}, bf16[2,2,4,64,128]{4,3,2,1,0:T(8,128)(2,1)S(1)}, u32[]{:S(2)}, u32[]{:S(2)}) %collective-permute-start.3) | collective-permute-done | bytes 262176 | tf_op jit(solution)/shard_map/ppermute | solution.py:307
  232.8 3.4 pack.4
  236.3 4.3 all-to-all-start
  241.2 3.4 build.1.matrix_ref
  244.6 3.1 mix.7
  247.7 8.3 %all-to-all-done.in_ref = bf16[8,4,128,128]{3,2,1,0:T(8,128)(2,1)S(1)} async-done(((bf16[8,4,128,128]{3,2,1,0:T(8,128)(2,1)}), bf16[8,4,128,128]{3,2,1,0:T(8,128)(2,1)S(1)}, u32[]{:S(2)}, u32[]{:S(2)}) %all-to-all-start) | async-done | bytes 1048608 | tf_op jit(solution)/shard_map/all_to_all | solution.py:302
  256.0 3.6 all-to-all-start.7
  259.5 3.1 mix.6
  262.6 12.2 %all-to-all-done.7.in_ref = bf16[8,4,128,128]{3,2,1,0:T(8,128)(2,1)S(1)} async-done(((bf16[8,4,128,128]{3,2,1,0:T(8,128)(2,1)}), bf16[8,4,128,128]{3,2,1,0:T(8,128)(2,1)S(1)}, u32[]{:S(2)}, u32[]{:S(2)}) %all-to-all-start.7) | async-done | bytes 1048608 | tf_op jit(solution)/shard_map/all_to_all | solution.py:302
  274.9 3.6 all-to-all-start.5
  278.4 3.1 mix.5
  281.5 12.2 %all-to-all-done.5.in_ref = bf16[8,4,128,128]{3,2,1,0:T(8,128)(2,1)S(1)} async-done(((bf16[8,4,128,128]{3,2,1,0:T(8,128)(2,1)}), bf16[8,4,128,128]{3,2,1,0:T(8,128)(2,1)S(1)}, u32[]{:S(2)}, u32[]{:S(2)}) %all-to-all-start.5) | async-done | bytes 1048608 | tf_op jit(solution)/shard_map/all_to_all | solution.py:302
  293.8 3.6 all-to-all-start.3
  300.4 12.3 %all-to-all-done.3.in_ref = bf16[8,4,128,128]{3,2,1,0:T(8,128)(2,1)S(1)} async-done(((bf16[8,4,128,128]{3,2,1,0:T(8,128)(2,1)}), bf16[8,4,128,128]{3,2,1,0:T(8,128)(2,1)S(1)}, u32[]{:S(2)}, u32[]{:S(2)}) %all-to-all-start.3) | async-done | bytes 1048608 | tf_op jit(solution)/shard_map/all_to_all | solution.py:302
  312.7 3.7 all-to-all-start.1
  316.4 3.4 unpack.7
  319.8 4.8 collective-permute-start.21
  327.0 3.4 unpack.6
  333.5 3.4 unpack.5
  338.7 7.4 %collective-permute-done.22.refs_2_ = bf16[2,2,4,64,128]{4,3,2,1,0:T(8,128)(2,1)S(1)} collective-permute-done((bf16[2,2,4,64,128]{4,3,2,1,0:T(8,128)(2,1)}, bf16[2,2,4,64,128]{4,3,2,1,0:T(8,128)(2,1)S(1)}, u32[]{:S(2)}, u32[]{:S(2)}) %collective-permute-start.22) | collective-permute-done | bytes 262176 | tf_op jit(solution)/shard_map/ppermute | solution.py:307
  347.2 3.4 unpack.4
  350.6 14.0 %collective-permute-start.12 = (bf16[2,2,4,64,128]{4,3,2,1,0:T(8,128)(2,1)}, bf16[2,2,4,64,128]{4,3,2,1,0:T(8,128)(2,1)S(1)}, u32[]{:S(2)}, u32[]{:S(2)}) collective-permute-start(bf16[2,2,4,64,128]{4,3,2,1,0:T(8,128)(2,1)} %get-tuple-element.50), channel_id=1, source_target_pairs={{0,8},{4,12},{8,0},{12,4},{1,9},{5,13},{9,1},{13,5},{2,10},{6,14},... | collective-permute-start | bytes 786440 | tf_op jit(solution)/shard_map/ppermute | solution.py:307
  365.9 13.9 %collective-permute-done.17.refs_2_ = bf16[2,2,4,64,128]{4,3,2,1,0:T(8,128)(2,1)S(1)} collective-permute-done((bf16[2,2,4,64,128]{4,3,2,1,0:T(8,128)(2,1)}, bf16[2,2,4,64,128]{4,3,2,1,0:T(8,128)(2,1)S(1)}, u32[]{:S(2)}, u32[]{:S(2)}) %collective-permute-start.17) | collective-permute-done | bytes 262176 | tf_op jit(solution)/shard_map/ppermute | solution.py:307
  379.9 7.1 %collective-permute-start.6 = (bf16[2,2,4,64,128]{4,3,2,1,0:T(8,128)(2,1)}, bf16[2,2,4,64,128]{4,3,2,1,0:T(8,128)(2,1)S(1)}, u32[]{:S(2)}, u32[]{:S(2)}) collective-permute-start(bf16[2,2,4,64,128]{4,3,2,1,0:T(8,128)(2,1)} %get-tuple-element.44), channel_id=1, source_target_pairs={{0,8},{4,12},{8,0},{12,4},{1,9},{5,13},{9,1},{13,5},{2,10},{6,14},... | collective-permute-start | bytes 786440 | tf_op jit(solution)/shard_map/ppermute | solution.py:307
  388.4 33.6 %join.4 = (bf16[2,1,4,256,512]{4,3,2,1,0:T(8,128)(2,1)}, bf16[2,1,4,256,512]{4,3,2,1,0:T(8,128)(2,1)}) custom-call(s32[2]{0:T(128)} %pad_add_fusion.place_ref, bf16[2,2,4,64,128]{4,3,2,1,0:T(8,128)(2,1)} %get-tuple-element.60.refs_0_, bf16[2,2,4,64,128]{4,3,2,1,0:T(8,128)(2,1)} %copy-done.20, bf16[2,2,4,64,128]{4,3,2,1,0:T(8,128)(2,1)} %copy-done.21, ...), custom_call_target="tpu_custom_call" | custom-call | tf_op jit(solution)/shard_map/join/pallas_call | solution.py:238
  422.1 33.6 %join.5 = (bf16[2,1,4,256,512]{4,3,2,1,0:T(8,128)(2,1)}, bf16[2,1,4,256,512]{4,3,2,1,0:T(8,128)(2,1)}) custom-call(s32[2]{0:T(128)} %pad_add_fusion.place_ref, bf16[2,2,4,64,128]{4,3,2,1,0:T(8,128)(2,1)} %get-tuple-element.54.refs_0_, bf16[2,2,4,64,128]{4,3,2,1,0:T(8,128)(2,1)} %copy-done.23, ...), custom_call_target="tpu_custom_call", output_to_operand_aliasing={{0}: (5, {}), {1}: (6, {})} | custom-call | tf_op jit(solution)/shard_map/join/pallas_call | solution.py:238
  456.5 33.6 %join.6 = (bf16[2,1,4,256,512]{4,3,2,1,0:T(8,128)(2,1)}, bf16[2,1,4,256,512]{4,3,2,1,0:T(8,128)(2,1)}) custom-call(s32[2]{0:T(128)} %pad_add_fusion.place_ref, bf16[2,2,4,64,128]{4,3,2,1,0:T(8,128)(2,1)} %get-tuple-element.48.refs_0_, bf16[2,2,4,64,128]{4,3,2,1,0:T(8,128)(2,1)} %copy-done.25, ...), custom_call_target="tpu_custom_call", output_to_operand_aliasing={{0}: (5, {}), {1}: (6, {})} | custom-call | tf_op jit(solution)/shard_map/join/pallas_call | solution.py:238
  491.1 33.6 %join.7 = (bf16[2,1,4,256,512]{4,3,2,1,0:T(8,128)(2,1)}, bf16[2,1,4,256,512]{4,3,2,1,0:T(8,128)(2,1)}) custom-call(s32[2]{0:T(128)} %pad_add_fusion.place_ref, bf16[2,2,4,64,128]{4,3,2,1,0:T(8,128)(2,1)} %get-tuple-element.42.refs_0_, bf16[2,2,4,64,128]{4,3,2,1,0:T(8,128)(2,1)} %copy-done.27, ...), custom_call_target="tpu_custom_call", output_to_operand_aliasing={{0}: (5, {}), {1}: (6, {})} | custom-call | tf_op jit(solution)/shard_map/join/pallas_call | solution.py:238
  (102 shorter events, 36.6 us)
Async XLA Ops:
  26.9 14.5 %collective-permute-start = (bf16[2,2,4,64,128]{4,3,2,1,0:T(8,128)(2,1)}, bf16[2,2,4,64,128]{4,3,2,1,0:T(8,128)(2,1)S(1)}, u32[]{:S(2)}, u32[]{:S(2)}) collective-permute-start(bf16[2,2,4,64,128]{4,3,2,1,0:T(8,128)(2,1)} %get-tuple-element.36.refs_0_), channel_id=1, source_target_pairs={{0,4},{4,0},{8,12},{12,8},{1,5},{5,1},{9,13},{13,9},{2,6},{6,2},{1... | collective-permute-start | bytes 786440 | tf_op jit(solution)/shard_map/ppermute | solution.py:307
  30.0 21.6 %collective-permute-start.19 = (bf16[2,2,4,64,128]{4,3,2,1,0:T(8,128)(2,1)}, bf16[2,2,4,64,128]{4,3,2,1,0:T(8,128)(2,1)S(1)}, u32[]{:S(2)}, u32[]{:S(2)}) collective-permute-start(bf16[2,2,4,64,128]{4,3,2,1,0:T(8,128)(2,1)} %get-tuple-element.58), channel_id=1, source_target_pairs={{0,8},{4,12},{8,0},{12,4},{1,9},{5,13},{9,1},{13,5},{2,10},{6,14},... | collective-permute-start | bytes 786440 | tf_op jit(solution)/shard_map/ppermute | solution.py:307
  32.6 19.0 %collective-permute-start.20 = (bf16[2,2,4,64,128]{4,3,2,1,0:T(8,128)(2,1)}, bf16[2,2,4,64,128]{4,3,2,1,0:T(8,128)(2,1)S(1)}, u32[]{:S(2)}, u32[]{:S(2)}) collective-permute-start(bf16[2,2,4,64,128]{4,3,2,1,0:T(8,128)(2,1)} %get-tuple-element.59), channel_id=1, source_target_pairs={{0,12},{4,8},{8,4},{12,0},{1,13},{5,9},{9,5},{13,1},{2,14},{6,10},... | collective-permute-start | bytes 786440 | tf_op jit(solution)/shard_map/ppermute | solution.py:307
  41.3 10.2 %copy-start.9 = (bf16[2,2,4,64,128]{4,3,2,1,0:T(8,128)(2,1)}, bf16[2,2,4,64,128]{4,3,2,1,0:T(8,128)(2,1)S(1)}, u32[]{:S(2)}) copy-start(bf16[2,2,4,64,128]{4,3,2,1,0:T(8,128)(2,1)S(1)} %collective-permute-done.refs_1_.refs_0_) | copy-start | bytes 786436
  56.4 59.9 %all-to-all-start.6 = ((bf16[8,4,128,128]{3,2,1,0:T(8,128)(2,1)}), bf16[8,4,128,128]{3,2,1,0:T(8,128)(2,1)S(1)}, u32[]{:S(2)}, u32[]{:S(2)}) async-start(bf16[8,4,128,128]{3,2,1,0:T(8,128)(2,1)} %pack.7), calls=%async_computation.6 | async-start | bytes 2097152 | tf_op jit(solution)/shard_map/all_to_all | solution.py:302
  85.8 16.5 %collective-permute-start.1 = (bf16[2,2,4,64,128]{4,3,2,1,0:T(8,128)(2,1)}, bf16[2,2,4,64,128]{4,3,2,1,0:T(8,128)(2,1)S(1)}, u32[]{:S(2)}, u32[]{:S(2)}) collective-permute-start(bf16[2,2,4,64,128]{4,3,2,1,0:T(8,128)(2,1)} %get-tuple-element.37.refs_0_), channel_id=1, source_target_pairs={{0,4},{4,0},{8,12},{12,8},{1,5},{5,1},{9,13},{13,9},{2,6},{6,2},{1... | collective-permute-start | bytes 786440 | tf_op jit(solution)/shard_map/ppermute | solution.py:307
  89.9 21.5 %collective-permute-start.14 = (bf16[2,2,4,64,128]{4,3,2,1,0:T(8,128)(2,1)}, bf16[2,2,4,64,128]{4,3,2,1,0:T(8,128)(2,1)S(1)}, u32[]{:S(2)}, u32[]{:S(2)}) collective-permute-start(bf16[2,2,4,64,128]{4,3,2,1,0:T(8,128)(2,1)} %get-tuple-element.52), channel_id=1, source_target_pairs={{0,8},{4,12},{8,0},{12,4},{1,9},{5,13},{9,1},{13,5},{2,10},{6,14},... | collective-permute-start | bytes 786440 | tf_op jit(solution)/shard_map/ppermute | solution.py:307
  91.0 20.4 %collective-permute-start.15 = (bf16[2,2,4,64,128]{4,3,2,1,0:T(8,128)(2,1)}, bf16[2,2,4,64,128]{4,3,2,1,0:T(8,128)(2,1)S(1)}, u32[]{:S(2)}, u32[]{:S(2)}) collective-permute-start(bf16[2,2,4,64,128]{4,3,2,1,0:T(8,128)(2,1)} %get-tuple-element.53), channel_id=1, source_target_pairs={{0,12},{4,8},{8,4},{12,0},{1,13},{5,9},{9,5},{13,1},{2,14},{6,10},... | collective-permute-start | bytes 786440 | tf_op jit(solution)/shard_map/ppermute | solution.py:307
  102.3 9.1 %copy-start.8 = (bf16[2,2,4,64,128]{4,3,2,1,0:T(8,128)(2,1)}, bf16[2,2,4,64,128]{4,3,2,1,0:T(8,128)(2,1)S(1)}, u32[]{:S(2)}) copy-start(bf16[2,2,4,64,128]{4,3,2,1,0:T(8,128)(2,1)S(1)} %collective-permute-done.1.refs_1_.refs_0_) | copy-start | bytes 786436
  116.3 29.9 %copy-start = (bf16[8,4,128,128]{3,2,1,0:T(8,128)(2,1)}, bf16[8,4,128,128]{3,2,1,0:T(8,128)(2,1)S(1)}, u32[]{:S(2)}) copy-start(bf16[8,4,128,128]{3,2,1,0:T(8,128)(2,1)S(1)} %all-to-all-done.6.in_ref) | copy-start | bytes 3145732
  116.4 63.8 %all-to-all-start.4 = ((bf16[8,4,128,128]{3,2,1,0:T(8,128)(2,1)}), bf16[8,4,128,128]{3,2,1,0:T(8,128)(2,1)S(1)}, u32[]{:S(2)}, u32[]{:S(2)}) async-start(bf16[8,4,128,128]{3,2,1,0:T(8,128)(2,1)} %pack.6), calls=%async_computation.4 | async-start | bytes 2097152 | tf_op jit(solution)/shard_map/all_to_all | solution.py:302
  146.2 11.7 %collective-permute-start.8 = (bf16[2,2,4,64,128]{4,3,2,1,0:T(8,128)(2,1)}, bf16[2,2,4,64,128]{4,3,2,1,0:T(8,128)(2,1)S(1)}, u32[]{:S(2)}, u32[]{:S(2)}) collective-permute-start(bf16[2,2,4,64,128]{4,3,2,1,0:T(8,128)(2,1)} %get-tuple-element.38.refs_0_), channel_id=1, source_target_pairs={{0,4},{4,0},{8,12},{12,8},{1,5},{5,1},{9,13},{13,9},{2,6},{6,2},{1... | collective-permute-start | bytes 786440 | tf_op jit(solution)/shard_map/ppermute | solution.py:307
  150.7 15.5 %collective-permute-start.10 = (bf16[2,2,4,64,128]{4,3,2,1,0:T(8,128)(2,1)}, bf16[2,2,4,64,128]{4,3,2,1,0:T(8,128)(2,1)S(1)}, u32[]{:S(2)}, u32[]{:S(2)}) collective-permute-start(bf16[2,2,4,64,128]{4,3,2,1,0:T(8,128)(2,1)} %get-tuple-element.47), channel_id=1, source_target_pairs={{0,12},{4,8},{8,4},{12,0},{1,13},{5,9},{9,5},{13,1},{2,14},{6,10},... | collective-permute-start | bytes 786440 | tf_op jit(solution)/shard_map/ppermute | solution.py:307
  153.2 22.8 %collective-permute-start.9 = (bf16[2,2,4,64,128]{4,3,2,1,0:T(8,128)(2,1)}, bf16[2,2,4,64,128]{4,3,2,1,0:T(8,128)(2,1)S(1)}, u32[]{:S(2)}, u32[]{:S(2)}) collective-permute-start(bf16[2,2,4,64,128]{4,3,2,1,0:T(8,128)(2,1)} %get-tuple-element.46), channel_id=1, source_target_pairs={{0,8},{4,12},{8,0},{12,4},{1,9},{5,13},{9,1},{13,5},{2,10},{6,14},... | collective-permute-start | bytes 786440 | tf_op jit(solution)/shard_map/ppermute | solution.py:307
  157.9 18.1 %copy-start.11 = (bf16[2,2,4,64,128]{4,3,2,1,0:T(8,128)(2,1)}, bf16[2,2,4,64,128]{4,3,2,1,0:T(8,128)(2,1)S(1)}, u32[]{:S(2)}) copy-start(bf16[2,2,4,64,128]{4,3,2,1,0:T(8,128)(2,1)S(1)} %collective-permute-done.8.refs_0_) | copy-start | bytes 786436
  166.2 9.8 %copy-start.13 = (bf16[2,2,4,64,128]{4,3,2,1,0:T(8,128)(2,1)}, bf16[2,2,4,64,128]{4,3,2,1,0:T(8,128)(2,1)S(1)}, u32[]{:S(2)}) copy-start(bf16[2,2,4,64,128]{4,3,2,1,0:T(8,128)(2,1)S(1)} %collective-permute-done.10.refs_2_) | copy-start | bytes 786436
  180.2 29.5 %copy-start.1 = (bf16[8,4,128,128]{3,2,1,0:T(8,128)(2,1)}, bf16[8,4,128,128]{3,2,1,0:T(8,128)(2,1)S(1)}, u32[]{:S(2)}) copy-start(bf16[8,4,128,128]{3,2,1,0:T(8,128)(2,1)S(1)} %all-to-all-done.4.in_ref) | copy-start | bytes 3145732
  180.2 56.1 %all-to-all-start.2 = ((bf16[8,4,128,128]{3,2,1,0:T(8,128)(2,1)}), bf16[8,4,128,128]{3,2,1,0:T(8,128)(2,1)S(1)}, u32[]{:S(2)}, u32[]{:S(2)}) async-start(bf16[8,4,128,128]{3,2,1,0:T(8,128)(2,1)} %pack.5), calls=%async_computation.2 | async-start | bytes 2097152 | tf_op jit(solution)/shard_map/all_to_all | solution.py:302
  209.7 14.3 %collective-permute-start.2 = (bf16[2,2,4,64,128]{4,3,2,1,0:T(8,128)(2,1)}, bf16[2,2,4,64,128]{4,3,2,1,0:T(8,128)(2,1)S(1)}, u32[]{:S(2)}, u32[]{:S(2)}) collective-permute-start(bf16[2,2,4,64,128]{4,3,2,1,0:T(8,128)(2,1)} %get-tuple-element.39), channel_id=1, source_target_pairs={{0,4},{4,0},{8,12},{12,8},{1,5},{5,1},{9,13},{13,9},{2,6},{6,2},{1... | collective-permute-start | bytes 786440 | tf_op jit(solution)/shard_map/ppermute | solution.py:307
  209.8 21.6 %collective-permute-start.3 = (bf16[2,2,4,64,128]{4,3,2,1,0:T(8,128)(2,1)}, bf16[2,2,4,64,128]{4,3,2,1,0:T(8,128)(2,1)S(1)}, u32[]{:S(2)}, u32[]{:S(2)}) collective-permute-start(bf16[2,2,4,64,128]{4,3,2,1,0:T(8,128)(2,1)} %get-tuple-element.40), channel_id=1, source_target_pairs={{0,8},{4,12},{8,0},{12,4},{1,9},{5,13},{9,1},{13,5},{2,10},{6,14},... | collective-permute-start | bytes 786440 | tf_op jit(solution)/shard_map/ppermute | solution.py:307
  212.9 18.6 %collective-permute-start.4 = (bf16[2,2,4,64,128]{4,3,2,1,0:T(8,128)(2,1)}, bf16[2,2,4,64,128]{4,3,2,1,0:T(8,128)(2,1)S(1)}, u32[]{:S(2)}, u32[]{:S(2)}) collective-permute-start(bf16[2,2,4,64,128]{4,3,2,1,0:T(8,128)(2,1)} %get-tuple-element.41), channel_id=1, source_target_pairs={{0,12},{4,8},{8,4},{12,0},{1,13},{5,9},{9,5},{13,1},{2,14},{6,10},... | collective-permute-start | bytes 786440 | tf_op jit(solution)/shard_map/ppermute | solution.py:307
  224.0 7.4 %copy-start.10 = (bf16[2,2,4,64,128]{4,3,2,1,0:T(8,128)(2,1)}, bf16[2,2,4,64,128]{4,3,2,1,0:T(8,128)(2,1)S(1)}, u32[]{:S(2)}) copy-start(bf16[2,2,4,64,128]{4,3,2,1,0:T(8,128)(2,1)S(1)} %collective-permute-done.2.refs_0_) | copy-start | bytes 786436
  236.3 11.4 %copy-start.2 = (bf16[8,4,128,128]{3,2,1,0:T(8,128)(2,1)}, bf16[8,4,128,128]{3,2,1,0:T(8,128)(2,1)S(1)}, u32[]{:S(2)}) copy-start(bf16[8,4,128,128]{3,2,1,0:T(8,128)(2,1)S(1)} %all-to-all-done.2.in_ref) | copy-start | bytes 3145732
  236.3 19.7 %all-to-all-start = ((bf16[8,4,128,128]{3,2,1,0:T(8,128)(2,1)}), bf16[8,4,128,128]{3,2,1,0:T(8,128)(2,1)S(1)}, u32[]{:S(2)}, u32[]{:S(2)}) async-start(bf16[8,4,128,128]{3,2,1,0:T(8,128)(2,1)} %pack.4), calls=%async_computation | async-start | bytes 2097152 | tf_op jit(solution)/shard_map/all_to_all | solution.py:302
  256.0 18.9 %all-to-all-start.7 = ((bf16[8,4,128,128]{3,2,1,0:T(8,128)(2,1)}), bf16[8,4,128,128]{3,2,1,0:T(8,128)(2,1)S(1)}, u32[]{:S(2)}, u32[]{:S(2)}) async-start(bf16[8,4,128,128]{3,2,1,0:T(8,128)(2,1)} %mix.7), calls=%async_computation.7 | async-start | bytes 2097152 | tf_op jit(solution)/shard_map/all_to_all | solution.py:302
  274.9 18.9 %all-to-all-start.5 = ((bf16[8,4,128,128]{3,2,1,0:T(8,128)(2,1)}), bf16[8,4,128,128]{3,2,1,0:T(8,128)(2,1)S(1)}, u32[]{:S(2)}, u32[]{:S(2)}) async-start(bf16[8,4,128,128]{3,2,1,0:T(8,128)(2,1)} %mix.6), calls=%async_computation.5 | async-start | bytes 2097152 | tf_op jit(solution)/shard_map/all_to_all | solution.py:302
  293.8 18.9 %all-to-all-start.3 = ((bf16[8,4,128,128]{3,2,1,0:T(8,128)(2,1)}), bf16[8,4,128,128]{3,2,1,0:T(8,128)(2,1)S(1)}, u32[]{:S(2)}, u32[]{:S(2)}) async-start(bf16[8,4,128,128]{3,2,1,0:T(8,128)(2,1)} %mix.5), calls=%async_computation.3 | async-start | bytes 2097152 | tf_op jit(solution)/shard_map/all_to_all | solution.py:302
  312.7 17.7 %copy-start.4 = (bf16[8,4,128,128]{3,2,1,0:T(8,128)(2,1)}, bf16[8,4,128,128]{3,2,1,0:T(8,128)(2,1)S(1)}, u32[]{:S(2)}) copy-start(bf16[8,4,128,128]{3,2,1,0:T(8,128)(2,1)S(1)} %all-to-all-done.3.in_ref) | copy-start | bytes 3145732
  312.7 33.5 %all-to-all-start.1 = ((bf16[8,4,128,128]{3,2,1,0:T(8,128)(2,1)}), bf16[8,4,128,128]{3,2,1,0:T(8,128)(2,1)S(1)}, u32[]{:S(2)}, u32[]{:S(2)}) async-start(bf16[8,4,128,128]{3,2,1,0:T(8,128)(2,1)} %mix.4), calls=%async_computation.1 | async-start | bytes 2097152 | tf_op jit(solution)/shard_map/all_to_all | solution.py:302
  319.8 17.1 %collective-permute-start.21 = (bf16[2,2,4,64,128]{4,3,2,1,0:T(8,128)(2,1)}, bf16[2,2,4,64,128]{4,3,2,1,0:T(8,128)(2,1)S(1)}, u32[]{:S(2)}, u32[]{:S(2)}) collective-permute-start(bf16[2,2,4,64,128]{4,3,2,1,0:T(8,128)(2,1)} %get-tuple-element.61), channel_id=1, source_target_pairs={{0,4},{4,0},{8,12},{12,8},{1,5},{5,1},{9,13},{13,9},{2,6},{6,2},{1... | collective-permute-start | bytes 786440 | tf_op jit(solution)/shard_map/ppermute | solution.py:307
  324.6 21.6 %collective-permute-start.22 = (bf16[2,2,4,64,128]{4,3,2,1,0:T(8,128)(2,1)}, bf16[2,2,4,64,128]{4,3,2,1,0:T(8,128)(2,1)S(1)}, u32[]{:S(2)}, u32[]{:S(2)}) collective-permute-start(bf16[2,2,4,64,128]{4,3,2,1,0:T(8,128)(2,1)} %get-tuple-element.62), channel_id=1, source_target_pairs={{0,8},{4,12},{8,0},{12,4},{1,9},{5,13},{9,1},{13,5},{2,10},{6,14},... | collective-permute-start | bytes 786440 | tf_op jit(solution)/shard_map/ppermute | solution.py:307
  325.6 24.9 %collective-permute-start.23 = (bf16[2,2,4,64,128]{4,3,2,1,0:T(8,128)(2,1)}, bf16[2,2,4,64,128]{4,3,2,1,0:T(8,128)(2,1)S(1)}, u32[]{:S(2)}, u32[]{:S(2)}) collective-permute-start(bf16[2,2,4,64,128]{4,3,2,1,0:T(8,128)(2,1)} %get-tuple-element.63), channel_id=1, source_target_pairs={{0,12},{4,8},{8,4},{12,0},{1,13},{5,9},{9,5},{13,1},{2,14},{6,10},... | collective-permute-start | bytes 786440 | tf_op jit(solution)/shard_map/ppermute | solution.py:307
  330.4 34.2 %collective-permute-start.16 = (bf16[2,2,4,64,128]{4,3,2,1,0:T(8,128)(2,1)}, bf16[2,2,4,64,128]{4,3,2,1,0:T(8,128)(2,1)S(1)}, u32[]{:S(2)}, u32[]{:S(2)}) collective-permute-start(bf16[2,2,4,64,128]{4,3,2,1,0:T(8,128)(2,1)} %get-tuple-element.55), channel_id=1, source_target_pairs={{0,4},{4,0},{8,12},{12,8},{1,5},{5,1},{9,13},{13,9},{2,6},{6,2},{1... | collective-permute-start | bytes 786440 | tf_op jit(solution)/shard_map/ppermute | solution.py:307
  331.5 48.3 %collective-permute-start.17 = (bf16[2,2,4,64,128]{4,3,2,1,0:T(8,128)(2,1)}, bf16[2,2,4,64,128]{4,3,2,1,0:T(8,128)(2,1)S(1)}, u32[]{:S(2)}, u32[]{:S(2)}) collective-permute-start(bf16[2,2,4,64,128]{4,3,2,1,0:T(8,128)(2,1)} %get-tuple-element.56), channel_id=1, source_target_pairs={{0,8},{4,12},{8,0},{12,4},{1,9},{5,13},{9,1},{13,5},{2,10},{6,14},... | collective-permute-start | bytes 786440 | tf_op jit(solution)/shard_map/ppermute | solution.py:307
  336.9 51.5 %copy-start.20 = (bf16[2,2,4,64,128]{4,3,2,1,0:T(8,128)(2,1)}, bf16[2,2,4,64,128]{4,3,2,1,0:T(8,128)(2,1)S(1)}, u32[]{:S(2)}) copy-start(bf16[2,2,4,64,128]{4,3,2,1,0:T(8,128)(2,1)S(1)} %collective-permute-done.21.refs_1_) | copy-start | bytes 786436
  336.9 42.9 %collective-permute-start.18 = (bf16[2,2,4,64,128]{4,3,2,1,0:T(8,128)(2,1)}, bf16[2,2,4,64,128]{4,3,2,1,0:T(8,128)(2,1)S(1)}, u32[]{:S(2)}, u32[]{:S(2)}) collective-permute-start(bf16[2,2,4,64,128]{4,3,2,1,0:T(8,128)(2,1)} %get-tuple-element.57), channel_id=1, source_target_pairs={{0,12},{4,8},{8,4},{12,0},{1,13},{5,9},{9,5},{13,1},{2,14},{6,10},... | collective-permute-start | bytes 786440 | tf_op jit(solution)/shard_map/ppermute | solution.py:307
  346.2 42.3 %copy-start.21 = (bf16[2,2,4,64,128]{4,3,2,1,0:T(8,128)(2,1)}, bf16[2,2,4,64,128]{4,3,2,1,0:T(8,128)(2,1)S(1)}, u32[]{:S(2)}) copy-start(bf16[2,2,4,64,128]{4,3,2,1,0:T(8,128)(2,1)S(1)} %collective-permute-done.22.refs_2_) | copy-start | bytes 786436
  346.2 40.9 %collective-permute-start.11 = (bf16[2,2,4,64,128]{4,3,2,1,0:T(8,128)(2,1)}, bf16[2,2,4,64,128]{4,3,2,1,0:T(8,128)(2,1)S(1)}, u32[]{:S(2)}, u32[]{:S(2)}) collective-permute-start(bf16[2,2,4,64,128]{4,3,2,1,0:T(8,128)(2,1)} %get-tuple-element.49), channel_id=1, source_target_pairs={{0,4},{4,0},{8,12},{12,8},{1,5},{5,1},{9,13},{13,9},{2,6},{6,2},{1... | collective-permute-start | bytes 786440 | tf_op jit(solution)/shard_map/ppermute | solution.py:307
  350.6 37.8 %copy-start.22 = (bf16[2,2,4,64,128]{4,3,2,1,0:T(8,128)(2,1)}, bf16[2,2,4,64,128]{4,3,2,1,0:T(8,128)(2,1)S(1)}, u32[]{:S(2)}) copy-start(bf16[2,2,4,64,128]{4,3,2,1,0:T(8,128)(2,1)S(1)} %collective-permute-done.23.refs_3_) | copy-start | bytes 786436
  350.6 105.1 %collective-permute-start.12 = (bf16[2,2,4,64,128]{4,3,2,1,0:T(8,128)(2,1)}, bf16[2,2,4,64,128]{4,3,2,1,0:T(8,128)(2,1)S(1)}, u32[]{:S(2)}, u32[]{:S(2)}) collective-permute-start(bf16[2,2,4,64,128]{4,3,2,1,0:T(8,128)(2,1)} %get-tuple-element.50), channel_id=1, source_target_pairs={{0,8},{4,12},{8,0},{12,4},{1,9},{5,13},{9,1},{13,5},{2,10},{6,14},... | collective-permute-start | bytes 786440 | tf_op jit(solution)/shard_map/ppermute | solution.py:307
  364.6 57.5 %copy-start.23 = (bf16[2,2,4,64,128]{4,3,2,1,0:T(8,128)(2,1)}, bf16[2,2,4,64,128]{4,3,2,1,0:T(8,128)(2,1)S(1)}, u32[]{:S(2)}) copy-start(bf16[2,2,4,64,128]{4,3,2,1,0:T(8,128)(2,1)S(1)} %collective-permute-done.16.refs_1_) | copy-start | bytes 786436
  364.6 91.2 %collective-permute-start.13 = (bf16[2,2,4,64,128]{4,3,2,1,0:T(8,128)(2,1)}, bf16[2,2,4,64,128]{4,3,2,1,0:T(8,128)(2,1)S(1)}, u32[]{:S(2)}, u32[]{:S(2)}) collective-permute-start(bf16[2,2,4,64,128]{4,3,2,1,0:T(8,128)(2,1)} %get-tuple-element.51), channel_id=1, source_target_pairs={{0,12},{4,8},{8,4},{12,0},{1,13},{5,9},{9,5},{13,1},{2,14},{6,10},... | collective-permute-start | bytes 786440 | tf_op jit(solution)/shard_map/ppermute | solution.py:307
  379.9 42.2 %copy-start.24 = (bf16[2,2,4,64,128]{4,3,2,1,0:T(8,128)(2,1)}, bf16[2,2,4,64,128]{4,3,2,1,0:T(8,128)(2,1)S(1)}, u32[]{:S(2)}) copy-start(bf16[2,2,4,64,128]{4,3,2,1,0:T(8,128)(2,1)S(1)} %collective-permute-done.17.refs_2_) | copy-start | bytes 786436
  379.9 110.3 %collective-permute-start.5 = (bf16[2,2,4,64,128]{4,3,2,1,0:T(8,128)(2,1)}, bf16[2,2,4,64,128]{4,3,2,1,0:T(8,128)(2,1)S(1)}, u32[]{:S(2)}, u32[]{:S(2)}) collective-permute-start(bf16[2,2,4,64,128]{4,3,2,1,0:T(8,128)(2,1)} %get-tuple-element.43), channel_id=1, source_target_pairs={{0,4},{4,0},{8,12},{12,8},{1,5},{5,1},{9,13},{13,9},{2,6},{6,2},{1... | collective-permute-start | bytes 786440 | tf_op jit(solution)/shard_map/ppermute | solution.py:307
  379.9 42.2 %copy-start.26 = (bf16[2,2,4,64,128]{4,3,2,1,0:T(8,128)(2,1)}, bf16[2,2,4,64,128]{4,3,2,1,0:T(8,128)(2,1)S(1)}, u32[]{:S(2)}) copy-start(bf16[2,2,4,64,128]{4,3,2,1,0:T(8,128)(2,1)S(1)} %collective-permute-done.18.refs_3_) | copy-start | bytes 786436
  379.9 110.3 %collective-permute-start.6 = (bf16[2,2,4,64,128]{4,3,2,1,0:T(8,128)(2,1)}, bf16[2,2,4,64,128]{4,3,2,1,0:T(8,128)(2,1)S(1)}, u32[]{:S(2)}, u32[]{:S(2)}) collective-permute-start(bf16[2,2,4,64,128]{4,3,2,1,0:T(8,128)(2,1)} %get-tuple-element.44), channel_id=1, source_target_pairs={{0,8},{4,12},{8,0},{12,4},{1,9},{5,13},{9,1},{13,5},{2,10},{6,14},... | collective-permute-start | bytes 786440 | tf_op jit(solution)/shard_map/ppermute | solution.py:307
  387.0 68.7 %copy-start.25 = (bf16[2,2,4,64,128]{4,3,2,1,0:T(8,128)(2,1)}, bf16[2,2,4,64,128]{4,3,2,1,0:T(8,128)(2,1)S(1)}, u32[]{:S(2)}) copy-start(bf16[2,2,4,64,128]{4,3,2,1,0:T(8,128)(2,1)S(1)} %collective-permute-done.11.refs_1_) | copy-start | bytes 786436
  387.0 103.2 %collective-permute-start.7 = (bf16[2,2,4,64,128]{4,3,2,1,0:T(8,128)(2,1)}, bf16[2,2,4,64,128]{4,3,2,1,0:T(8,128)(2,1)S(1)}, u32[]{:S(2)}, u32[]{:S(2)}) collective-permute-start(bf16[2,2,4,64,128]{4,3,2,1,0:T(8,128)(2,1)} %get-tuple-element.45), channel_id=1, source_target_pairs={{0,12},{4,8},{8,4},{12,0},{1,13},{5,9},{9,5},{13,1},{2,14},{6,10},... | collective-permute-start | bytes 786440 | tf_op jit(solution)/shard_map/ppermute | solution.py:307
  (16 other events, 29.9 us)

commit v6 on v3

--- a/solution.py
+++ b/solution.py
@@ -11,7 +11,8 @@
 
 SMAX = 2
 TILE = 16
-VMEM_BYTES = 48 * 1024 * 1024
+VMEM_BYTES = 40 * 1024 * 1024
+VMEM_WHOLE = 60 * 1024 * 1024
 APART = 1 << 16
 AXES = ("grp", "mom")
 
@@ -26,64 +27,67 @@
     return matrix
 
 
-def place_of(place_ref, pieces, far):
-    place = place_ref[0]
-    half = pieces // 2
-    block = lax.rem(place, jnp.int32(pieces))
-    low = lax.rem(block, jnp.int32(half))
-    high = lax.div(block, jnp.int32(half))
-    return lax.div(place, jnp.int32(pieces)), low, (1 - high if far else high) * half
-
-
-def pack_kernel(pieces, far, place_ref, perm_ref, lesser_ref, greater_ref, *refs):
-    half = pieces // 2
-    outs, held, arrived = refs[: 2 * half], refs[-2], refs[-1]
+def pack_kernel(pieces, order, place_ref, perm_ref, lesser_ref, greater_ref, *refs):
+    outs, (held, packed, arrived, sent) = refs[:-4], refs[-4:]
     rows = held.shape[4]
     size, width = outs[0].shape
-    side, low, base = place_of(place_ref, pieces, far)
-    copies = []
-    for step in range(half):
-        start = pl.multiple_of((base + (low ^ step)) * rows, rows)
+    side, block = lax.div(place_ref[0], jnp.int32(pieces)), lax.rem(place_ref[0], jnp.int32(pieces))
+    come = {}
+    for step in order:
+        start = pl.multiple_of((block ^ step) * rows, rows)
         for which, ref in enumerate((lesser_ref, greater_ref)):
-            copy = pltpu.make_async_copy(
+            come[step, which] = pltpu.make_async_copy(
                 ref.at[:, 0, :, pl.ds(start, rows), :],
                 held.at[step, which],
                 arrived.at[step, which],
             )
-            copy.start()
-            copies.append(copy)
-    for step in range(half):
+            come[step, which].start()
+    gone = []
+    for step in order:
         moved = []
         for which in range(2):
-            copies[2 * step + which].wait()
-            block = held[step, which].reshape(size, width)
-            moved.append(jnp.dot(perm_ref[...], block, preferred_element_type=jnp.float32))
-        outs[step][...] = jnp.where(side == 0, moved[0], moved[1]).astype(outs[0].dtype)
-        outs[half + step][...] = jnp.where(side == 0, moved[1], moved[0]).astype(outs[0].dtype)
-
-
-def unpack_kernel(pieces, far, place_ref, perm_ref, *refs):
-    half = pieces // 2
-    ins, held, sent = refs[: 2 * half], refs[-2], refs[-1]
-    outs = refs[-4:-2]
+            come[step, which].wait()
+            moved.append(
+                jnp.dot(
+                    perm_ref[...],
+                    held[step, which].reshape(size, width),
+                    preferred_element_type=jnp.float32,
+                )
+            )
+        packed[step, 0] = jnp.where(side == 0, moved[0], moved[1]).astype(packed.dtype)
+        packed[step, 1] = jnp.where(side == 0, moved[1], moved[0]).astype(packed.dtype)
+        for turn in range(2):
+            gone.append(
+                pltpu.make_async_copy(
+                    packed.at[step, turn], outs[turn * pieces + step], sent.at[step, turn]
+                )
+            )
+            gone[-1].start()
+    for copy in gone:
+        copy.wait()
+
+
+def unpack_kernel(pieces, order, place_ref, perm_ref, *refs):
+    ins, (lesser_ref, greater_ref, held, sent) = refs[:-4], refs[-4:]
     rows = held.shape[4]
-    side, low, base = place_of(place_ref, pieces, far)
-    copies = []
-    for step in range(half):
-        own = jnp.dot(perm_ref[...], ins[step][...], preferred_element_type=jnp.float32)
-        other = jnp.dot(perm_ref[...], ins[half + step][...], preferred_element_type=jnp.float32)
-        start = pl.multiple_of((base + (low ^ step)) * rows, rows)
-        for which, ref in enumerate(outs):
+    side, block = lax.div(place_ref[0], jnp.int32(pieces)), lax.rem(place_ref[0], jnp.int32(pieces))
+    gone = []
+    for at, step in enumerate(order):
+        own = jnp.dot(perm_ref[...], ins[2 * at][...], preferred_element_type=jnp.float32)
+        other = jnp.dot(perm_ref[...], ins[2 * at + 1][...], preferred_element_type=jnp.float32)
+        start = pl.multiple_of((block ^ step) * rows, rows)
+        for which, ref in enumerate((lesser_ref, greater_ref)):
             moved = jnp.where(side == which, own, other).astype(held.dtype)
             held[step, which] = moved.reshape(held.shape[2:])
-            copy = pltpu.make_async_copy(
-                held.at[step, which],
-                ref.at[:, 0, :, pl.ds(start, rows), :],
-                sent.at[step, which],
+            gone.append(
+                pltpu.make_async_copy(
+                    held.at[step, which],
+                    ref.at[:, 0, :, pl.ds(start, rows), :],
+                    sent.at[step, which],
+                )
             )
-            copy.start()
-            copies.append(copy)
-    for copy in copies:
+            gone[-1].start()
+    for copy in gone:
         copy.wait()
 
 
@@ -100,7 +104,7 @@
 
 def build_kernel(
     shares, momenta, energies, pieces,
-    place_ref, region_ref, shift_ref, occupation_ref, coupling_ref, down_ref, across_ref, *out_refs
+    place_ref, region_ref, shift_ref, occupation_ref, coupling_ref, down_ref, across_ref, out_ref
 ):
     points = shares * momenta
     modes = coupling_ref.shape[1]
@@ -123,12 +127,12 @@
     for step in range(-SMAX, SMAX + 1):
         if step == 0:
             continue
-        row = jnp.zeros((1, 2 * points), jnp.float32)
+        row = jnp.zeros((1, points), jnp.float32)
         for mode in range(modes):
             filling = occupation_ref[mode] + (greater if step > 0 else 1.0 - greater)
             weight = jnp.where(shift_ref[mode] == abs(step), filling, 0.0)
             row = row + weight * chosen[mode : mode + 1, :]
-        wide = jnp.broadcast_to(row, (points, 2 * points))
+        wide = jnp.broadcast_to(jnp.concatenate([row, row], axis=1), (points, 2 * points))
         turned = pltpu.roll(wide, 0, 1, stride=1, stride_axis=0)[:, :points]
         half = jnp.dot(
             pick, turned.astype(jnp.bfloat16), preferred_element_type=jnp.float32
@@ -137,18 +141,16 @@
             pick, half, (((1,), (1,)), ((), ())), preferred_element_type=jnp.float32
         )
         total = jnp.where(apart == step, full, total)
-    first = out_refs[0].shape[0]
-    out_refs[0][...] = total[:first].astype(out_refs[0].dtype)
-    out_refs[1][...] = total[first:].astype(out_refs[1].dtype)
-
-
-def params():
-    return pltpu.CompilerParams(vmem_limit_bytes=VMEM_BYTES)
+    out_ref[...] = total.astype(out_ref.dtype)
+
+
+def params(size=VMEM_BYTES):
+    return pltpu.CompilerParams(vmem_limit_bytes=size)
 
 
 SCALARS = pl.BlockSpec(memory_space=pltpu.SMEM)
 VECTORS = pl.BlockSpec(memory_space=pltpu.VMEM)
-WHERE_IT_LIES = pl.BlockSpec(memory_space=pl.ANY)
+ANYWHERE = pl.BlockSpec(memory_space=pl.ANY)
 
 
 def build(place, coupling, occupation, shift, region_map, slots, shares, energies, momenta, pieces):
@@ -159,12 +161,11 @@
     static = [slot.ravel(), (row * APART + energy).ravel(), momentum.ravel()]
     down = np.stack(static, axis=1).astype(np.int32)
     size = down.shape[0]
-    part = jax.ShapeDtypeStruct((size // 2, size), jnp.bfloat16)
     return pl.pallas_call(
         functools.partial(build_kernel, shares, momenta, energies, pieces),
-        out_shape=(part, part),
+        out_shape=jax.ShapeDtypeStruct((size, size), jnp.bfloat16),
         in_specs=[SCALARS] * 4 + [VECTORS] * 3,
-        out_specs=(VECTORS, VECTORS),
+        out_specs=VECTORS,
         compiler_params=params(),
         name="build",
     )(
@@ -172,60 +173,58 @@
         region_map,
         shift,
         occupation,
-        jnp.concatenate([coupling, coupling], axis=2),
+        coupling,
         jnp.asarray(down),
         jnp.asarray(down.T),
     )
 
 
-def pack(place, lesser, greater, pieces, rows, far):
+def pack(place, lesser, greater, pieces, rows, order):
     energies, _, momenta, _, columns = lesser.shape
     size = energies * momenta * rows
-    half = pieces // 2
     perm = jnp.asarray(permutation(energies, momenta, rows), jnp.bfloat16)
     piece = jax.ShapeDtypeStruct((size, columns), lesser.dtype)
     return pl.pallas_call(
-        functools.partial(pack_kernel, pieces, far),
-        out_shape=(piece,) * (2 * half),
-        in_specs=[SCALARS, VECTORS, WHERE_IT_LIES, WHERE_IT_LIES],
-        out_specs=(VECTORS,) * (2 * half),
+        functools.partial(pack_kernel, pieces, order),
+        out_shape=(piece,) * (2 * pieces),
+        in_specs=[SCALARS, VECTORS, ANYWHERE, ANYWHERE],
+        out_specs=(ANYWHERE,) * (2 * pieces),
         scratch_shapes=[
-            pltpu.VMEM((half, 2, energies, momenta, rows, columns), lesser.dtype),
-            pltpu.SemaphoreType.DMA((half, 2)),
+            pltpu.VMEM((pieces, 2, energies, momenta, rows, columns), lesser.dtype),
+            pltpu.VMEM((pieces, 2, size, columns), lesser.dtype),
+            pltpu.SemaphoreType.DMA((pieces, 2)),
+            pltpu.SemaphoreType.DMA((pieces, 2)),
         ],
-        compiler_params=params(),
+        compiler_params=params(VMEM_WHOLE),
         name="pack",
     )(place, perm, lesser, greater)
 
 
-def unpack(place, parts, filled, shape, pieces, rows, far):
+def unpack(place, parts, shape, pieces, rows, order):
     energies, _, momenta, _, columns = shape
-    half = pieces // 2
     perm = jnp.asarray(permutation(energies, momenta, rows).T, jnp.bfloat16)
     out = jax.ShapeDtypeStruct(shape, parts[0].dtype)
     return pl.pallas_call(
-        functools.partial(unpack_kernel, pieces, far),
+        functools.partial(unpack_kernel, pieces, order),
         out_shape=(out, out),
-        in_specs=[SCALARS, VECTORS] + [VECTORS] * len(parts) + [WHERE_IT_LIES] * len(filled),
-        out_specs=(WHERE_IT_LIES, WHERE_IT_LIES),
+        in_specs=[SCALARS, VECTORS] + [VECTORS] * len(parts),
+        out_specs=(ANYWHERE, ANYWHERE),
         scratch_shapes=[
-            pltpu.VMEM((half, 2, energies, momenta, rows, columns), parts[0].dtype),
-            pltpu.SemaphoreType.DMA((half, 2)),
+            pltpu.VMEM((pieces, 2, energies, momenta, rows, columns), parts[0].dtype),
+            pltpu.SemaphoreType.DMA((pieces, 2)),
         ],
-        input_output_aliases={2 + len(parts) + side: side for side in range(len(filled))},
         compiler_params=params(),
         name="unpack",
-    )(place, perm, *parts, *filled)
+    )(place, perm, *parts)
 
 
 def mix(matrix, parts):
     piece = jax.ShapeDtypeStruct(parts[0].shape, parts[0].dtype)
-    count = matrix.shape[0] // TILE
     return pl.pallas_call(
         functools.partial(mix_kernel, len(parts)),
-        out_shape=(piece,) * count,
+        out_shape=(piece,) * len(parts),
         in_specs=[VECTORS] * (1 + len(parts)),
-        out_specs=(VECTORS,) * count,
+        out_specs=(VECTORS,) * len(parts),
         compiler_params=params(),
         name="mix",
     )(matrix, *parts)
@@ -246,19 +245,16 @@
     pieces = devices // 2
     half = pieces // 2
     rows = height // pieces
-    far = [side * pieces + half + step for side in range(2) for step in range(half)]
-    near = [side * pieces + step for side in range(2) for step in range(half)]
+    order = [step + far for step in range(half) for far in (half, 0)]
+    slots = [step + side for step in order for side in (0, pieces)]
     place = (lax.axis_index("grp") * shares + lax.axis_index("mom")).astype(jnp.int32).reshape(1)
-    far_in = exchange(pack(place, lesser, greater, pieces, rows, True), far, devices)
-    near_in = exchange(pack(place, lesser, greater, pieces, rows, False), near, devices)
-    far_matrix, near_matrix = build(
-        place, coupling, occupation, shift, region_map, far + near, shares, energies, momenta, pieces
-    )
-    received = far_in + near_in
-    far_out = exchange(mix(far_matrix, received), far, devices)
-    near_out = exchange(mix(near_matrix, received), near, devices)
-    filled = unpack(place, far_out, (), lesser.shape, pieces, rows, True)
-    return unpack(place, near_out, filled, lesser.shape, pieces, rows, False)
+    sent = pack(place, lesser, greater, pieces, rows, order)
+    received = exchange([sent[slot] for slot in slots], slots, devices)
+    matrix = build(
+        place, coupling, occupation, shift, region_map, slots, shares, energies, momenta, pieces
+    )
+    returned = exchange(mix(matrix, received), slots, devices)
+    return unpack(place, returned, lesser.shape, pieces, rows, order)
 
 
 def with_halo(shard, sides, width):

time: 269 us -> 224 us (0.83)
  starting transfers between devices: 158 us -> 110 us
  waiting for transfers between devices: 87.7 us -> 94.6 us
    ppermute x62, starting transfers between devices: 158 us -> 110 us  [exchange(): lax.ppermute(part, AXES, [(device, device ^ slot) for device in range(dev...]
    ppermute x62, waiting for transfers between devices: 87.7 us -> 94.6 us  [exchange(): lax.ppermute(part, AXES, [(device, device ^ slot) for device in range(dev...]
    pallas_call x4 -> x2, Pallas kernels: 10.7 us -> 11.1 us  [the longest x1 8.59 us: pack(): pl.pallas_call(functools.partial(pack_kernel, pieces, order), out_shape=(...]
  transfers between devices with their start and end apart: 62 -> 62, of which waited for: 18 -> 35; matrix products, arithmetic and copies ran while one was open for 0% -> 0% of each run, Pallas kernels for 4% -> 1%
where the time goes in v6:
time: 224 us; the launch traced here: 223 us
  starting transfers between devices  110 us (49%)
  waiting for transfers between devices  94.6 us (42%)
  Pallas kernels  15.6 us (7%)
    ppermute x62, starting transfers between devices, exchange(): lax.ppermute(part, AXES, [(device, device ^ slot) for device in range(dev...  110 us
    ppermute x62, waiting for transfers between devices, exchange(): lax.ppermute(part, AXES, [(device, device ^ slot) for device in range(dev...  94.6 us
    pallas_call x1, Pallas kernels, pack(): pl.pallas_call(functools.partial(pack_kernel, pieces, order), out_shape=(...  8.59 us
  transfers between devices with their start and end apart: 62, of which 35 were waited for; matrix products, arithmetic and copies ran while one was open for 0% of the time, Pallas kernels for 1%

profile of v6, /device:TPU:0, one launch (start us, length us, event | category | flops | bytes accessed | tf_op | source)
XLA Modules:
  0.0 222.9 jit_solution(68470024468517126)
XLA Ops:
  0.7 8.6 %pack.1 = (bf16[128,512]{1,0:T(8,128)(2,1)}, bf16[128,512]{1,0:T(8,128)(2,1)}, bf16[128,512]{1,0:T(8,128)(2,1)}, bf16[128,512]{1,0:T(8,128)(2,1)}, bf16[128,512]...) custom-call(s32[1]{0:T(128)} %bitcast.place_ref, ...), custom_call_target="tpu_custom_call" | custom-call | tf_op jit(solution)/shard_map/pack/pallas_call | solution.py:187
  9.3 4.1 %collective-permute-start = (bf16[128,512]{1,0:T(8,128)(2,1)}, bf16[128,512]{1,0:T(8,128)(2,1)S(1)}, u32[]{:S(2)}, u32[]{:S(2)}) collective-permute-start(bf16[128,512]{1,0:T(8,128)(2,1)} %get-tuple-element.66), channel_id=1, source_target_pairs={{0,8},{1,9},{2,10},{3,11},{4,12},{5,13},{6,14},{7,15},{8,0},{9,1},... | collective-permute-start | bytes 393224 | tf_op jit(solution)/shard_map/ppermute | solution.py:237
  16.4 2.4 %collective-permute-start.4 = (bf16[128,512]{1,0:T(8,128)(2,1)}, bf16[128,512]{1,0:T(8,128)(2,1)S(1)}, u32[]{:S(2)}, u32[]{:S(2)}) collective-permute-start(bf16[128,512]{1,0:T(8,128)(2,1)} %get-tuple-element.71), channel_id=1, source_target_pairs={{0,25},{1,24},{2,27},{3,26},{4,29},{5,28},{6,31},{7,30},{8,17},{9,... | collective-permute-start | bytes 393224 | tf_op jit(solution)/shard_map/ppermute | solution.py:237
  18.8 10.4 %collective-permute-done.refs_0_ = bf16[128,512]{1,0:T(8,128)(2,1)S(1)} collective-permute-done((bf16[128,512]{1,0:T(8,128)(2,1)}, bf16[128,512]{1,0:T(8,128)(2,1)S(1)}, u32[]{:S(2)}, u32[]{:S(2)}) %collective-permute-start) | collective-permute-done | bytes 131104 | tf_op jit(solution)/shard_map/ppermute | solution.py:237
  29.2 4.1 %collective-permute-done.1.refs_1_ = bf16[128,512]{1,0:T(8,128)(2,1)S(1)} collective-permute-done((bf16[128,512]{1,0:T(8,128)(2,1)}, bf16[128,512]{1,0:T(8,128)(2,1)S(1)}, u32[]{:S(2)}, u32[]{:S(2)}) %collective-permute-start.1) | collective-permute-done | bytes 131104 | tf_op jit(solution)/shard_map/ppermute | solution.py:237
  33.3 3.4 %collective-permute-start.8 = (bf16[128,512]{1,0:T(8,128)(2,1)}, bf16[128,512]{1,0:T(8,128)(2,1)S(1)}, u32[]{:S(2)}, u32[]{:S(2)}) collective-permute-start(bf16[128,512]{1,0:T(8,128)(2,1)} %get-tuple-element.75), channel_id=1, source_target_pairs={{0,26},{1,27},{2,24},{3,25},{4,30},{5,31},{6,28},{7,29},{8,18},{9,... | collective-permute-start | bytes 393224 | tf_op jit(solution)/shard_map/ppermute | solution.py:237
  40.6 6.4 %collective-permute-done.7.refs_8_ = bf16[128,512]{1,0:T(8,128)(2,1)S(1)} collective-permute-done((bf16[128,512]{1,0:T(8,128)(2,1)}, bf16[128,512]{1,0:T(8,128)(2,1)S(1)}, u32[]{:S(2)}, u32[]{:S(2)}) %collective-permute-start.7) | collective-permute-done | bytes 131104 | tf_op jit(solution)/shard_map/ppermute | solution.py:237
  47.2 2.0 collective-permute-done.8.refs_9_
  52.4 3.8 %collective-permute-done.10.refs_11_ = bf16[128,512]{1,0:T(8,128)(2,1)S(1)} collective-permute-done((bf16[128,512]{1,0:T(8,128)(2,1)}, bf16[128,512]{1,0:T(8,128)(2,1)S(1)}, u32[]{:S(2)}, u32[]{:S(2)}) %collective-permute-start.10) | collective-permute-done | bytes 131104 | tf_op jit(solution)/shard_map/ppermute | solution.py:237
  56.2 11.7 %collective-permute-start.15 = (bf16[128,512]{1,0:T(8,128)(2,1)}, bf16[128,512]{1,0:T(8,128)(2,1)S(1)}, u32[]{:S(2)}, u32[]{:S(2)}) collective-permute-start(bf16[128,512]{1,0:T(8,128)(2,1)} %get-tuple-element.82), channel_id=1, source_target_pairs={{0,12},{1,13},{2,14},{3,15},{4,8},{5,9},{6,10},{7,11},{8,4},{9,5},... | collective-permute-start | bytes 393224 | tf_op jit(solution)/shard_map/ppermute | solution.py:237
  68.4 2.5 %collective-permute-start.18 = (bf16[128,512]{1,0:T(8,128)(2,1)}, bf16[128,512]{1,0:T(8,128)(2,1)S(1)}, u32[]{:S(2)}, u32[]{:S(2)}) collective-permute-start(bf16[128,512]{1,0:T(8,128)(2,1)} %get-tuple-element.85), channel_id=1, source_target_pairs={{0,20},{1,21},{2,22},{3,23},{4,16},{5,17},{6,18},{7,19},{8,28},{9,... | collective-permute-start | bytes 393224 | tf_op jit(solution)/shard_map/ppermute | solution.py:237
  72.5 2.3 %collective-permute-start.20 = (bf16[128,512]{1,0:T(8,128)(2,1)}, bf16[128,512]{1,0:T(8,128)(2,1)S(1)}, u32[]{:S(2)}, u32[]{:S(2)}) collective-permute-start(bf16[128,512]{1,0:T(8,128)(2,1)} %get-tuple-element.87), channel_id=1, source_target_pairs={{0,29},{1,28},{2,31},{3,30},{4,25},{5,24},{6,27},{7,26},{8,21},{9,... | collective-permute-start | bytes 393224 | tf_op jit(solution)/shard_map/ppermute | solution.py:237
  74.8 2.5 %collective-permute-done.16.refs_17_ = bf16[128,512]{1,0:T(8,128)(2,1)S(1)} collective-permute-done((bf16[128,512]{1,0:T(8,128)(2,1)}, bf16[128,512]{1,0:T(8,128)(2,1)S(1)}, u32[]{:S(2)}, u32[]{:S(2)}) %collective-permute-start.16) | collective-permute-done | bytes 131104 | tf_op jit(solution)/shard_map/ppermute | solution.py:237
  79.4 2.3 %collective-permute-done.18.refs_19_ = bf16[128,512]{1,0:T(8,128)(2,1)S(1)} collective-permute-done((bf16[128,512]{1,0:T(8,128)(2,1)}, bf16[128,512]{1,0:T(8,128)(2,1)S(1)}, u32[]{:S(2)}, u32[]{:S(2)}) %collective-permute-start.18) | collective-permute-done | bytes 131104 | tf_op jit(solution)/shard_map/ppermute | solution.py:237
  81.7 6.5 %collective-permute-start.23 = (bf16[128,512]{1,0:T(8,128)(2,1)}, bf16[128,512]{1,0:T(8,128)(2,1)S(1)}, u32[]{:S(2)}, u32[]{:S(2)}) collective-permute-start(bf16[128,512]{1,0:T(8,128)(2,1)} %get-tuple-element.90), channel_id=1, source_target_pairs={{0,14},{1,15},{2,12},{3,13},{4,10},{5,11},{6,8},{7,9},{8,6},{9,7},... | collective-permute-start | bytes 393224 | tf_op jit(solution)/shard_map/ppermute | solution.py:237
  89.1 2.9 %collective-permute-start.26 = (bf16[128,512]{1,0:T(8,128)(2,1)}, bf16[128,512]{1,0:T(8,128)(2,1)S(1)}, u32[]{:S(2)}, u32[]{:S(2)}) collective-permute-start(bf16[128,512]{1,0:T(8,128)(2,1)} %get-tuple-element.93), channel_id=1, source_target_pairs={{0,22},{1,23},{2,20},{3,21},{4,18},{5,19},{6,16},{7,17},{8,30},{9,... | collective-permute-start | bytes 393224 | tf_op jit(solution)/shard_map/ppermute | solution.py:237
  92.2 6.9 %collective-permute-start.27 = (bf16[128,512]{1,0:T(8,128)(2,1)}, bf16[128,512]{1,0:T(8,128)(2,1)S(1)}, u32[]{:S(2)}, u32[]{:S(2)}) collective-permute-start(bf16[128,512]{1,0:T(8,128)(2,1)} %get-tuple-element.94), channel_id=1, source_target_pairs={{0,15},{1,14},{2,13},{3,12},{4,11},{5,10},{6,9},{7,8},{8,7},{9,6},... | collective-permute-start | bytes 393224 | tf_op jit(solution)/shard_map/ppermute | solution.py:237
  101.2 2.5 %collective-permute-start.30 = (bf16[128,512]{1,0:T(8,128)(2,1)}, bf16[128,512]{1,0:T(8,128)(2,1)S(1)}, u32[]{:S(2)}, u32[]{:S(2)}) collective-permute-start(bf16[128,512]{1,0:T(8,128)(2,1)} %get-tuple-element.97), channel_id=1, source_target_pairs={{0,23},{1,22},{2,21},{3,20},{4,19},{5,18},{6,17},{7,16},{8,31},{9,... | collective-permute-start | bytes 393224 | tf_op jit(solution)/shard_map/ppermute | solution.py:237
  104.4 2.2 build.1.matrix_ref
  106.8 2.8 %collective-permute-done.28.refs_29_ = bf16[128,512]{1,0:T(8,128)(2,1)S(1)} collective-permute-done((bf16[128,512]{1,0:T(8,128)(2,1)}, bf16[128,512]{1,0:T(8,128)(2,1)S(1)}, u32[]{:S(2)}, u32[]{:S(2)}) %collective-permute-start.28) | collective-permute-done | bytes 131104 | tf_op jit(solution)/shard_map/ppermute | solution.py:237
  109.6 2.3 %collective-permute-done.29.refs_30_ = bf16[128,512]{1,0:T(8,128)(2,1)S(1)} collective-permute-done((bf16[128,512]{1,0:T(8,128)(2,1)}, bf16[128,512]{1,0:T(8,128)(2,1)S(1)}, u32[]{:S(2)}, u32[]{:S(2)}) %collective-permute-start.29) | collective-permute-done | bytes 131104 | tf_op jit(solution)/shard_map/ppermute | solution.py:237
  111.9 3.1 %collective-permute-done.30.refs_31_ = bf16[128,512]{1,0:T(8,128)(2,1)S(1)} collective-permute-done((bf16[128,512]{1,0:T(8,128)(2,1)}, bf16[128,512]{1,0:T(8,128)(2,1)S(1)}, u32[]{:S(2)}, u32[]{:S(2)}) %collective-permute-start.30) | collective-permute-done | bytes 131104 | tf_op jit(solution)/shard_map/ppermute | solution.py:237
  115.9 2.3 %mix.1 = (bf16[128,512]{1,0:T(8,128)(2,1)S(1)}, bf16[128,512]{1,0:T(8,128)(2,1)S(1)}, bf16[128,512]{1,0:T(8,128)(2,1)S(1)}, bf16[128,512]{1,0:T(8,128)(2,1)S(1)}...) custom-call(bf16[512,512]{1,0:T(8,128)(2,1)S(1)} %build.1.matrix_ref, ...), custom_call_target="tpu_custom_call" | custom-call | tf_op jit(solution)/shard_map/mix/pallas_call | solution.py:223
  118.8 2.4 %collective-permute-start.32 = (bf16[128,512]{1,0:T(8,128)(2,1)S(1)}, bf16[128,512]{1,0:T(8,128)(2,1)S(1)}, u32[]{:S(2)}, u32[]{:S(2)}) collective-permute-start(bf16[128,512]{1,0:T(8,128)(2,1)S(1)} %get-tuple-element.99), channel_id=1, source_target_pairs={{0,24},{1,25},{2,26},{3,27},{4,28},{5,29},{6,30},{7,31},{8,16},{9,... | collective-permute-start | bytes 393224 | tf_op jit(solution)/shard_map/ppermute | solution.py:237
  122.7 2.6 %collective-permute-start.35 = (bf16[128,512]{1,0:T(8,128)(2,1)S(1)}, bf16[128,512]{1,0:T(8,128)(2,1)S(1)}, u32[]{:S(2)}, u32[]{:S(2)}) collective-permute-start(bf16[128,512]{1,0:T(8,128)(2,1)S(1)} %get-tuple-element.103), channel_id=1, source_target_pairs={{0,25},{1,24},{2,27},{3,26},{4,29},{5,28},{6,31},{7,30},{8,17},{9,... | collective-permute-start | bytes 393224 | tf_op jit(solution)/shard_map/ppermute | solution.py:237
  125.3 10.9 %collective-permute-done.31.refs_0_ = bf16[128,512]{1,0:T(8,128)(2,1)S(1)} collective-permute-done((bf16[128,512]{1,0:T(8,128)(2,1)S(1)}, bf16[128,512]{1,0:T(8,128)(2,1)S(1)}, u32[]{:S(2)}, u32[]{:S(2)}) %collective-permute-start.31) | collective-permute-done | bytes 131104 | tf_op jit(solution)/shard_map/ppermute | solution.py:237
  136.3 2.5 %collective-permute-done.32.refs_1_ = bf16[128,512]{1,0:T(8,128)(2,1)S(1)} collective-permute-done((bf16[128,512]{1,0:T(8,128)(2,1)S(1)}, bf16[128,512]{1,0:T(8,128)(2,1)S(1)}, u32[]{:S(2)}, u32[]{:S(2)}) %collective-permute-start.32) | collective-permute-done | bytes 131104 | tf_op jit(solution)/shard_map/ppermute | solution.py:237
  141.2 2.6 %collective-permute-start.39 = (bf16[128,512]{1,0:T(8,128)(2,1)S(1)}, bf16[128,512]{1,0:T(8,128)(2,1)S(1)}, u32[]{:S(2)}, u32[]{:S(2)}) collective-permute-start(bf16[128,512]{1,0:T(8,128)(2,1)S(1)} %get-tuple-element.107), channel_id=1, source_target_pairs={{0,26},{1,27},{2,24},{3,25},{4,30},{5,31},{6,28},{7,29},{8,18},{9,... | collective-permute-start | bytes 393224 | tf_op jit(solution)/shard_map/ppermute | solution.py:237
  143.8 6.1 %collective-permute-done.35.refs_5_ = bf16[128,512]{1,0:T(8,128)(2,1)S(1)} collective-permute-done((bf16[128,512]{1,0:T(8,128)(2,1)S(1)}, bf16[128,512]{1,0:T(8,128)(2,1)S(1)}, u32[]{:S(2)}, u32[]{:S(2)}) %collective-permute-start.35) | collective-permute-done | bytes 131104 | tf_op jit(solution)/shard_map/ppermute | solution.py:237
  150.0 3.0 %collective-permute-done.38.refs_8_ = bf16[128,512]{1,0:T(8,128)(2,1)S(1)} collective-permute-done((bf16[128,512]{1,0:T(8,128)(2,1)S(1)}, bf16[128,512]{1,0:T(8,128)(2,1)S(1)}, u32[]{:S(2)}, u32[]{:S(2)}) %collective-permute-start.38) | collective-permute-done | bytes 131104 | tf_op jit(solution)/shard_map/ppermute | solution.py:237
  153.0 3.4 %collective-permute-start.43 = (bf16[128,512]{1,0:T(8,128)(2,1)S(1)}, bf16[128,512]{1,0:T(8,128)(2,1)S(1)}, u32[]{:S(2)}, u32[]{:S(2)}) collective-permute-start(bf16[128,512]{1,0:T(8,128)(2,1)S(1)} %get-tuple-element.111), channel_id=1, source_target_pairs={{0,27},{1,26},{2,25},{3,24},{4,31},{5,30},{6,29},{7,28},{8,19},{9,... | collective-permute-start | bytes 393224 | tf_op jit(solution)/shard_map/ppermute | solution.py:237
  158.5 2.8 %collective-permute-start.45 = (bf16[128,512]{1,0:T(8,128)(2,1)S(1)}, bf16[128,512]{1,0:T(8,128)(2,1)S(1)}, u32[]{:S(2)}, u32[]{:S(2)}) collective-permute-start(bf16[128,512]{1,0:T(8,128)(2,1)S(1)} %get-tuple-element.113), channel_id=1, source_target_pairs={{0,19},{1,18},{2,17},{3,16},{4,23},{5,22},{6,21},{7,20},{8,27},{9,... | collective-permute-start | bytes 393224 | tf_op jit(solution)/shard_map/ppermute | solution.py:237
  162.6 2.2 %collective-permute-start.46 = (bf16[128,512]{1,0:T(8,128)(2,1)S(1)}, bf16[128,512]{1,0:T(8,128)(2,1)S(1)}, u32[]{:S(2)}, u32[]{:S(2)}) collective-permute-start(bf16[128,512]{1,0:T(8,128)(2,1)S(1)} %get-tuple-element.114), channel_id=1, source_target_pairs={{0,12},{1,13},{2,14},{3,15},{4,8},{5,9},{6,10},{7,11},{8,4},{9,5},... | collective-permute-start | bytes 393224 | tf_op jit(solution)/shard_map/ppermute | solution.py:237
  164.9 2.4 %collective-permute-start.47 = (bf16[128,512]{1,0:T(8,128)(2,1)S(1)}, bf16[128,512]{1,0:T(8,128)(2,1)S(1)}, u32[]{:S(2)}, u32[]{:S(2)}) collective-permute-start(bf16[128,512]{1,0:T(8,128)(2,1)S(1)} %get-tuple-element.115), channel_id=1, source_target_pairs={{0,28},{1,29},{2,30},{3,31},{4,24},{5,25},{6,26},{7,27},{8,20},{9,... | collective-permute-start | bytes 393224 | tf_op jit(solution)/shard_map/ppermute | solution.py:237
  167.4 1.9 collective-permute-done.44.refs_14_
  169.4 5.8 %collective-permute-done.45.refs_15_ = bf16[128,512]{1,0:T(8,128)(2,1)S(1)} collective-permute-done((bf16[128,512]{1,0:T(8,128)(2,1)S(1)}, bf16[128,512]{1,0:T(8,128)(2,1)S(1)}, u32[]{:S(2)}, u32[]{:S(2)}) %collective-permute-start.45) | collective-permute-done | bytes 131104 | tf_op jit(solution)/shard_map/ppermute | solution.py:237
  176.3 2.2 collective-permute-start.51
  179.3 2.1 collective-permute-start.53
  181.4 2.3 %collective-permute-start.54 = (bf16[128,512]{1,0:T(8,128)(2,1)S(1)}, bf16[128,512]{1,0:T(8,128)(2,1)S(1)}, u32[]{:S(2)}, u32[]{:S(2)}) collective-permute-start(bf16[128,512]{1,0:T(8,128)(2,1)S(1)} %get-tuple-element.122), channel_id=1, source_target_pairs={{0,14},{1,15},{2,12},{3,13},{4,10},{5,11},{6,8},{7,9},{8,6},{9,7},... | collective-permute-start | bytes 393224 | tf_op jit(solution)/shard_map/ppermute | solution.py:237
  183.7 2.7 %collective-permute-start.55 = (bf16[128,512]{1,0:T(8,128)(2,1)S(1)}, bf16[128,512]{1,0:T(8,128)(2,1)S(1)}, u32[]{:S(2)}, u32[]{:S(2)}) collective-permute-start(bf16[128,512]{1,0:T(8,128)(2,1)S(1)} %get-tuple-element.123), channel_id=1, source_target_pairs={{0,30},{1,31},{2,28},{3,29},{4,26},{5,27},{6,24},{7,25},{8,22},{9,... | collective-permute-start | bytes 393224 | tf_op jit(solution)/shard_map/ppermute | solution.py:237
  186.4 4.5 %collective-permute-start.56 = (bf16[128,512]{1,0:T(8,128)(2,1)S(1)}, bf16[128,512]{1,0:T(8,128)(2,1)S(1)}, u32[]{:S(2)}, u32[]{:S(2)}) collective-permute-start(bf16[128,512]{1,0:T(8,128)(2,1)S(1)} %get-tuple-element.124), channel_id=1, source_target_pairs={{0,6},{1,7},{2,4},{3,5},{4,2},{5,3},{6,0},{7,1},{8,14},{9,15},{10,... | collective-permute-start | bytes 393224 | tf_op jit(solution)/shard_map/ppermute | solution.py:237
  191.6 4.8 %collective-permute-start.58 = (bf16[128,512]{1,0:T(8,128)(2,1)S(1)}, bf16[128,512]{1,0:T(8,128)(2,1)S(1)}, u32[]{:S(2)}, u32[]{:S(2)}) collective-permute-start(bf16[128,512]{1,0:T(8,128)(2,1)S(1)} %get-tuple-element.126), channel_id=1, source_target_pairs={{0,15},{1,14},{2,13},{3,12},{4,11},{5,10},{6,9},{7,8},{8,7},{9,6},... | collective-permute-start | bytes 393224 | tf_op jit(solution)/shard_map/ppermute | solution.py:237
  197.9 2.1 collective-permute-done.55.refs_25_
  200.0 4.1 %collective-permute-start.60 = (bf16[128,512]{1,0:T(8,128)(2,1)S(1)}, bf16[128,512]{1,0:T(8,128)(2,1)S(1)}, u32[]{:S(2)}, u32[]{:S(2)}) collective-permute-start(bf16[128,512]{1,0:T(8,128)(2,1)S(1)} %get-tuple-element.128), channel_id=1, source_target_pairs={{0,7},{1,6},{2,5},{3,4},{4,3},{5,2},{6,1},{7,0},{8,15},{9,14},{10,... | collective-permute-start | bytes 393224 | tf_op jit(solution)/shard_map/ppermute | solution.py:237
  206.7 5.4 %collective-permute-done.58.refs_28_ = bf16[128,512]{1,0:T(8,128)(2,1)S(1)} collective-permute-done((bf16[128,512]{1,0:T(8,128)(2,1)S(1)}, bf16[128,512]{1,0:T(8,128)(2,1)S(1)}, u32[]{:S(2)}, u32[]{:S(2)}) %collective-permute-start.58) | collective-permute-done | bytes 131104 | tf_op jit(solution)/shard_map/ppermute | solution.py:237
  212.1 3.6 %collective-permute-done.59.refs_29_ = bf16[128,512]{1,0:T(8,128)(2,1)S(1)} collective-permute-done((bf16[128,512]{1,0:T(8,128)(2,1)S(1)}, bf16[128,512]{1,0:T(8,128)(2,1)S(1)}, u32[]{:S(2)}, u32[]{:S(2)}) %collective-permute-start.59) | collective-permute-done | bytes 131104 | tf_op jit(solution)/shard_map/ppermute | solution.py:237
  217.0 3.4 %collective-permute-done.61.refs_31_ = bf16[128,512]{1,0:T(8,128)(2,1)S(1)} collective-permute-done((bf16[128,512]{1,0:T(8,128)(2,1)S(1)}, bf16[128,512]{1,0:T(8,128)(2,1)S(1)}, u32[]{:S(2)}, u32[]{:S(2)}) %collective-permute-start.61) | collective-permute-done | bytes 131104 | tf_op jit(solution)/shard_map/ppermute | solution.py:237
  220.5 2.5 %unpack.1 = (bf16[2,1,4,256,512]{4,3,2,1,0:T(8,128)(2,1)}, bf16[2,1,4,256,512]{4,3,2,1,0:T(8,128)(2,1)}) custom-call(s32[1]{0:T(128)} %bitcast.place_ref, bf16[128,128]{1,0:T(8,128)(2,1)S(1)} %copy-done.2, bf16[128,512]{1,0:T(8,128)(2,1)S(1)} %collective-permute-done.31.refs_0_, bf16[128,512]{1,0:T(8,128)(2,1)S(1)} %collective-permute-done.32.refs_1_, ...), custom_call_target="tpu_custom_call" | custom-call | tf_op jit(solution)/shard_map/unpack/pallas_call | solution.py:207
  (94 shorter events, 34.9 us)
Async XLA Ops:
  9.3 19.9 %collective-permute-start = (bf16[128,512]{1,0:T(8,128)(2,1)}, bf16[128,512]{1,0:T(8,128)(2,1)S(1)}, u32[]{:S(2)}, u32[]{:S(2)}) collective-permute-start(bf16[128,512]{1,0:T(8,128)(2,1)} %get-tuple-element.66), channel_id=1, source_target_pairs={{0,8},{1,9},{2,10},{3,11},{4,12},{5,13},{6,14},{7,15},{8,0},{9,1},... | collective-permute-start | bytes 393224 | tf_op jit(solution)/shard_map/ppermute | solution.py:237
  13.4 19.9 %collective-permute-start.1 = (bf16[128,512]{1,0:T(8,128)(2,1)}, bf16[128,512]{1,0:T(8,128)(2,1)S(1)}, u32[]{:S(2)}, u32[]{:S(2)}) collective-permute-start(bf16[128,512]{1,0:T(8,128)(2,1)} %get-tuple-element.67), channel_id=1, source_target_pairs={{0,24},{1,25},{2,26},{3,27},{4,28},{5,29},{6,30},{7,31},{8,16},{9,... | collective-permute-start | bytes 393224 | tf_op jit(solution)/shard_map/ppermute | solution.py:237
  14.7 18.6 %collective-permute-start.2 = (bf16[128,512]{1,0:T(8,128)(2,1)}, bf16[128,512]{1,0:T(8,128)(2,1)S(1)}, u32[]{:S(2)}, u32[]{:S(2)}) collective-permute-start(bf16[128,512]{1,0:T(8,128)(2,1)} %get-tuple-element.69), channel_id=1, source_target_pairs={{0,16},{1,17},{2,18},{3,19},{4,20},{5,21},{6,22},{7,23},{8,24},{9,... | collective-permute-start | bytes 393224 | tf_op jit(solution)/shard_map/ppermute | solution.py:237
  14.9 18.4 %collective-permute-start.3 = (bf16[128,512]{1,0:T(8,128)(2,1)}, bf16[128,512]{1,0:T(8,128)(2,1)S(1)}, u32[]{:S(2)}, u32[]{:S(2)}) collective-permute-start(bf16[128,512]{1,0:T(8,128)(2,1)} %get-tuple-element.70), channel_id=1, source_target_pairs={{0,9},{1,8},{2,11},{3,10},{4,13},{5,12},{6,15},{7,14},{8,1},{9,0},... | collective-permute-start | bytes 393224 | tf_op jit(solution)/shard_map/ppermute | solution.py:237
  16.4 20.3 %collective-permute-start.4 = (bf16[128,512]{1,0:T(8,128)(2,1)}, bf16[128,512]{1,0:T(8,128)(2,1)S(1)}, u32[]{:S(2)}, u32[]{:S(2)}) collective-permute-start(bf16[128,512]{1,0:T(8,128)(2,1)} %get-tuple-element.71), channel_id=1, source_target_pairs={{0,25},{1,24},{2,27},{3,26},{4,29},{5,28},{6,31},{7,30},{8,17},{9,... | collective-permute-start | bytes 393224 | tf_op jit(solution)/shard_map/ppermute | solution.py:237
  33.3 13.7 %collective-permute-start.7 = (bf16[128,512]{1,0:T(8,128)(2,1)}, bf16[128,512]{1,0:T(8,128)(2,1)S(1)}, u32[]{:S(2)}, u32[]{:S(2)}) collective-permute-start(bf16[128,512]{1,0:T(8,128)(2,1)} %get-tuple-element.74), channel_id=1, source_target_pairs={{0,10},{1,11},{2,8},{3,9},{4,14},{5,15},{6,12},{7,13},{8,2},{9,3},... | collective-permute-start | bytes 393224 | tf_op jit(solution)/shard_map/ppermute | solution.py:237
  33.3 16.0 %collective-permute-start.8 = (bf16[128,512]{1,0:T(8,128)(2,1)}, bf16[128,512]{1,0:T(8,128)(2,1)S(1)}, u32[]{:S(2)}, u32[]{:S(2)}) collective-permute-start(bf16[128,512]{1,0:T(8,128)(2,1)} %get-tuple-element.75), channel_id=1, source_target_pairs={{0,26},{1,27},{2,24},{3,25},{4,30},{5,31},{6,28},{7,29},{8,18},{9,... | collective-permute-start | bytes 393224 | tf_op jit(solution)/shard_map/ppermute | solution.py:237
  36.7 14.0 %collective-permute-start.9 = (bf16[128,512]{1,0:T(8,128)(2,1)}, bf16[128,512]{1,0:T(8,128)(2,1)S(1)}, u32[]{:S(2)}, u32[]{:S(2)}) collective-permute-start(bf16[128,512]{1,0:T(8,128)(2,1)} %get-tuple-element.76), channel_id=1, source_target_pairs={{0,2},{1,3},{2,0},{3,1},{4,6},{5,7},{6,4},{7,5},{8,10},{9,11},{10,... | collective-permute-start | bytes 393224 | tf_op jit(solution)/shard_map/ppermute | solution.py:237
  38.5 17.7 %collective-permute-start.10 = (bf16[128,512]{1,0:T(8,128)(2,1)}, bf16[128,512]{1,0:T(8,128)(2,1)S(1)}, u32[]{:S(2)}, u32[]{:S(2)}) collective-permute-start(bf16[128,512]{1,0:T(8,128)(2,1)} %get-tuple-element.77), channel_id=1, source_target_pairs={{0,18},{1,19},{2,16},{3,17},{4,22},{5,23},{6,20},{7,21},{8,26},{9,... | collective-permute-start | bytes 393224 | tf_op jit(solution)/shard_map/ppermute | solution.py:237
  40.1 27.9 %collective-permute-start.11 = (bf16[128,512]{1,0:T(8,128)(2,1)}, bf16[128,512]{1,0:T(8,128)(2,1)S(1)}, u32[]{:S(2)}, u32[]{:S(2)}) collective-permute-start(bf16[128,512]{1,0:T(8,128)(2,1)} %get-tuple-element.78), channel_id=1, source_target_pairs={{0,11},{1,10},{2,9},{3,8},{4,15},{5,14},{6,13},{7,12},{8,3},{9,2},... | collective-permute-start | bytes 393224 | tf_op jit(solution)/shard_map/ppermute | solution.py:237
  47.0 21.4 %collective-permute-start.12 = (bf16[128,512]{1,0:T(8,128)(2,1)}, bf16[128,512]{1,0:T(8,128)(2,1)S(1)}, u32[]{:S(2)}, u32[]{:S(2)}) collective-permute-start(bf16[128,512]{1,0:T(8,128)(2,1)} %get-tuple-element.79), channel_id=1, source_target_pairs={{0,27},{1,26},{2,25},{3,24},{4,31},{5,30},{6,29},{7,28},{8,19},{9,... | collective-permute-start | bytes 393224 | tf_op jit(solution)/shard_map/ppermute | solution.py:237
  49.3 19.1 %collective-permute-start.13 = (bf16[128,512]{1,0:T(8,128)(2,1)}, bf16[128,512]{1,0:T(8,128)(2,1)S(1)}, u32[]{:S(2)}, u32[]{:S(2)}) collective-permute-start(bf16[128,512]{1,0:T(8,128)(2,1)} %get-tuple-element.80), channel_id=1, source_target_pairs={{0,3},{1,2},{2,1},{3,0},{4,7},{5,6},{6,5},{7,4},{8,11},{9,10},{10,... | collective-permute-start | bytes 393224 | tf_op jit(solution)/shard_map/ppermute | solution.py:237
  50.7 20.2 %collective-permute-start.14 = (bf16[128,512]{1,0:T(8,128)(2,1)}, bf16[128,512]{1,0:T(8,128)(2,1)S(1)}, u32[]{:S(2)}, u32[]{:S(2)}) collective-permute-start(bf16[128,512]{1,0:T(8,128)(2,1)} %get-tuple-element.81), channel_id=1, source_target_pairs={{0,19},{1,18},{2,17},{3,16},{4,23},{5,22},{6,21},{7,20},{8,27},{9,... | collective-permute-start | bytes 393224 | tf_op jit(solution)/shard_map/ppermute | solution.py:237
  56.2 16.3 %collective-permute-start.15 = (bf16[128,512]{1,0:T(8,128)(2,1)}, bf16[128,512]{1,0:T(8,128)(2,1)S(1)}, u32[]{:S(2)}, u32[]{:S(2)}) collective-permute-start(bf16[128,512]{1,0:T(8,128)(2,1)} %get-tuple-element.82), channel_id=1, source_target_pairs={{0,12},{1,13},{2,14},{3,15},{4,8},{5,9},{6,10},{7,11},{8,4},{9,5},... | collective-permute-start | bytes 393224 | tf_op jit(solution)/shard_map/ppermute | solution.py:237
  68.4 13.3 %collective-permute-start.18 = (bf16[128,512]{1,0:T(8,128)(2,1)}, bf16[128,512]{1,0:T(8,128)(2,1)S(1)}, u32[]{:S(2)}, u32[]{:S(2)}) collective-permute-start(bf16[128,512]{1,0:T(8,128)(2,1)} %get-tuple-element.85), channel_id=1, source_target_pairs={{0,20},{1,21},{2,22},{3,23},{4,16},{5,17},{6,18},{7,19},{8,28},{9,... | collective-permute-start | bytes 393224 | tf_op jit(solution)/shard_map/ppermute | solution.py:237
  70.9 17.3 %collective-permute-start.19 = (bf16[128,512]{1,0:T(8,128)(2,1)}, bf16[128,512]{1,0:T(8,128)(2,1)S(1)}, u32[]{:S(2)}, u32[]{:S(2)}) collective-permute-start(bf16[128,512]{1,0:T(8,128)(2,1)} %get-tuple-element.86), channel_id=1, source_target_pairs={{0,13},{1,12},{2,15},{3,14},{4,9},{5,8},{6,11},{7,10},{8,5},{9,4},... | collective-permute-start | bytes 393224 | tf_op jit(solution)/shard_map/ppermute | solution.py:237
  72.5 16.4 %collective-permute-start.20 = (bf16[128,512]{1,0:T(8,128)(2,1)}, bf16[128,512]{1,0:T(8,128)(2,1)S(1)}, u32[]{:S(2)}, u32[]{:S(2)}) collective-permute-start(bf16[128,512]{1,0:T(8,128)(2,1)} %get-tuple-element.87), channel_id=1, source_target_pairs={{0,29},{1,28},{2,31},{3,30},{4,25},{5,24},{6,27},{7,26},{8,21},{9,... | collective-permute-start | bytes 393224 | tf_op jit(solution)/shard_map/ppermute | solution.py:237
  77.8 14.4 %collective-permute-start.22 = (bf16[128,512]{1,0:T(8,128)(2,1)}, bf16[128,512]{1,0:T(8,128)(2,1)S(1)}, u32[]{:S(2)}, u32[]{:S(2)}) collective-permute-start(bf16[128,512]{1,0:T(8,128)(2,1)} %get-tuple-element.89), channel_id=1, source_target_pairs={{0,21},{1,20},{2,23},{3,22},{4,17},{5,16},{6,19},{7,18},{8,29},{9,... | collective-permute-start | bytes 393224 | tf_op jit(solution)/shard_map/ppermute | solution.py:237
  81.7 17.4 %collective-permute-start.23 = (bf16[128,512]{1,0:T(8,128)(2,1)}, bf16[128,512]{1,0:T(8,128)(2,1)S(1)}, u32[]{:S(2)}, u32[]{:S(2)}) collective-permute-start(bf16[128,512]{1,0:T(8,128)(2,1)} %get-tuple-element.90), channel_id=1, source_target_pairs={{0,14},{1,15},{2,12},{3,13},{4,10},{5,11},{6,8},{7,9},{8,6},{9,7},... | collective-permute-start | bytes 393224 | tf_op jit(solution)/shard_map/ppermute | solution.py:237
  88.9 12.3 %collective-permute-start.25 = (bf16[128,512]{1,0:T(8,128)(2,1)}, bf16[128,512]{1,0:T(8,128)(2,1)S(1)}, u32[]{:S(2)}, u32[]{:S(2)}) collective-permute-start(bf16[128,512]{1,0:T(8,128)(2,1)} %get-tuple-element.92), channel_id=1, source_target_pairs={{0,6},{1,7},{2,4},{3,5},{4,2},{5,3},{6,0},{7,1},{8,14},{9,15},{10,... | collective-permute-start | bytes 393224 | tf_op jit(solution)/shard_map/ppermute | solution.py:237
  89.1 17.5 %collective-permute-start.26 = (bf16[128,512]{1,0:T(8,128)(2,1)}, bf16[128,512]{1,0:T(8,128)(2,1)S(1)}, u32[]{:S(2)}, u32[]{:S(2)}) collective-permute-start(bf16[128,512]{1,0:T(8,128)(2,1)} %get-tuple-element.93), channel_id=1, source_target_pairs={{0,22},{1,23},{2,20},{3,21},{4,18},{5,19},{6,16},{7,17},{8,30},{9,... | collective-permute-start | bytes 393224 | tf_op jit(solution)/shard_map/ppermute | solution.py:237
  92.2 14.6 %collective-permute-start.27 = (bf16[128,512]{1,0:T(8,128)(2,1)}, bf16[128,512]{1,0:T(8,128)(2,1)S(1)}, u32[]{:S(2)}, u32[]{:S(2)}) collective-permute-start(bf16[128,512]{1,0:T(8,128)(2,1)} %get-tuple-element.94), channel_id=1, source_target_pairs={{0,15},{1,14},{2,13},{3,12},{4,11},{5,10},{6,9},{7,8},{8,7},{9,6},... | collective-permute-start | bytes 393224 | tf_op jit(solution)/shard_map/ppermute | solution.py:237
  101.2 13.8 %collective-permute-start.30 = (bf16[128,512]{1,0:T(8,128)(2,1)}, bf16[128,512]{1,0:T(8,128)(2,1)S(1)}, u32[]{:S(2)}, u32[]{:S(2)}) collective-permute-start(bf16[128,512]{1,0:T(8,128)(2,1)} %get-tuple-element.97), channel_id=1, source_target_pairs={{0,23},{1,22},{2,21},{3,20},{4,19},{5,18},{6,17},{7,16},{8,31},{9,... | collective-permute-start | bytes 393224 | tf_op jit(solution)/shard_map/ppermute | solution.py:237
  118.2 18.0 %collective-permute-start.31 = (bf16[128,512]{1,0:T(8,128)(2,1)S(1)}, bf16[128,512]{1,0:T(8,128)(2,1)S(1)}, u32[]{:S(2)}, u32[]{:S(2)}) collective-permute-start(bf16[128,512]{1,0:T(8,128)(2,1)S(1)} %get-tuple-element.98), channel_id=1, source_target_pairs={{0,8},{1,9},{2,10},{3,11},{4,12},{5,13},{6,14},{7,15},{8,0},{9,1},... | collective-permute-start | bytes 393224 | tf_op jit(solution)/shard_map/ppermute | solution.py:237
  118.8 20.0 %collective-permute-start.32 = (bf16[128,512]{1,0:T(8,128)(2,1)S(1)}, bf16[128,512]{1,0:T(8,128)(2,1)S(1)}, u32[]{:S(2)}, u32[]{:S(2)}) collective-permute-start(bf16[128,512]{1,0:T(8,128)(2,1)S(1)} %get-tuple-element.99), channel_id=1, source_target_pairs={{0,24},{1,25},{2,26},{3,27},{4,28},{5,29},{6,30},{7,31},{8,16},{9,... | collective-permute-start | bytes 393224 | tf_op jit(solution)/shard_map/ppermute | solution.py:237
  121.2 18.3 %collective-permute-start.33 = (bf16[128,512]{1,0:T(8,128)(2,1)S(1)}, bf16[128,512]{1,0:T(8,128)(2,1)S(1)}, u32[]{:S(2)}, u32[]{:S(2)}) collective-permute-start(bf16[128,512]{1,0:T(8,128)(2,1)S(1)} %get-tuple-element.101), channel_id=1, source_target_pairs={{0,16},{1,17},{2,18},{3,19},{4,20},{5,21},{6,22},{7,23},{8,24},{9,... | collective-permute-start | bytes 393224 | tf_op jit(solution)/shard_map/ppermute | solution.py:237
  122.7 18.5 %collective-permute-start.34 = (bf16[128,512]{1,0:T(8,128)(2,1)S(1)}, bf16[128,512]{1,0:T(8,128)(2,1)S(1)}, u32[]{:S(2)}, u32[]{:S(2)}) collective-permute-start(bf16[128,512]{1,0:T(8,128)(2,1)S(1)} %get-tuple-element.102), channel_id=1, source_target_pairs={{0,9},{1,8},{2,11},{3,10},{4,13},{5,12},{6,15},{7,14},{8,1},{9,0},... | collective-permute-start | bytes 393224 | tf_op jit(solution)/shard_map/ppermute | solution.py:237
  122.7 27.2 %collective-permute-start.35 = (bf16[128,512]{1,0:T(8,128)(2,1)S(1)}, bf16[128,512]{1,0:T(8,128)(2,1)S(1)}, u32[]{:S(2)}, u32[]{:S(2)}) collective-permute-start(bf16[128,512]{1,0:T(8,128)(2,1)S(1)} %get-tuple-element.103), channel_id=1, source_target_pairs={{0,25},{1,24},{2,27},{3,26},{4,29},{5,28},{6,31},{7,30},{8,17},{9,... | collective-permute-start | bytes 393224 | tf_op jit(solution)/shard_map/ppermute | solution.py:237
  136.3 13.6 %collective-permute-start.36 = (bf16[128,512]{1,0:T(8,128)(2,1)S(1)}, bf16[128,512]{1,0:T(8,128)(2,1)S(1)}, u32[]{:S(2)}, u32[]{:S(2)}) collective-permute-start(bf16[128,512]{1,0:T(8,128)(2,1)S(1)} %get-tuple-element.104), channel_id=1, source_target_pairs={{0,1},{1,0},{2,3},{3,2},{4,5},{5,4},{6,7},{7,6},{8,9},{9,8},{10,11... | collective-permute-start | bytes 393224 | tf_op jit(solution)/shard_map/ppermute | solution.py:237
  139.6 13.5 %collective-permute-start.38 = (bf16[128,512]{1,0:T(8,128)(2,1)S(1)}, bf16[128,512]{1,0:T(8,128)(2,1)S(1)}, u32[]{:S(2)}, u32[]{:S(2)}) collective-permute-start(bf16[128,512]{1,0:T(8,128)(2,1)S(1)} %get-tuple-element.106), channel_id=1, source_target_pairs={{0,10},{1,11},{2,8},{3,9},{4,14},{5,15},{6,12},{7,13},{8,2},{9,3},... | collective-permute-start | bytes 393224 | tf_op jit(solution)/shard_map/ppermute | solution.py:237
  141.2 15.2 %collective-permute-start.39 = (bf16[128,512]{1,0:T(8,128)(2,1)S(1)}, bf16[128,512]{1,0:T(8,128)(2,1)S(1)}, u32[]{:S(2)}, u32[]{:S(2)}) collective-permute-start(bf16[128,512]{1,0:T(8,128)(2,1)S(1)} %get-tuple-element.107), channel_id=1, source_target_pairs={{0,26},{1,27},{2,24},{3,25},{4,30},{5,31},{6,28},{7,29},{8,18},{9,... | collective-permute-start | bytes 393224 | tf_op jit(solution)/shard_map/ppermute | solution.py:237
  149.9 12.8 %collective-permute-start.41 = (bf16[128,512]{1,0:T(8,128)(2,1)S(1)}, bf16[128,512]{1,0:T(8,128)(2,1)S(1)}, u32[]{:S(2)}, u32[]{:S(2)}) collective-permute-start(bf16[128,512]{1,0:T(8,128)(2,1)S(1)} %get-tuple-element.109), channel_id=1, source_target_pairs={{0,18},{1,19},{2,16},{3,17},{4,22},{5,23},{6,20},{7,21},{8,26},{9,... | collective-permute-start | bytes 393224 | tf_op jit(solution)/shard_map/ppermute | solution.py:237
  149.9 15.0 %collective-permute-start.42 = (bf16[128,512]{1,0:T(8,128)(2,1)S(1)}, bf16[128,512]{1,0:T(8,128)(2,1)S(1)}, u32[]{:S(2)}, u32[]{:S(2)}) collective-permute-start(bf16[128,512]{1,0:T(8,128)(2,1)S(1)} %get-tuple-element.110), channel_id=1, source_target_pairs={{0,11},{1,10},{2,9},{3,8},{4,15},{5,14},{6,13},{7,12},{8,3},{9,2},... | collective-permute-start | bytes 393224 | tf_op jit(solution)/shard_map/ppermute | solution.py:237
  153.0 14.4 %collective-permute-start.43 = (bf16[128,512]{1,0:T(8,128)(2,1)S(1)}, bf16[128,512]{1,0:T(8,128)(2,1)S(1)}, u32[]{:S(2)}, u32[]{:S(2)}) collective-permute-start(bf16[128,512]{1,0:T(8,128)(2,1)S(1)} %get-tuple-element.111), channel_id=1, source_target_pairs={{0,27},{1,26},{2,25},{3,24},{4,31},{5,30},{6,29},{7,28},{8,19},{9,... | collective-permute-start | bytes 393224 | tf_op jit(solution)/shard_map/ppermute | solution.py:237
  156.4 12.9 %collective-permute-start.44 = (bf16[128,512]{1,0:T(8,128)(2,1)S(1)}, bf16[128,512]{1,0:T(8,128)(2,1)S(1)}, u32[]{:S(2)}, u32[]{:S(2)}) collective-permute-start(bf16[128,512]{1,0:T(8,128)(2,1)S(1)} %get-tuple-element.112), channel_id=1, source_target_pairs={{0,3},{1,2},{2,1},{3,0},{4,7},{5,6},{6,5},{7,4},{8,11},{9,10},{10,... | collective-permute-start | bytes 393224 | tf_op jit(solution)/shard_map/ppermute | solution.py:237
  158.5 16.7 %collective-permute-start.45 = (bf16[128,512]{1,0:T(8,128)(2,1)S(1)}, bf16[128,512]{1,0:T(8,128)(2,1)S(1)}, u32[]{:S(2)}, u32[]{:S(2)}) collective-permute-start(bf16[128,512]{1,0:T(8,128)(2,1)S(1)} %get-tuple-element.113), channel_id=1, source_target_pairs={{0,19},{1,18},{2,17},{3,16},{4,23},{5,22},{6,21},{7,20},{8,27},{9,... | collective-permute-start | bytes 393224 | tf_op jit(solution)/shard_map/ppermute | solution.py:237
  162.6 13.7 %collective-permute-start.46 = (bf16[128,512]{1,0:T(8,128)(2,1)S(1)}, bf16[128,512]{1,0:T(8,128)(2,1)S(1)}, u32[]{:S(2)}, u32[]{:S(2)}) collective-permute-start(bf16[128,512]{1,0:T(8,128)(2,1)S(1)} %get-tuple-element.114), channel_id=1, source_target_pairs={{0,12},{1,13},{2,14},{3,15},{4,8},{5,9},{6,10},{7,11},{8,4},{9,5},... | collective-permute-start | bytes 393224 | tf_op jit(solution)/shard_map/ppermute | solution.py:237
  164.9 13.6 %collective-permute-start.47 = (bf16[128,512]{1,0:T(8,128)(2,1)S(1)}, bf16[128,512]{1,0:T(8,128)(2,1)S(1)}, u32[]{:S(2)}, u32[]{:S(2)}) collective-permute-start(bf16[128,512]{1,0:T(8,128)(2,1)S(1)} %get-tuple-element.115), channel_id=1, source_target_pairs={{0,28},{1,29},{2,30},{3,31},{4,24},{5,25},{6,26},{7,27},{8,20},{9,... | collective-permute-start | bytes 393224 | tf_op jit(solution)/shard_map/ppermute | solution.py:237
  178.5 12.4 %collective-permute-start.52 = (bf16[128,512]{1,0:T(8,128)(2,1)S(1)}, bf16[128,512]{1,0:T(8,128)(2,1)S(1)}, u32[]{:S(2)}, u32[]{:S(2)}) collective-permute-start(bf16[128,512]{1,0:T(8,128)(2,1)S(1)} %get-tuple-element.120), channel_id=1, source_target_pairs={{0,5},{1,4},{2,7},{3,6},{4,1},{5,0},{6,3},{7,2},{8,13},{9,12},{10,... | collective-permute-start | bytes 393224 | tf_op jit(solution)/shard_map/ppermute | solution.py:237
  179.3 12.3 %collective-permute-start.53 = (bf16[128,512]{1,0:T(8,128)(2,1)S(1)}, bf16[128,512]{1,0:T(8,128)(2,1)S(1)}, u32[]{:S(2)}, u32[]{:S(2)}) collective-permute-start(bf16[128,512]{1,0:T(8,128)(2,1)S(1)} %get-tuple-element.121), channel_id=1, source_target_pairs={{0,21},{1,20},{2,23},{3,22},{4,17},{5,16},{6,19},{7,18},{8,29},{9,... | collective-permute-start | bytes 393224 | tf_op jit(solution)/shard_map/ppermute | solution.py:237
  181.4 15.4 %collective-permute-start.54 = (bf16[128,512]{1,0:T(8,128)(2,1)S(1)}, bf16[128,512]{1,0:T(8,128)(2,1)S(1)}, u32[]{:S(2)}, u32[]{:S(2)}) collective-permute-start(bf16[128,512]{1,0:T(8,128)(2,1)S(1)} %get-tuple-element.122), channel_id=1, source_target_pairs={{0,14},{1,15},{2,12},{3,13},{4,10},{5,11},{6,8},{7,9},{8,6},{9,7},... | collective-permute-start | bytes 393224 | tf_op jit(solution)/shard_map/ppermute | solution.py:237
  183.7 16.2 %collective-permute-start.55 = (bf16[128,512]{1,0:T(8,128)(2,1)S(1)}, bf16[128,512]{1,0:T(8,128)(2,1)S(1)}, u32[]{:S(2)}, u32[]{:S(2)}) collective-permute-start(bf16[128,512]{1,0:T(8,128)(2,1)S(1)} %get-tuple-element.123), channel_id=1, source_target_pairs={{0,30},{1,31},{2,28},{3,29},{4,26},{5,27},{6,24},{7,25},{8,22},{9,... | collective-permute-start | bytes 393224 | tf_op jit(solution)/shard_map/ppermute | solution.py:237
  186.4 17.6 %collective-permute-start.56 = (bf16[128,512]{1,0:T(8,128)(2,1)S(1)}, bf16[128,512]{1,0:T(8,128)(2,1)S(1)}, u32[]{:S(2)}, u32[]{:S(2)}) collective-permute-start(bf16[128,512]{1,0:T(8,128)(2,1)S(1)} %get-tuple-element.124), channel_id=1, source_target_pairs={{0,6},{1,7},{2,4},{3,5},{4,2},{5,3},{6,0},{7,1},{8,14},{9,15},{10,... | collective-permute-start | bytes 393224 | tf_op jit(solution)/shard_map/ppermute | solution.py:237
  190.9 15.8 %collective-permute-start.57 = (bf16[128,512]{1,0:T(8,128)(2,1)S(1)}, bf16[128,512]{1,0:T(8,128)(2,1)S(1)}, u32[]{:S(2)}, u32[]{:S(2)}) collective-permute-start(bf16[128,512]{1,0:T(8,128)(2,1)S(1)} %get-tuple-element.125), channel_id=1, source_target_pairs={{0,22},{1,23},{2,20},{3,21},{4,18},{5,19},{6,16},{7,17},{8,30},{9,... | collective-permute-start | bytes 393224 | tf_op jit(solution)/shard_map/ppermute | solution.py:237
  191.6 20.5 %collective-permute-start.58 = (bf16[128,512]{1,0:T(8,128)(2,1)S(1)}, bf16[128,512]{1,0:T(8,128)(2,1)S(1)}, u32[]{:S(2)}, u32[]{:S(2)}) collective-permute-start(bf16[128,512]{1,0:T(8,128)(2,1)S(1)} %get-tuple-element.126), channel_id=1, source_target_pairs={{0,15},{1,14},{2,13},{3,12},{4,11},{5,10},{6,9},{7,8},{8,7},{9,6},... | collective-permute-start | bytes 393224 | tf_op jit(solution)/shard_map/ppermute | solution.py:237
  196.8 18.9 %collective-permute-start.59 = (bf16[128,512]{1,0:T(8,128)(2,1)S(1)}, bf16[128,512]{1,0:T(8,128)(2,1)S(1)}, u32[]{:S(2)}, u32[]{:S(2)}) collective-permute-start(bf16[128,512]{1,0:T(8,128)(2,1)S(1)} %get-tuple-element.127), channel_id=1, source_target_pairs={{0,31},{1,30},{2,29},{3,28},{4,27},{5,26},{6,25},{7,24},{8,23},{9,... | collective-permute-start | bytes 393224 | tf_op jit(solution)/shard_map/ppermute | solution.py:237
  200.0 17.1 %collective-permute-start.60 = (bf16[128,512]{1,0:T(8,128)(2,1)S(1)}, bf16[128,512]{1,0:T(8,128)(2,1)S(1)}, u32[]{:S(2)}, u32[]{:S(2)}) collective-permute-start(bf16[128,512]{1,0:T(8,128)(2,1)S(1)} %get-tuple-element.128), channel_id=1, source_target_pairs={{0,7},{1,6},{2,5},{3,4},{4,3},{5,2},{6,1},{7,0},{8,15},{9,14},{10,... | collective-permute-start | bytes 393224 | tf_op jit(solution)/shard_map/ppermute | solution.py:237
  204.1 16.4 %collective-permute-start.61 = (bf16[128,512]{1,0:T(8,128)(2,1)S(1)}, bf16[128,512]{1,0:T(8,128)(2,1)S(1)}, u32[]{:S(2)}, u32[]{:S(2)}) collective-permute-start(bf16[128,512]{1,0:T(8,128)(2,1)S(1)} %get-tuple-element.129), channel_id=1, source_target_pairs={{0,23},{1,22},{2,21},{3,20},{4,19},{5,18},{6,17},{7,16},{8,31},{9,... | collective-permute-start | bytes 393224 | tf_op jit(solution)/shard_map/ppermute | solution.py:237
  (21 other events, 767.7 us)

commit v7 on v4

--- a/solution.py
+++ b/solution.py
@@ -3,7 +3,6 @@
 
 import jax
 import jax.numpy as jnp
-import numpy as np
 from jax import lax
 from jax.experimental import pallas as pl
 from jax.experimental.pallas import tpu as pltpu
@@ -11,20 +10,20 @@
 
 SMAX = 2
 TILE = 16
-VMEM_BYTES = 40 * 1024 * 1024
-VMEM_WHOLE = 60 * 1024 * 1024
+VMEM_BYTES = 32 * 1024 * 1024
 APART = 1 << 16
 AXES = ("grp", "mom")
 
 
-def permutation(energies, momenta, rows):
-    inner = energies * momenta
-    size = inner * rows
-    matrix = np.zeros((size, size), np.float32)
-    for state in range(inner):
-        for row in range(rows):
-            matrix[row * inner + state, state * rows + row] = 1.0
-    return matrix
+def turned(states, rows, back):
+    size = states * rows
+    down = lax.broadcasted_iota(jnp.int32, (size, size), 0)
+    across = lax.broadcasted_iota(jnp.int32, (size, size), 1)
+    if back:
+        down, across = across, down
+    bits = states.bit_length() - 1
+    there = (down & (states - 1)) * rows + (down >> bits) == across
+    return jnp.where(there, 1.0, 0.0).astype(jnp.bfloat16)
 
 
 def mix_kernel(matrix_ref, in_ref, out_ref):
@@ -37,14 +36,13 @@
         )
 
 
-def unpack_kernel(perm_ref, in_ref, lesser_ref, greater_ref, held, sent):
+def unpack_kernel(in_ref, lesser_ref, greater_ref, held, sent):
     pieces, rows = held.shape[1], held.shape[4]
+    perm = turned(in_ref.shape[1] // rows, rows, True)
     copies = []
     for side, ref in enumerate((lesser_ref, greater_ref)):
         for piece in range(pieces):
-            moved = jnp.dot(
-                perm_ref[...], in_ref[side * pieces + piece], preferred_element_type=jnp.float32
-            )
+            moved = jnp.dot(perm, in_ref[side * pieces + piece], preferred_element_type=jnp.float32)
             held[side, piece] = moved.astype(held.dtype).reshape(held.shape[2:])
             copy = pltpu.make_async_copy(
                 held.at[side, piece],
@@ -57,53 +55,42 @@
         copy.wait()
 
 
-def pack_kernel(
-    shares, momenta, energies,
-    place_ref, region_ref, shift_ref, occupation_ref, coupling_ref, down_ref, across_ref,
-    perm_ref, lesser_ref, greater_ref, matrix_ref, out_ref, held, arrived, packed, sent,
-):
-    pieces, rows = held.shape[1], held.shape[4]
-    size, width = out_ref.shape[1:]
-    copies = []
+def pack_kernel(matrix_ref, lesser_ref, greater_ref, out_ref):
+    pieces, (size, width) = out_ref.shape[0] // 2, out_ref.shape[1:]
+    rows = lesser_ref.shape[3] // pieces
+    perm = turned(size // rows, rows, False)
     for side, ref in enumerate((lesser_ref, greater_ref)):
         for piece in range(pieces):
-            copy = pltpu.make_async_copy(
-                ref.at[:, 0, :, piece * rows : (piece + 1) * rows, :],
-                held.at[side, piece],
-                arrived.at[side, piece],
-            )
-            copy.start()
-            copies.append(copy)
-    build_kernel(
-        shares, momenta, energies, pieces,
-        place_ref, region_ref, shift_ref, occupation_ref, coupling_ref, down_ref, across_ref,
-        matrix_ref,
-    )
-    for side in range(2):
-        for piece in range(pieces):
-            copies[side * pieces + piece].wait()
-            block = held[side, piece].reshape(size, width)
-            moved = jnp.dot(perm_ref[...], block, preferred_element_type=jnp.float32)
-            place = side * pieces + piece
-            packed[place] = moved.astype(packed.dtype)
-            copies.append(pltpu.make_async_copy(packed.at[place], out_ref.at[place], sent.at[place]))
-            copies[-1].start()
-    for copy in copies[2 * pieces :]:
-        copy.wait()
+            block = ref[:, :, :, piece * rows : (piece + 1) * rows, :].reshape(size, width)
+            moved = jnp.dot(perm, block, preferred_element_type=jnp.float32)
+            out_ref[side * pieces + piece] = moved.astype(out_ref.dtype)
 
 
 def build_kernel(
-    shares, momenta, energies, pieces,
-    place_ref, region_ref, shift_ref, occupation_ref, coupling_ref, down_ref, across_ref, out_ref
+    groups, shares, momenta, energies, region_ref, shift_ref, occupation_ref, coupling_ref, out_ref
 ):
     points = shares * momenta
-    modes = coupling_ref.shape[1]
-    greater = lax.div(place_ref[0], jnp.int32(pieces)).astype(jnp.float32)
-    chosen = coupling_ref[region_ref[0]]
-    size = down_ref.shape[0]
-    pick = down_ref[:, 1:2] == lax.broadcasted_iota(jnp.int32, (size, points), 1)
+    states = energies * momenta
+    regions, modes = coupling_ref.shape[:2]
+    size = out_ref.shape[0]
+    place = lax.axis_index("grp") * shares + lax.axis_index("mom")
+    greater = lax.div(place, jnp.int32(groups * shares // 2)).astype(jnp.float32)
+    chosen = jnp.zeros(coupling_ref.shape[1:], jnp.float32)
+    for region in range(regions):
+        chosen = jnp.where(region_ref[...] == region, coupling_ref[region], chosen)
+
+    def energy_code(at):
+        device, row = at >> (TILE.bit_length() - 1), (at & (TILE - 1)) >> (states.bit_length() - 1)
+        energy = (at & (states - 1)) >> (momenta.bit_length() - 1)
+        return row * APART + (device >> (shares.bit_length() - 1)) * energies + energy
+
+    down = lax.broadcasted_iota(jnp.int32, (size, points), 0)
+    momentum = ((down >> (TILE.bit_length() - 1)) & (shares - 1)) * momenta + (down & (momenta - 1))
+    pick = momentum == lax.broadcasted_iota(jnp.int32, (size, points), 1)
     pick = jnp.where(pick, 1.0, 0.0).astype(jnp.bfloat16)
-    apart = down_ref[:, 0:1] - across_ref[0:1, :]
+    apart = energy_code(lax.broadcasted_iota(jnp.int32, (size, 1), 0)) - energy_code(
+        lax.broadcasted_iota(jnp.int32, (1, size), 1)
+    )
     total = jnp.zeros((size, size), jnp.float32)
     for step in range(-SMAX, SMAX + 1):
         if step == 0:
@@ -114,9 +101,9 @@
             weight = jnp.where(shift_ref[mode] == abs(step), filling, 0.0)
             row = row + weight * chosen[mode : mode + 1, :]
         wide = jnp.broadcast_to(jnp.concatenate([row, row], axis=1), (points, 2 * points))
-        turned = pltpu.roll(wide, 0, 1, stride=1, stride_axis=0)[:, :points]
+        circle = pltpu.roll(wide, 0, 1, stride=1, stride_axis=0)[:, :points]
         half = jnp.dot(
-            pick, turned.astype(jnp.bfloat16), preferred_element_type=jnp.float32
+            pick, circle.astype(jnp.bfloat16), preferred_element_type=jnp.float32
         ).astype(jnp.bfloat16)
         full = lax.dot_general(
             pick, half, (((1,), (1,)), ((), ())), preferred_element_type=jnp.float32
@@ -134,55 +121,41 @@
 SLABS = pl.BlockSpec(memory_space=pl.ANY)
 
 
-def pack(place, lesser, greater, coupling, occupation, shift, region_map, shares, pieces, rows):
+def build(coupling, occupation, shift, region_map, groups, shares, momenta, energies):
+    size, points = groups * shares * TILE, shares * momenta
+    return pl.pallas_call(
+        functools.partial(build_kernel, groups, shares, momenta, energies),
+        out_shape=jax.ShapeDtypeStruct((size, size), jnp.bfloat16),
+        in_specs=[VECTORS, SCALARS, SCALARS, VECTORS],
+        out_specs=VECTORS,
+        compiler_params=params(),
+        cost_estimate=pl.CostEstimate(
+            flops=400 * size * size * points, bytes_accessed=80 * size * size, transcendentals=0
+        ),
+        name="build",
+    )(region_map.reshape(1, 1), shift, occupation, coupling)
+
+
+def pack(matrix, lesser, greater, pieces, rows):
     energies, _, momenta, _, columns = lesser.shape
-    devices = 2 * pieces
     size = energies * momenta * rows
-    fold = TILE // (energies * momenta)
-    group, share, row, energy, momentum = np.unravel_index(
-        np.arange(devices * TILE), (devices // shares, shares, fold, energies, momenta)
-    )
-    code = np.stack([row * APART + group * energies + energy, share * momenta + momentum], axis=1)
-    code = code.astype(np.int32)
-    perm = jnp.asarray(permutation(energies, momenta, rows), jnp.bfloat16)
     return pl.pallas_call(
-        functools.partial(pack_kernel, shares, momenta, energies),
-        out_shape=(
-            jax.ShapeDtypeStruct((devices * TILE, devices * TILE), jnp.bfloat16),
-            jax.ShapeDtypeStruct((devices, size, columns), lesser.dtype),
-        ),
-        in_specs=[SCALARS] * 4 + [VECTORS] * 4 + [SLABS] * 2,
-        out_specs=(VECTORS, SLABS),
-        scratch_shapes=[
-            pltpu.VMEM((2, pieces, energies, momenta, rows, columns), lesser.dtype),
-            pltpu.SemaphoreType.DMA((2, pieces)),
-            pltpu.VMEM((devices, size, columns), lesser.dtype),
-            pltpu.SemaphoreType.DMA((devices,)),
-        ],
-        compiler_params=pltpu.CompilerParams(vmem_limit_bytes=VMEM_WHOLE),
+        pack_kernel,
+        out_shape=jax.ShapeDtypeStruct((2 * pieces, size, columns), lesser.dtype),
+        in_specs=[SLABS, VECTORS, VECTORS],
+        out_specs=VECTORS,
+        compiler_params=params(),
         name="pack",
-    )(
-        place,
-        region_map,
-        shift,
-        occupation,
-        coupling,
-        jnp.asarray(code),
-        jnp.asarray(code.T),
-        perm,
-        lesser,
-        greater,
-    )
+    )(matrix, lesser, greater)
 
 
 def unpack(packed, shape, pieces, rows):
     energies, _, momenta, _, columns = shape
-    perm = jnp.asarray(permutation(energies, momenta, rows).T, jnp.bfloat16)
     out = jax.ShapeDtypeStruct(shape, packed.dtype)
     return pl.pallas_call(
         unpack_kernel,
         out_shape=(out, out),
-        in_specs=[VECTORS, VECTORS],
+        in_specs=[VECTORS],
         out_specs=(SLABS, SLABS),
         scratch_shapes=[
             pltpu.VMEM((2, pieces, energies, momenta, rows, columns), packed.dtype),
@@ -190,7 +163,7 @@
         ],
         compiler_params=params(),
         name="unpack",
-    )(perm, packed)
+    )(packed)
 
 
 def mix(matrix, received):
@@ -211,10 +184,10 @@
 def by_rows(lesser, greater, coupling, occupation, shift, region_map, groups, shares):
     pieces = groups * shares // 2
     rows = lesser.shape[3] // pieces
-    place = (lax.axis_index("grp") * shares + lax.axis_index("mom")).astype(jnp.int32).reshape(1)
-    matrix, sent = pack(
-        place, lesser, greater, coupling, occupation, shift, region_map, shares, pieces, rows
-    )
+    matrix = build(
+        coupling, occupation, shift, region_map, groups, shares, lesser.shape[2], lesser.shape[0]
+    )
+    sent = pack(matrix, lesser, greater, pieces, rows)
     returned = exchange(mix(matrix, exchange(sent)))
     return unpack(returned, lesser.shape, pieces, rows)
 

time: 215 us -> 210 us (0.977)
  Pallas kernels: 14.9 us -> 8.2 us
    pallas_call x2 -> x3, Pallas kernels: 12.6 us -> 5.86 us  [the longest x1 2.44 us: unpack(): pl.pallas_call(unpack_kernel, out_shape=(out, out), in_specs=[VECTORS], o...]
where the time goes in v7:
time: 210 us
  blocking collectives  198 us (94%)
  Pallas kernels  8.2 us (4%)
    all_to_all x2, blocking collectives, exchange(): return lax.all_to_all(array, AXES, split_axis=0, concat_axis=0, tiled=True)  198 us

profile of v7, /device:TPU:0, one launch (start us, length us, event | category | flops | bytes accessed | tf_op | source)
XLA Modules:
  0.0 209.8 jit_solution(3039083351209771097)
XLA Ops:
  1.3 0.0 copy-start.2
  1.3 0.7 copy-done.2
  2.0 0.0 copy-start.3
  2.0 0.7 copy-done.3
  2.6 0.0 copy-start.4
  2.6 0.7 copy-done.4
  3.3 0.0 copy-start
  3.3 0.0 copy-start.1
  3.3 2.2 %build.1.matrix_ref = bf16[512,512]{1,0:T(8,128)(2,1)S(1)} custom-call(s32[1,1]{1,0:T(1,128)} %bitcast.1.region_ref, s32[4]{0:T(128)S(1)} %copy-done.3, f32[4]{0:T(128)S(1)} %copy-done.4, f32[4,4,64]{2,1,0:T(4,128)S(1)} %copy-done.2), custom_call_target="tpu_custom_call" | custom-call | flops 6710886400 | bytes 20971520 | tf_op jit(solution)/shard_map/build/pallas_call | solution.py:126
  5.5 0.0 copy-done
  5.5 0.0 copy-done.1
  5.5 1.2 pack.1
  6.8 101.8 %all_to_all.10.in_ref = bf16[32,128,512]{2,1,0:T(8,128)(2,1)S(1)} all-to-all(bf16[32,128,512]{2,1,0:T(8,128)(2,1)S(1)} %pack.1), channel_id=1, replica_groups=mesh['grp'=2,'mom'=16] {'grp','mom'}, dimensions={0} | all-to-all | bytes 8388608 | tf_op jit(solution)/shard_map/all_to_all | solution.py:181
  108.5 2.3 %mix.1 = bf16[32,128,512]{2,1,0:T(8,128)(2,1)S(1)} custom-call(bf16[512,512]{1,0:T(8,128)(2,1)S(1)} %build.1.matrix_ref, bf16[32,128,512]{2,1,0:T(8,128)(2,1)S(1)} %all_to_all.10.in_ref), custom_call_target="tpu_custom_call" | custom-call | tf_op jit(solution)/shard_map/mix/pallas_call | solution.py:170
  110.9 96.4 %all_to_all.11.in_ref = bf16[32,128,512]{2,1,0:T(8,128)(2,1)S(1)} all-to-all(bf16[32,128,512]{2,1,0:T(8,128)(2,1)S(1)} %mix.1), channel_id=1, replica_groups=mesh['grp'=2,'mom'=16] {'grp','mom'}, dimensions={0} | all-to-all | bytes 8388608 | tf_op jit(solution)/shard_map/all_to_all | solution.py:181
  207.3 2.4 %unpack.1 = (bf16[2,1,4,256,512]{4,3,2,1,0:T(8,128)(2,1)}, bf16[2,1,4,256,512]{4,3,2,1,0:T(8,128)(2,1)}) custom-call(bf16[32,128,512]{2,1,0:T(8,128)(2,1)S(1)} %all_to_all.11.in_ref), custom_call_target="tpu_custom_call" | custom-call | tf_op jit(solution)/shard_map/unpack/pallas_call | solution.py:155
Async XLA Ops:
  1.3 0.7 copy-start.2
  2.0 0.7 copy-start.3
  2.6 0.7 copy-start.4
  3.3 2.2 %copy-start = (bf16[2,1,4,256,512]{4,3,2,1,0:T(8,128)(2,1)S(1)}, bf16[2,1,4,256,512]{4,3,2,1,0:T(8,128)(2,1)}, u32[]{:S(2)}) copy-start(bf16[2,1,4,256,512]{4,3,2,1,0:T(8,128)(2,1)} %lesser_ref.1) | copy-start | bytes 6291460
  3.3 2.2 %copy-start.1 = (bf16[2,1,4,256,512]{4,3,2,1,0:T(8,128)(2,1)S(1)}, bf16[2,1,4,256,512]{4,3,2,1,0:T(8,128)(2,1)}, u32[]{:S(2)}) copy-start(bf16[2,1,4,256,512]{4,3,2,1,0:T(8,128)(2,1)} %greater_ref.1) | copy-start | bytes 6291460

commit v8 on v7

--- a/solution.py
+++ b/solution.py
@@ -12,7 +12,7 @@
 TILE = 16
 VMEM_BYTES = 32 * 1024 * 1024
 APART = 1 << 16
-AXES = ("grp", "mom")
+AXES = ("grp", "near", "half")
 
 
 def turned(states, rows, back):
@@ -73,8 +73,7 @@
     states = energies * momenta
     regions, modes = coupling_ref.shape[:2]
     size = out_ref.shape[0]
-    place = lax.axis_index("grp") * shares + lax.axis_index("mom")
-    greater = lax.div(place, jnp.int32(groups * shares // 2)).astype(jnp.float32)
+    greater = lax.axis_index("grp").astype(jnp.float32)
     chosen = jnp.zeros(coupling_ref.shape[1:], jnp.float32)
     for region in range(regions):
         chosen = jnp.where(region_ref[...] == region, coupling_ref[region], chosen)
@@ -85,7 +84,9 @@
         return row * APART + (device >> (shares.bit_length() - 1)) * energies + energy
 
     down = lax.broadcasted_iota(jnp.int32, (size, points), 0)
-    momentum = ((down >> (TILE.bit_length() - 1)) & (shares - 1)) * momenta + (down & (momenta - 1))
+    share = (down >> (TILE.bit_length() - 1)) & (shares - 1)
+    share = (share & 1) * (shares // 2) + (share >> 1)
+    momentum = share * momenta + (down & (momenta - 1))
     pick = momentum == lax.broadcasted_iota(jnp.int32, (size, points), 1)
     pick = jnp.where(pick, 1.0, 0.0).astype(jnp.bfloat16)
     apart = energy_code(lax.broadcasted_iota(jnp.int32, (size, 1), 0)) - energy_code(
@@ -274,10 +275,10 @@
     return (jnp.concatenate([real_part, imag_part], axis=-1) * (1.0 / points)).astype(jnp.bfloat16)
 
 
-def by_groups(lesser, greater, coupling, occupation, shift, region_map):
+def by_groups(lesser, greater, coupling, occupation, shift, region_map, momentum):
     stacked = jnp.stack([lesser, greater])
     widened = with_halo(stacked, (("grp", 1),), SMAX)
-    regrouped = lax.all_to_all(widened, "mom", split_axis=4, concat_axis=3, tiled=True)
+    regrouped = lax.all_to_all(widened, momentum, split_axis=4, concat_axis=3, tiled=True)
     points = regrouped.shape[3]
     basis = dft_basis(points)
     basis_low = basis.astype(jnp.bfloat16)
@@ -287,41 +288,37 @@
         hat_real, hat_imag, spec_real, spec_imag, occupation, shift, lesser.shape[0]
     )
     result = inverse(sigma_real, sigma_imag, basis_low)
-    returned = lax.all_to_all(result, "mom", split_axis=3, concat_axis=4, tiled=True)
+    returned = lax.all_to_all(result, momentum, split_axis=3, concat_axis=4, tiled=True)
     return (returned[0], returned[1])
 
 
-def on_device(groups, shares, lesser, greater, coupling, occupation, shift, region_map):
-    energies, blocks, momenta, height, columns = lesser.shape
-    devices = groups * shares
-    states = energies * momenta
-    whole_tiles = (
-        blocks == 1
-        and devices >= 4
-        and devices & (devices - 1) == 0
-        and height % (TILE * (devices // 2)) == 0
-        and TILE % states == 0
+def whole_tiles(shape, groups, shares):
+    energies, blocks, momenta, height, columns = shape
+    return (
+        groups == 2
+        and shares & (shares - 1) == 0
+        and blocks == 1
+        and height == TILE * shares
+        and TILE % (energies * momenta) == 0
         and columns % 128 == 0
     )
-    if whole_tiles:
-        return by_rows(
-            lesser, greater, coupling, occupation, shift, region_map, groups, shares
-        )
-    return by_groups(lesser, greater, coupling, occupation, shift, region_map)
 
 
 def solution(mesh):
+    groups, shares = mesh.shape["grp"], mesh.shape["mom"]
+    momentum = ("half", "near")
+    split = jax.sharding.Mesh(mesh.devices.reshape(groups, 2, shares // 2), ("grp",) + momentum)
+
+    def on_device(lesser, *rest):
+        if whole_tiles(lesser.shape, groups, shares):
+            return by_rows(lesser, *rest, groups, shares)
+        return by_groups(lesser, *rest, momentum)
+
+    slab = P("grp", None, momentum, None, None)
     return jax.shard_map(
-        functools.partial(on_device, mesh.shape["grp"], mesh.shape["mom"]),
-        mesh=mesh,
-        in_specs=(
-            P("grp", None, "mom", None, None),
-            P("grp", None, "mom", None, None),
-            P(),
-            P(),
-            P(),
-            P(),
-        ),
-        out_specs=(P("grp", None, "mom", None, None), P("grp", None, "mom", None, None)),
+        on_device,
+        mesh=split,
+        in_specs=(slab, slab, P(), P(), P(), P()),
+        out_specs=(slab, slab),
         check_vma=False,
     )

time: 210 us -> 210 us (level)
  no operation moved by 1% of the time
where the time goes in v8:
time: 210 us; the launch traced here: 209 us
  blocking collectives  197 us (94%)
  Pallas kernels  8.19 us (4%)
    all_to_all x2, blocking collectives, exchange(): return lax.all_to_all(array, AXES, split_axis=0, concat_axis=0, tiled=True)  197 us

profile of v8, /device:TPU:0, one launch (start us, length us, event | category | flops | bytes accessed | tf_op | source)
XLA Modules:
  0.0 208.6 jit_solution(7362344251595402569)
XLA Ops:
  1.3 0.0 copy-start.2
  1.3 0.7 copy-done.2
  2.0 0.0 copy-start.3
  2.0 0.7 copy-done.3
  2.6 0.0 copy-start.4
  2.6 0.7 copy-done.4
  3.3 0.0 copy-start
  3.3 0.0 copy-start.1
  3.3 2.2 %build.1.matrix_ref = bf16[512,512]{1,0:T(8,128)(2,1)S(1)} custom-call(s32[1,1]{1,0:T(1,128)} %bitcast.1.region_ref, s32[4]{0:T(128)S(1)} %copy-done.3, f32[4]{0:T(128)S(1)} %copy-done.4, f32[4,4,64]{2,1,0:T(4,128)S(1)} %copy-done.2), custom_call_target="tpu_custom_call" | custom-call | flops 6710886400 | bytes 20971520 | tf_op jit(solution)/shard_map/build/pallas_call | solution.py:127
  5.5 0.0 copy-done
  5.5 0.0 copy-done.1
  5.5 1.2 pack.1
  6.8 99.8 %all_to_all.10.in_ref = bf16[32,128,512]{2,1,0:T(8,128)(2,1)S(1)} all-to-all(bf16[32,128,512]{2,1,0:T(8,128)(2,1)S(1)} %pack.1), channel_id=1, replica_groups=mesh['grp'=2,'half'=2,'near'=8] {'grp','near','half'}, dimensions={0} | all-to-all | bytes 8388608 | tf_op jit(solution)/shard_map/all_to_all | solution.py:182
  106.6 2.3 %mix.1 = bf16[32,128,512]{2,1,0:T(8,128)(2,1)S(1)} custom-call(bf16[512,512]{1,0:T(8,128)(2,1)S(1)} %build.1.matrix_ref, bf16[32,128,512]{2,1,0:T(8,128)(2,1)S(1)} %all_to_all.10.in_ref), custom_call_target="tpu_custom_call" | custom-call | tf_op jit(solution)/shard_map/mix/pallas_call | solution.py:171
  108.9 97.2 %all_to_all.11.in_ref = bf16[32,128,512]{2,1,0:T(8,128)(2,1)S(1)} all-to-all(bf16[32,128,512]{2,1,0:T(8,128)(2,1)S(1)} %mix.1), channel_id=1, replica_groups=mesh['grp'=2,'half'=2,'near'=8] {'grp','near','half'}, dimensions={0} | all-to-all | bytes 8388608 | tf_op jit(solution)/shard_map/all_to_all | solution.py:182
  206.2 2.4 %unpack.1 = (bf16[2,1,4,256,512]{4,3,2,1,0:T(8,128)(2,1)}, bf16[2,1,4,256,512]{4,3,2,1,0:T(8,128)(2,1)}) custom-call(bf16[32,128,512]{2,1,0:T(8,128)(2,1)S(1)} %all_to_all.11.in_ref), custom_call_target="tpu_custom_call" | custom-call | tf_op jit(solution)/shard_map/unpack/pallas_call | solution.py:156
Async XLA Ops:
  1.3 0.7 copy-start.2
  2.0 0.7 copy-start.3
  2.6 0.7 copy-start.4
  3.3 2.2 %copy-start = (bf16[2,1,4,256,512]{4,3,2,1,0:T(8,128)(2,1)S(1)}, bf16[2,1,4,256,512]{4,3,2,1,0:T(8,128)(2,1)}, u32[]{:S(2)}) copy-start(bf16[2,1,4,256,512]{4,3,2,1,0:T(8,128)(2,1)} %lesser_ref.1) | copy-start | bytes 6291460
  3.3 2.2 %copy-start.1 = (bf16[2,1,4,256,512]{4,3,2,1,0:T(8,128)(2,1)S(1)}, bf16[2,1,4,256,512]{4,3,2,1,0:T(8,128)(2,1)}, u32[]{:S(2)}) copy-start(bf16[2,1,4,256,512]{4,3,2,1,0:T(8,128)(2,1)} %greater_ref.1) | copy-start | bytes 6291460

commit v9 on v7

--- a/solution.py
+++ b/solution.py
@@ -11,7 +11,6 @@
 SMAX = 2
 TILE = 16
 VMEM_BYTES = 32 * 1024 * 1024
-APART = 1 << 16
 AXES = ("grp", "mom")
 
 
@@ -66,74 +65,85 @@
             out_ref[side * pieces + piece] = moved.astype(out_ref.dtype)
 
 
-def build_kernel(
-    groups, shares, momenta, energies, region_ref, shift_ref, occupation_ref, coupling_ref, out_ref
-):
+def build_kernel(groups, shares, momenta, energies, regions, small_ref, out_ref):
     points = shares * momenta
     states = energies * momenta
-    regions, modes = coupling_ref.shape[:2]
-    size = out_ref.shape[0]
+    size, levels = out_ref.shape[0], groups * energies
+    modes = (small_ref.shape[0] - 3) // regions
+    occupation, shift, region = (
+        small_ref[at : at + 1, :] for at in range(regions * modes, regions * modes + 3)
+    )
     place = lax.axis_index("grp") * shares + lax.axis_index("mom")
     greater = lax.div(place, jnp.int32(groups * shares // 2)).astype(jnp.float32)
-    chosen = jnp.zeros(coupling_ref.shape[1:], jnp.float32)
-    for region in range(regions):
-        chosen = jnp.where(region_ref[...] == region, coupling_ref[region], chosen)
-
-    def energy_code(at):
-        device, row = at >> (TILE.bit_length() - 1), (at & (TILE - 1)) >> (states.bit_length() - 1)
-        energy = (at & (states - 1)) >> (momenta.bit_length() - 1)
-        return row * APART + (device >> (shares.bit_length() - 1)) * energies + energy
-
-    down = lax.broadcasted_iota(jnp.int32, (size, points), 0)
-    momentum = ((down >> (TILE.bit_length() - 1)) & (shares - 1)) * momenta + (down & (momenta - 1))
-    pick = momentum == lax.broadcasted_iota(jnp.int32, (size, points), 1)
-    pick = jnp.where(pick, 1.0, 0.0).astype(jnp.bfloat16)
-    apart = energy_code(lax.broadcasted_iota(jnp.int32, (size, 1), 0)) - energy_code(
-        lax.broadcasted_iota(jnp.int32, (1, size), 1)
-    )
-    total = jnp.zeros((size, size), jnp.float32)
+    chosen = jnp.zeros((modes, points), jnp.float32)
+    for at in range(regions):
+        here = region[:, 0:1] == float(at)
+        chosen = jnp.where(here, small_ref[at * modes : (at + 1) * modes, :], chosen)
+    circles = {}
     for step in range(-SMAX, SMAX + 1):
         if step == 0:
             continue
         row = jnp.zeros((1, points), jnp.float32)
         for mode in range(modes):
-            filling = occupation_ref[mode] + (greater if step > 0 else 1.0 - greater)
-            weight = jnp.where(shift_ref[mode] == abs(step), filling, 0.0)
+            filling = occupation[:, mode : mode + 1] + (greater if step > 0 else 1.0 - greater)
+            weight = jnp.where(shift[:, mode : mode + 1] == float(abs(step)), filling, 0.0)
             row = row + weight * chosen[mode : mode + 1, :]
         wide = jnp.broadcast_to(jnp.concatenate([row, row], axis=1), (points, 2 * points))
-        circle = pltpu.roll(wide, 0, 1, stride=1, stride_axis=0)[:, :points]
-        half = jnp.dot(
-            pick, circle.astype(jnp.bfloat16), preferred_element_type=jnp.float32
-        ).astype(jnp.bfloat16)
-        full = lax.dot_general(
-            pick, half, (((1,), (1,)), ((), ())), preferred_element_type=jnp.float32
-        )
-        total = jnp.where(apart == step, full, total)
-    out_ref[...] = total.astype(out_ref.dtype)
+        circles[step] = pltpu.roll(wide, 0, 1, stride=1, stride_axis=0)[:, :points]
+    nothing = jnp.zeros((points, points), jnp.float32)
+    plain = jnp.concatenate(
+        [
+            jnp.concatenate([circles.get(out - level, nothing) for out in range(levels)], axis=1)
+            for level in range(levels)
+        ],
+        axis=0,
+    ).astype(jnp.bfloat16)
+
+    def parts(at):
+        device, row = at >> (TILE.bit_length() - 1), (at & (TILE - 1)) >> (states.bit_length() - 1)
+        energy = (at & (states - 1)) >> (momenta.bit_length() - 1)
+        energy = (device >> (shares.bit_length() - 1)) * energies + energy
+        return row, (energy * shares + (device & (shares - 1))) * momenta + (at & (momenta - 1))
+
+    state = parts(lax.broadcasted_iota(jnp.int32, (size, 1), 0))[1]
+    pick = state == lax.broadcasted_iota(jnp.int32, (size, levels * points), 1)
+    pick = jnp.where(pick, 1.0, 0.0).astype(jnp.bfloat16)
+    half = jnp.dot(pick, plain, preferred_element_type=jnp.float32).astype(jnp.bfloat16)
+    full = lax.dot_general(
+        pick, half, (((1,), (1,)), ((), ())), preferred_element_type=jnp.float32
+    )
+    same = parts(lax.broadcasted_iota(jnp.int32, (size, 1), 0))[0] == parts(
+        lax.broadcasted_iota(jnp.int32, (1, size), 1)
+    )[0]
+    out_ref[...] = jnp.where(same, full, 0.0).astype(out_ref.dtype)
 
 
 def params():
     return pltpu.CompilerParams(vmem_limit_bytes=VMEM_BYTES)
 
 
-SCALARS = pl.BlockSpec(memory_space=pltpu.SMEM)
 VECTORS = pl.BlockSpec(memory_space=pltpu.VMEM)
 SLABS = pl.BlockSpec(memory_space=pl.ANY)
 
 
 def build(coupling, occupation, shift, region_map, groups, shares, momenta, energies):
     size, points = groups * shares * TILE, shares * momenta
+    scalars = [
+        jnp.pad(part[None, :], ((0, 0), (0, points - part.shape[0]))).astype(jnp.float32)
+        for part in (occupation, shift, region_map)
+    ]
+    small = jnp.concatenate([coupling.reshape(-1, points)] + scalars, axis=0)
     return pl.pallas_call(
-        functools.partial(build_kernel, groups, shares, momenta, energies),
+        functools.partial(build_kernel, groups, shares, momenta, energies, coupling.shape[0]),
         out_shape=jax.ShapeDtypeStruct((size, size), jnp.bfloat16),
-        in_specs=[VECTORS, SCALARS, SCALARS, VECTORS],
+        in_specs=[VECTORS],
         out_specs=VECTORS,
         compiler_params=params(),
         cost_estimate=pl.CostEstimate(
             flops=400 * size * size * points, bytes_accessed=80 * size * size, transcendentals=0
         ),
         name="build",
-    )(region_map.reshape(1, 1), shift, occupation, coupling)
+    )(small)
 
 
 def pack(matrix, lesser, greater, pieces, rows):

time: 210 us -> 209 us (level)
  no operation moved by 1% of the time
where the time goes in v9:
time: 209 us
  blocking collectives  198 us (95%)
  Pallas kernels  6.85 us (3%)
    all_to_all x2, blocking collectives, exchange(): return lax.all_to_all(array, AXES, split_axis=0, concat_axis=0, tiled=True)  198 us

profile of v9, /device:TPU:0, one launch (start us, length us, event | category | flops | bytes accessed | tf_op | source)
XLA Modules:
  0.0 209.2 jit_solution(5171923421941204793)
XLA Ops:
  1.3 0.7 pad_convert_fusion
  1.9 0.7 fusion.1.small_ref
  2.7 0.0 copy-start
  2.7 0.0 copy-start.1
  2.7 0.8 build.1.matrix_ref
  3.5 0.7 copy-done
  4.3 0.6 copy-done.1
  4.9 1.2 pack.1
  6.1 101.8 %all_to_all.10.in_ref = bf16[32,128,512]{2,1,0:T(8,128)(2,1)S(1)} all-to-all(bf16[32,128,512]{2,1,0:T(8,128)(2,1)S(1)} %pack.1), channel_id=1, replica_groups=mesh['grp'=2,'mom'=16] {'grp','mom'}, dimensions={0} | all-to-all | bytes 8388608 | tf_op jit(solution)/shard_map/all_to_all | solution.py:191
  107.9 2.3 %mix.1 = bf16[32,128,512]{2,1,0:T(8,128)(2,1)S(1)} custom-call(bf16[512,512]{1,0:T(8,128)(2,1)S(1)} %build.1.matrix_ref, bf16[32,128,512]{2,1,0:T(8,128)(2,1)S(1)} %all_to_all.10.in_ref), custom_call_target="tpu_custom_call" | custom-call | tf_op jit(solution)/shard_map/mix/pallas_call | solution.py:180
  110.3 96.4 %all_to_all.11.in_ref = bf16[32,128,512]{2,1,0:T(8,128)(2,1)S(1)} all-to-all(bf16[32,128,512]{2,1,0:T(8,128)(2,1)S(1)} %mix.1), channel_id=1, replica_groups=mesh['grp'=2,'mom'=16] {'grp','mom'}, dimensions={0} | all-to-all | bytes 8388608 | tf_op jit(solution)/shard_map/all_to_all | solution.py:191
  206.7 2.4 %unpack.1 = (bf16[2,1,4,256,512]{4,3,2,1,0:T(8,128)(2,1)}, bf16[2,1,4,256,512]{4,3,2,1,0:T(8,128)(2,1)}) custom-call(bf16[32,128,512]{2,1,0:T(8,128)(2,1)S(1)} %all_to_all.11.in_ref), custom_call_target="tpu_custom_call" | custom-call | tf_op jit(solution)/shard_map/unpack/pallas_call | solution.py:165
Async XLA Ops:
  2.7 1.6 copy-start
  2.7 2.2 %copy-start.1 = (bf16[2,1,4,256,512]{4,3,2,1,0:T(8,128)(2,1)S(1)}, bf16[2,1,4,256,512]{4,3,2,1,0:T(8,128)(2,1)}, u32[]{:S(2)}) copy-start(bf16[2,1,4,256,512]{4,3,2,1,0:T(8,128)(2,1)} %greater_ref.1) | copy-start | bytes 6291460

commit v10 on v9

--- a/solution.py
+++ b/solution.py
@@ -128,11 +128,11 @@
 
 def build(coupling, occupation, shift, region_map, groups, shares, momenta, energies):
     size, points = groups * shares * TILE, shares * momenta
-    scalars = [
-        jnp.pad(part[None, :], ((0, 0), (0, points - part.shape[0]))).astype(jnp.float32)
-        for part in (occupation, shift, region_map)
-    ]
-    small = jnp.concatenate([coupling.reshape(-1, points)] + scalars, axis=0)
+    rows = coupling.shape[0] * coupling.shape[1]
+    small = jnp.pad(coupling.reshape(rows, points), ((0, 3), (0, 0)))
+    for at, part in enumerate((occupation, shift, region_map)):
+        part = jnp.pad(part[None, :], ((rows + at, 2 - at), (0, points - part.shape[0])))
+        small = small + part.astype(jnp.float32)
     return pl.pallas_call(
         functools.partial(build_kernel, groups, shares, momenta, energies, coupling.shape[0]),
         out_shape=jax.ShapeDtypeStruct((size, size), jnp.bfloat16),

time: 209 us -> 209 us (level)
  no operation moved by 1% of the time
where the time goes in v10:
time: 209 us
  blocking collectives  198 us (95%)
  Pallas kernels  6.86 us (3%)
    all_to_all x2, blocking collectives, exchange(): return lax.all_to_all(array, AXES, split_axis=0, concat_axis=0, tiled=True)  198 us

profile of v10, /device:TPU:0, one launch (start us, length us, event | category | flops | bytes accessed | tf_op | source)
XLA Modules:
  0.0 208.5 jit_solution(2499175025668775103)
XLA Ops:
  1.3 0.7 convert_add_fusion.small_ref
  2.0 0.0 copy-start
  2.0 0.0 copy-start.1
  2.0 0.8 build.1.matrix_ref
  2.9 0.7 copy-done
  3.6 0.6 copy-done.1
  4.2 1.2 pack.1
  5.5 101.8 %all_to_all.10.in_ref = bf16[32,128,512]{2,1,0:T(8,128)(2,1)S(1)} all-to-all(bf16[32,128,512]{2,1,0:T(8,128)(2,1)S(1)} %pack.1), channel_id=1, replica_groups=mesh['grp'=2,'mom'=16] {'grp','mom'}, dimensions={0} | all-to-all | bytes 8388608 | tf_op jit(solution)/shard_map/all_to_all | solution.py:191
  107.3 2.3 %mix.1 = bf16[32,128,512]{2,1,0:T(8,128)(2,1)S(1)} custom-call(bf16[512,512]{1,0:T(8,128)(2,1)S(1)} %build.1.matrix_ref, bf16[32,128,512]{2,1,0:T(8,128)(2,1)S(1)} %all_to_all.10.in_ref), custom_call_target="tpu_custom_call" | custom-call | tf_op jit(solution)/shard_map/mix/pallas_call | solution.py:180
  109.6 96.4 %all_to_all.11.in_ref = bf16[32,128,512]{2,1,0:T(8,128)(2,1)S(1)} all-to-all(bf16[32,128,512]{2,1,0:T(8,128)(2,1)S(1)} %mix.1), channel_id=1, replica_groups=mesh['grp'=2,'mom'=16] {'grp','mom'}, dimensions={0} | all-to-all | bytes 8388608 | tf_op jit(solution)/shard_map/all_to_all | solution.py:191
  206.1 2.4 %unpack.1 = (bf16[2,1,4,256,512]{4,3,2,1,0:T(8,128)(2,1)}, bf16[2,1,4,256,512]{4,3,2,1,0:T(8,128)(2,1)}) custom-call(bf16[32,128,512]{2,1,0:T(8,128)(2,1)S(1)} %all_to_all.11.in_ref), custom_call_target="tpu_custom_call" | custom-call | tf_op jit(solution)/shard_map/unpack/pallas_call | solution.py:165
Async XLA Ops:
  2.0 1.6 copy-start
  2.0 2.2 %copy-start.1 = (bf16[2,1,4,256,512]{4,3,2,1,0:T(8,128)(2,1)S(1)}, bf16[2,1,4,256,512]{4,3,2,1,0:T(8,128)(2,1)}, u32[]{:S(2)}) copy-start(bf16[2,1,4,256,512]{4,3,2,1,0:T(8,128)(2,1)} %greater_ref.1) | copy-start | bytes 6291460

commit v11 on v10

--- a/solution.py
+++ b/solution.py
@@ -140,7 +140,7 @@
         out_specs=VECTORS,
         compiler_params=params(),
         cost_estimate=pl.CostEstimate(
-            flops=400 * size * size * points, bytes_accessed=80 * size * size, transcendentals=0
+            flops=110 * size * size * points, bytes_accessed=22 * size * size, transcendentals=0
         ),
         name="build",
     )(small)

time: 209 us -> 208 us (level)
  no operation moved by 1% of the time
where the time goes in v11:
time: 208 us
  blocking collectives  198 us (95%)
  Pallas kernels  6.85 us (3%)
    all_to_all x2, blocking collectives, exchange(): return lax.all_to_all(array, AXES, split_axis=0, concat_axis=0, tiled=True)  198 us

profile of v11, /device:TPU:0, one launch (start us, length us, event | category | flops | bytes accessed | tf_op | source)
XLA Modules:
  0.0 207.7 jit_solution(14362625506443836657)
XLA Ops:
  0.6 0.0 copy-start.1
  0.6 0.0 copy-start
  1.4 1.2 convert_add_fusion.small_ref
  2.6 0.8 build.1.matrix_ref
  3.4 0.0 copy-done.1
  3.5 0.0 copy-done
  3.5 1.2 pack.1
  4.7 101.8 %all_to_all.10.in_ref = bf16[32,128,512]{2,1,0:T(8,128)(2,1)S(1)} all-to-all(bf16[32,128,512]{2,1,0:T(8,128)(2,1)S(1)} %pack.1), channel_id=1, replica_groups=mesh['grp'=2,'mom'=16] {'grp','mom'}, dimensions={0} | all-to-all | bytes 8388608 | tf_op jit(solution)/shard_map/all_to_all | solution.py:191
  106.5 2.3 %mix.1 = bf16[32,128,512]{2,1,0:T(8,128)(2,1)S(1)} custom-call(bf16[512,512]{1,0:T(8,128)(2,1)S(1)} %build.1.matrix_ref, bf16[32,128,512]{2,1,0:T(8,128)(2,1)S(1)} %all_to_all.10.in_ref), custom_call_target="tpu_custom_call" | custom-call | tf_op jit(solution)/shard_map/mix/pallas_call | solution.py:180
  108.9 96.4 %all_to_all.11.in_ref = bf16[32,128,512]{2,1,0:T(8,128)(2,1)S(1)} all-to-all(bf16[32,128,512]{2,1,0:T(8,128)(2,1)S(1)} %mix.1), channel_id=1, replica_groups=mesh['grp'=2,'mom'=16] {'grp','mom'}, dimensions={0} | all-to-all | bytes 8388608 | tf_op jit(solution)/shard_map/all_to_all | solution.py:191
  205.3 2.4 %unpack.1 = (bf16[2,1,4,256,512]{4,3,2,1,0:T(8,128)(2,1)}, bf16[2,1,4,256,512]{4,3,2,1,0:T(8,128)(2,1)}) custom-call(bf16[32,128,512]{2,1,0:T(8,128)(2,1)S(1)} %all_to_all.11.in_ref), custom_call_target="tpu_custom_call" | custom-call | tf_op jit(solution)/shard_map/unpack/pallas_call | solution.py:165
Async XLA Ops:
  0.6 2.8 %copy-start.1 = (bf16[2,1,4,256,512]{4,3,2,1,0:T(8,128)(2,1)S(1)}, bf16[2,1,4,256,512]{4,3,2,1,0:T(8,128)(2,1)}, u32[]{:S(2)}) copy-start(bf16[2,1,4,256,512]{4,3,2,1,0:T(8,128)(2,1)} %greater_ref.1) | copy-start | bytes 6291460
  0.6 2.8 %copy-start = (bf16[2,1,4,256,512]{4,3,2,1,0:T(8,128)(2,1)S(1)}, bf16[2,1,4,256,512]{4,3,2,1,0:T(8,128)(2,1)}, u32[]{:S(2)}) copy-start(bf16[2,1,4,256,512]{4,3,2,1,0:T(8,128)(2,1)} %lesser_ref.1) | copy-start | bytes 6291460

commit v12 on v11

--- a/solution.py
+++ b/solution.py
@@ -27,11 +27,12 @@
 
 def mix_kernel(matrix_ref, in_ref, out_ref):
     devices, size, width = in_ref.shape
-    for start in range(0, size, TILE):
-        block = in_ref[:, start : start + TILE, :].reshape(devices * TILE, width)
+    states = matrix_ref.shape[0] // devices
+    for start in range(0, size, states):
+        block = in_ref[:, start : start + states, :].reshape(devices * states, width)
         mixed = jnp.dot(matrix_ref[...], block, preferred_element_type=jnp.float32)
-        out_ref[:, start : start + TILE, :] = mixed.astype(out_ref.dtype).reshape(
-            devices, TILE, width
+        out_ref[:, start : start + states, :] = mixed.astype(out_ref.dtype).reshape(
+            devices, states, width
         )
 
 
@@ -99,23 +100,17 @@
         axis=0,
     ).astype(jnp.bfloat16)
 
-    def parts(at):
-        device, row = at >> (TILE.bit_length() - 1), (at & (TILE - 1)) >> (states.bit_length() - 1)
-        energy = (at & (states - 1)) >> (momenta.bit_length() - 1)
-        energy = (device >> (shares.bit_length() - 1)) * energies + energy
-        return row, (energy * shares + (device & (shares - 1))) * momenta + (at & (momenta - 1))
-
-    state = parts(lax.broadcasted_iota(jnp.int32, (size, 1), 0))[1]
+    at = lax.broadcasted_iota(jnp.int32, (size, 1), 0)
+    device, energy = at >> (states.bit_length() - 1), (at & (states - 1)) >> (momenta.bit_length() - 1)
+    energy = (device >> (shares.bit_length() - 1)) * energies + energy
+    state = (energy * shares + (device & (shares - 1))) * momenta + (at & (momenta - 1))
     pick = state == lax.broadcasted_iota(jnp.int32, (size, levels * points), 1)
     pick = jnp.where(pick, 1.0, 0.0).astype(jnp.bfloat16)
     half = jnp.dot(pick, plain, preferred_element_type=jnp.float32).astype(jnp.bfloat16)
     full = lax.dot_general(
         pick, half, (((1,), (1,)), ((), ())), preferred_element_type=jnp.float32
     )
-    same = parts(lax.broadcasted_iota(jnp.int32, (size, 1), 0))[0] == parts(
-        lax.broadcasted_iota(jnp.int32, (1, size), 1)
-    )[0]
-    out_ref[...] = jnp.where(same, full, 0.0).astype(out_ref.dtype)
+    out_ref[...] = full.astype(out_ref.dtype)
 
 
 def params():
@@ -127,7 +122,7 @@
 
 
 def build(coupling, occupation, shift, region_map, groups, shares, momenta, energies):
-    size, points = groups * shares * TILE, shares * momenta
+    size, points = groups * shares * energies * momenta, shares * momenta
     rows = coupling.shape[0] * coupling.shape[1]
     small = jnp.pad(coupling.reshape(rows, points), ((0, 3), (0, 0)))
     for at, part in enumerate((occupation, shift, region_map)):
@@ -140,7 +135,7 @@
         out_specs=VECTORS,
         compiler_params=params(),
         cost_estimate=pl.CostEstimate(
-            flops=110 * size * size * points, bytes_accessed=22 * size * size, transcendentals=0
+            flops=440 * size * size * points, bytes_accessed=88 * size * size, transcendentals=0
         ),
         name="build",
     )(small)

time: 208 us -> 207 us (level)
  no operation moved by 1% of the time
where the time goes in v12:
time: 207 us
  blocking collectives  198 us (96%)
  Pallas kernels  5.63 us (3%)
    all_to_all x2, blocking collectives, exchange(): return lax.all_to_all(array, AXES, split_axis=0, concat_axis=0, tiled=True)  198 us

profile of v12, /device:TPU:0, one launch (start us, length us, event | category | flops | bytes accessed | tf_op | source)
XLA Modules:
  0.0 206.5 jit_solution(224490454868024069)
XLA Ops:
  0.6 0.0 copy-start.1
  0.6 0.0 copy-start
  1.4 1.2 convert_add_fusion.small_ref
  2.6 0.7 build.1.matrix_ref
  3.3 0.0 copy-done.1
  3.3 0.0 copy-done
  3.3 1.2 pack.1
  4.6 101.8 %all_to_all.10.in_ref = bf16[32,128,512]{2,1,0:T(8,128)(2,1)S(1)} all-to-all(bf16[32,128,512]{2,1,0:T(8,128)(2,1)S(1)} %pack.1), channel_id=1, replica_groups=mesh['grp'=2,'mom'=16] {'grp','mom'}, dimensions={0} | all-to-all | bytes 8388608 | tf_op jit(solution)/shard_map/all_to_all | solution.py:186
  106.4 1.3 mix.1
  107.6 96.4 %all_to_all.11.in_ref = bf16[32,128,512]{2,1,0:T(8,128)(2,1)S(1)} all-to-all(bf16[32,128,512]{2,1,0:T(8,128)(2,1)S(1)} %mix.1), channel_id=1, replica_groups=mesh['grp'=2,'mom'=16] {'grp','mom'}, dimensions={0} | all-to-all | bytes 8388608 | tf_op jit(solution)/shard_map/all_to_all | solution.py:186
  204.1 2.4 %unpack.1 = (bf16[2,1,4,256,512]{4,3,2,1,0:T(8,128)(2,1)}, bf16[2,1,4,256,512]{4,3,2,1,0:T(8,128)(2,1)}) custom-call(bf16[32,128,512]{2,1,0:T(8,128)(2,1)S(1)} %all_to_all.11.in_ref), custom_call_target="tpu_custom_call" | custom-call | tf_op jit(solution)/shard_map/unpack/pallas_call | solution.py:160
Async XLA Ops:
  0.6 2.7 %copy-start.1 = (bf16[2,1,4,256,512]{4,3,2,1,0:T(8,128)(2,1)S(1)}, bf16[2,1,4,256,512]{4,3,2,1,0:T(8,128)(2,1)}, u32[]{:S(2)}) copy-start(bf16[2,1,4,256,512]{4,3,2,1,0:T(8,128)(2,1)} %greater_ref.1) | copy-start | bytes 6291460
  0.6 2.7 %copy-start = (bf16[2,1,4,256,512]{4,3,2,1,0:T(8,128)(2,1)S(1)}, bf16[2,1,4,256,512]{4,3,2,1,0:T(8,128)(2,1)}, u32[]{:S(2)}) copy-start(bf16[2,1,4,256,512]{4,3,2,1,0:T(8,128)(2,1)} %lesser_ref.1) | copy-start | bytes 6291460

commit v13 on v12

--- a/solution.py
+++ b/solution.py
@@ -37,17 +37,23 @@
 
 
 def unpack_kernel(in_ref, lesser_ref, greater_ref, held, sent):
-    pieces, rows = held.shape[1], held.shape[4]
+    pieces, steps = in_ref.shape[0] // 2, sent.shape[1]
+    rows = held.shape[3] // pieces
+    batch = pieces // steps
     perm = turned(in_ref.shape[1] // rows, rows, True)
     copies = []
-    for side, ref in enumerate((lesser_ref, greater_ref)):
-        for piece in range(pieces):
-            moved = jnp.dot(perm, in_ref[side * pieces + piece], preferred_element_type=jnp.float32)
-            held[side, piece] = moved.astype(held.dtype).reshape(held.shape[2:])
+    for step in range(steps):
+        span = slice(step * batch * rows, (step + 1) * batch * rows)
+        for side, ref in enumerate((lesser_ref, greater_ref)):
+            for piece in range(step * batch, (step + 1) * batch):
+                moved = jnp.dot(
+                    perm, in_ref[side * pieces + piece], preferred_element_type=jnp.float32
+                )
+                held[side, :, :, piece * rows : (piece + 1) * rows, :] = moved.astype(
+                    held.dtype
+                ).reshape(held.shape[1:3] + (rows, held.shape[4]))
             copy = pltpu.make_async_copy(
-                held.at[side, piece],
-                ref.at[:, 0, :, piece * rows : (piece + 1) * rows, :],
-                sent.at[side, piece],
+                held.at[side, :, :, span, :], ref.at[:, 0, :, span, :], sent.at[side, step]
             )
             copy.start()
             copies.append(copy)
@@ -163,8 +169,8 @@
         in_specs=[VECTORS],
         out_specs=(SLABS, SLABS),
         scratch_shapes=[
-            pltpu.VMEM((2, pieces, energies, momenta, rows, columns), packed.dtype),
-            pltpu.SemaphoreType.DMA((2, pieces)),
+            pltpu.VMEM((2, energies, momenta, pieces * rows, columns), packed.dtype),
+            pltpu.SemaphoreType.DMA((2, math.gcd(pieces, 4))),
         ],
         compiler_params=params(),
         name="unpack",

time: 207 us -> 207 us (level)
  no operation moved by 1% of the time
where the time goes in v13:
time: 207 us; the launch traced here: 206 us
  blocking collectives  198 us (96%)
  Pallas kernels  5.54 us (3%)
    all_to_all x2, blocking collectives, exchange(): return lax.all_to_all(array, AXES, split_axis=0, concat_axis=0, tiled=True)  198 us

profile of v13, /device:TPU:0, one launch (start us, length us, event | category | flops | bytes accessed | tf_op | source)
XLA Modules:
  0.0 206.4 jit_solution(3680892130478880042)
XLA Ops:
  0.6 0.0 copy-start.1
  0.6 0.0 copy-start
  1.4 1.2 convert_add_fusion.small_ref
  2.6 0.7 build.1.matrix_ref
  3.3 0.0 copy-done.1
  3.3 0.0 copy-done
  3.3 1.2 pack.1
  4.6 101.8 %all_to_all.10.in_ref = bf16[32,128,512]{2,1,0:T(8,128)(2,1)S(1)} all-to-all(bf16[32,128,512]{2,1,0:T(8,128)(2,1)S(1)} %pack.1), channel_id=1, replica_groups=mesh['grp'=2,'mom'=16] {'grp','mom'}, dimensions={0} | all-to-all | bytes 8388608 | tf_op jit(solution)/shard_map/all_to_all | solution.py:192
  106.4 1.3 mix.1
  107.6 96.4 %all_to_all.11.in_ref = bf16[32,128,512]{2,1,0:T(8,128)(2,1)S(1)} all-to-all(bf16[32,128,512]{2,1,0:T(8,128)(2,1)S(1)} %mix.1), channel_id=1, replica_groups=mesh['grp'=2,'mom'=16] {'grp','mom'}, dimensions={0} | all-to-all | bytes 8388608 | tf_op jit(solution)/shard_map/all_to_all | solution.py:192
  204.1 2.4 %unpack.1 = (bf16[2,1,4,256,512]{4,3,2,1,0:T(8,128)(2,1)}, bf16[2,1,4,256,512]{4,3,2,1,0:T(8,128)(2,1)}) custom-call(bf16[32,128,512]{2,1,0:T(8,128)(2,1)S(1)} %all_to_all.11.in_ref), custom_call_target="tpu_custom_call" | custom-call | tf_op jit(solution)/shard_map/unpack/pallas_call | solution.py:166
Async XLA Ops:
  0.6 2.7 %copy-start.1 = (bf16[2,1,4,256,512]{4,3,2,1,0:T(8,128)(2,1)S(1)}, bf16[2,1,4,256,512]{4,3,2,1,0:T(8,128)(2,1)}, u32[]{:S(2)}) copy-start(bf16[2,1,4,256,512]{4,3,2,1,0:T(8,128)(2,1)} %greater_ref.1) | copy-start | bytes 6291460
  0.6 2.7 %copy-start = (bf16[2,1,4,256,512]{4,3,2,1,0:T(8,128)(2,1)S(1)}, bf16[2,1,4,256,512]{4,3,2,1,0:T(8,128)(2,1)}, u32[]{:S(2)}) copy-start(bf16[2,1,4,256,512]{4,3,2,1,0:T(8,128)(2,1)} %lesser_ref.1) | copy-start | bytes 6291460

commit v14 on v13

--- a/solution.py
+++ b/solution.py
@@ -14,14 +14,15 @@
 AXES = ("grp", "mom")
 
 
-def turned(states, rows, back):
-    size = states * rows
-    down = lax.broadcasted_iota(jnp.int32, (size, size), 0)
-    across = lax.broadcasted_iota(jnp.int32, (size, size), 1)
+def turned(states, rows, pairs, back):
+    piece = states * rows
+    down = lax.broadcasted_iota(jnp.int32, (pairs * piece, pairs * piece), 0)
+    across = lax.broadcasted_iota(jnp.int32, (pairs * piece, pairs * piece), 1)
     if back:
         down, across = across, down
     bits = states.bit_length() - 1
-    there = (down & (states - 1)) * rows + (down >> bits) == across
+    inside = down & (piece - 1)
+    there = (inside & (states - 1)) * rows + (inside >> bits) + (down - inside) == across
     return jnp.where(there, 1.0, 0.0).astype(jnp.bfloat16)
 
 
@@ -40,18 +41,21 @@
     pieces, steps = in_ref.shape[0] // 2, sent.shape[1]
     rows = held.shape[3] // pieces
     batch = pieces // steps
-    perm = turned(in_ref.shape[1] // rows, rows, True)
+    perm = turned(in_ref.shape[1] // rows, rows, 2, True)
+    size, width = in_ref.shape[1:]
     copies = []
     for step in range(steps):
         span = slice(step * batch * rows, (step + 1) * batch * rows)
         for side, ref in enumerate((lesser_ref, greater_ref)):
-            for piece in range(step * batch, (step + 1) * batch):
-                moved = jnp.dot(
-                    perm, in_ref[side * pieces + piece], preferred_element_type=jnp.float32
-                )
-                held[side, :, :, piece * rows : (piece + 1) * rows, :] = moved.astype(
-                    held.dtype
-                ).reshape(held.shape[1:3] + (rows, held.shape[4]))
+            for piece in range(step * batch, (step + 1) * batch, 2):
+                at = side * pieces + piece
+                pair = in_ref[at : at + 2].reshape(2 * size, width)
+                moved = jnp.dot(perm, pair, preferred_element_type=jnp.float32).astype(held.dtype)
+                for turn in range(2):
+                    begin = (piece + turn) * rows
+                    held[side, :, :, begin : begin + rows, :] = moved[
+                        turn * size : (turn + 1) * size
+                    ].reshape(held.shape[1:3] + (rows, width))
             copy = pltpu.make_async_copy(
                 held.at[side, :, :, span, :], ref.at[:, 0, :, span, :], sent.at[side, step]
             )
@@ -64,12 +68,18 @@
 def pack_kernel(matrix_ref, lesser_ref, greater_ref, out_ref):
     pieces, (size, width) = out_ref.shape[0] // 2, out_ref.shape[1:]
     rows = lesser_ref.shape[3] // pieces
-    perm = turned(size // rows, rows, False)
+    perm = turned(size // rows, rows, 2, False)
     for side, ref in enumerate((lesser_ref, greater_ref)):
-        for piece in range(pieces):
-            block = ref[:, :, :, piece * rows : (piece + 1) * rows, :].reshape(size, width)
-            moved = jnp.dot(perm, block, preferred_element_type=jnp.float32)
-            out_ref[side * pieces + piece] = moved.astype(out_ref.dtype)
+        for piece in range(0, pieces, 2):
+            pair = [
+                ref[:, :, :, at * rows : (at + 1) * rows, :].reshape(size, width)
+                for at in (piece, piece + 1)
+            ]
+            moved = jnp.dot(
+                perm, jnp.concatenate(pair, axis=0), preferred_element_type=jnp.float32
+            )
+            at = side * pieces + piece
+            out_ref[at : at + 2] = moved.astype(out_ref.dtype).reshape(2, size, width)
 
 
 def build_kernel(groups, shares, momenta, energies, regions, small_ref, out_ref):
@@ -308,8 +318,9 @@
     states = energies * momenta
     whole_tiles = (
         blocks == 1
-        and devices >= 4
+        and devices >= 16
         and devices & (devices - 1) == 0
+        and height & (height - 1) == 0
         and height % (TILE * (devices // 2)) == 0
         and TILE % states == 0
         and columns % 128 == 0

time: 207 us -> 207 us (level)
  no operation moved by 1% of the time
where the time goes in v14:
time: 207 us; the launch traced here: 206 us
  blocking collectives  198 us (96%)
  Pallas kernels  5.58 us (3%)
    all_to_all x2, blocking collectives, exchange(): return lax.all_to_all(array, AXES, split_axis=0, concat_axis=0, tiled=True)  198 us

profile of v14, /device:TPU:0, one launch (start us, length us, event | category | flops | bytes accessed | tf_op | source)
XLA Modules:
  0.0 206.5 jit_solution(15290253516507467224)
XLA Ops:
  0.6 0.0 copy-start.1
  0.6 0.0 copy-start
  1.4 1.2 convert_add_fusion.small_ref
  2.6 0.7 build.1.matrix_ref
  3.3 0.0 copy-done.1
  3.3 0.0 copy-done
  3.3 1.3 pack.1
  4.6 101.8 %all_to_all.10.in_ref = bf16[32,128,512]{2,1,0:T(8,128)(2,1)S(1)} all-to-all(bf16[32,128,512]{2,1,0:T(8,128)(2,1)S(1)} %pack.1), channel_id=1, replica_groups=mesh['grp'=2,'mom'=16] {'grp','mom'}, dimensions={0} | all-to-all | bytes 8388608 | tf_op jit(solution)/shard_map/all_to_all | solution.py:202
  106.4 1.3 mix.1
  107.6 96.4 %all_to_all.11.in_ref = bf16[32,128,512]{2,1,0:T(8,128)(2,1)S(1)} all-to-all(bf16[32,128,512]{2,1,0:T(8,128)(2,1)S(1)} %mix.1), channel_id=1, replica_groups=mesh['grp'=2,'mom'=16] {'grp','mom'}, dimensions={0} | all-to-all | bytes 8388608 | tf_op jit(solution)/shard_map/all_to_all | solution.py:202
  204.1 2.4 %unpack.1 = (bf16[2,1,4,256,512]{4,3,2,1,0:T(8,128)(2,1)}, bf16[2,1,4,256,512]{4,3,2,1,0:T(8,128)(2,1)}) custom-call(bf16[32,128,512]{2,1,0:T(8,128)(2,1)S(1)} %all_to_all.11.in_ref), custom_call_target="tpu_custom_call" | custom-call | tf_op jit(solution)/shard_map/unpack/pallas_call | solution.py:176
Async XLA Ops:
  0.6 2.7 %copy-start.1 = (bf16[2,1,4,256,512]{4,3,2,1,0:T(8,128)(2,1)S(1)}, bf16[2,1,4,256,512]{4,3,2,1,0:T(8,128)(2,1)}, u32[]{:S(2)}) copy-start(bf16[2,1,4,256,512]{4,3,2,1,0:T(8,128)(2,1)} %greater_ref.1) | copy-start | bytes 6291460
  0.6 2.7 %copy-start = (bf16[2,1,4,256,512]{4,3,2,1,0:T(8,128)(2,1)S(1)}, bf16[2,1,4,256,512]{4,3,2,1,0:T(8,128)(2,1)}, u32[]{:S(2)}) copy-start(bf16[2,1,4,256,512]{4,3,2,1,0:T(8,128)(2,1)} %lesser_ref.1) | copy-start | bytes 6291460

commit v15 on v13

--- a/solution.py
+++ b/solution.py
@@ -55,7 +55,7 @@
             copy = pltpu.make_async_copy(
                 held.at[side, :, :, span, :], ref.at[:, 0, :, span, :], sent.at[side, step]
             )
-            copy.start()
+            copy.start(priority=side)
             copies.append(copy)
     for copy in copies:
         copy.wait()

time: 207 us -> 207 us (level)
  no operation moved by 1% of the time
where the time goes in v15:
time: 207 us; the launch traced here: 206 us
  blocking collectives  198 us (96%)
  Pallas kernels  5.54 us (3%)
    all_to_all x2, blocking collectives, exchange(): return lax.all_to_all(array, AXES, split_axis=0, concat_axis=0, tiled=True)  198 us

profile of v15, /device:TPU:0, one launch (start us, length us, event | category | flops | bytes accessed | tf_op | source)
XLA Modules:
  0.0 206.4 jit_solution(11903602453302562182)
XLA Ops:
  0.6 0.0 copy-start.1
  0.6 0.0 copy-start
  1.4 1.2 convert_add_fusion.small_ref
  2.6 0.7 build.1.matrix_ref
  3.3 0.0 copy-done.1
  3.3 0.0 copy-done
  3.3 1.2 pack.1
  4.6 101.8 %all_to_all.10.in_ref = bf16[32,128,512]{2,1,0:T(8,128)(2,1)S(1)} all-to-all(bf16[32,128,512]{2,1,0:T(8,128)(2,1)S(1)} %pack.1), channel_id=1, replica_groups=mesh['grp'=2,'mom'=16] {'grp','mom'}, dimensions={0} | all-to-all | bytes 8388608 | tf_op jit(solution)/shard_map/all_to_all | solution.py:192
  106.4 1.3 mix.1
  107.6 96.4 %all_to_all.11.in_ref = bf16[32,128,512]{2,1,0:T(8,128)(2,1)S(1)} all-to-all(bf16[32,128,512]{2,1,0:T(8,128)(2,1)S(1)} %mix.1), channel_id=1, replica_groups=mesh['grp'=2,'mom'=16] {'grp','mom'}, dimensions={0} | all-to-all | bytes 8388608 | tf_op jit(solution)/shard_map/all_to_all | solution.py:192
  204.1 2.4 %unpack.1 = (bf16[2,1,4,256,512]{4,3,2,1,0:T(8,128)(2,1)}, bf16[2,1,4,256,512]{4,3,2,1,0:T(8,128)(2,1)}) custom-call(bf16[32,128,512]{2,1,0:T(8,128)(2,1)S(1)} %all_to_all.11.in_ref), custom_call_target="tpu_custom_call" | custom-call | tf_op jit(solution)/shard_map/unpack/pallas_call | solution.py:166
Async XLA Ops:
  0.6 2.7 %copy-start.1 = (bf16[2,1,4,256,512]{4,3,2,1,0:T(8,128)(2,1)S(1)}, bf16[2,1,4,256,512]{4,3,2,1,0:T(8,128)(2,1)}, u32[]{:S(2)}) copy-start(bf16[2,1,4,256,512]{4,3,2,1,0:T(8,128)(2,1)} %greater_ref.1) | copy-start | bytes 6291460
  0.6 2.7 %copy-start = (bf16[2,1,4,256,512]{4,3,2,1,0:T(8,128)(2,1)S(1)}, bf16[2,1,4,256,512]{4,3,2,1,0:T(8,128)(2,1)}, u32[]{:S(2)}) copy-start(bf16[2,1,4,256,512]{4,3,2,1,0:T(8,128)(2,1)} %lesser_ref.1) | copy-start | bytes 6291460

commit v16 on v15

--- a/solution.py
+++ b/solution.py
@@ -28,12 +28,16 @@
 def mix_kernel(matrix_ref, in_ref, out_ref):
     devices, size, width = in_ref.shape
     states = matrix_ref.shape[0] // devices
-    for start in range(0, size, states):
-        block = in_ref[:, start : start + states, :].reshape(devices * states, width)
-        mixed = jnp.dot(matrix_ref[...], block, preferred_element_type=jnp.float32)
-        out_ref[:, start : start + states, :] = mixed.astype(out_ref.dtype).reshape(
-            devices, states, width
-        )
+    beside = math.gcd(size // states, 4)
+    for first in range(0, size, beside * states):
+        starts = range(first, first + beside * states, states)
+        rows = [in_ref[:, at : at + states, :].reshape(devices * states, width) for at in starts]
+        mixed = jnp.dot(
+            matrix_ref[...], jnp.concatenate(rows, axis=1), preferred_element_type=jnp.float32
+        ).astype(out_ref.dtype)
+        for turn, at in enumerate(starts):
+            row = mixed[:, turn * width : (turn + 1) * width]
+            out_ref[:, at : at + states, :] = row.reshape(devices, states, width)
 
 
 def unpack_kernel(in_ref, lesser_ref, greater_ref, held, sent):

time: 207 us -> 207 us (level)
  no operation moved by 1% of the time
where the time goes in v16:
time: 207 us; the launch traced here: 206 us
  blocking collectives  198 us (96%)
  Pallas kernels  5.54 us (3%)
    all_to_all x2, blocking collectives, exchange(): return lax.all_to_all(array, AXES, split_axis=0, concat_axis=0, tiled=True)  198 us

profile of v16, /device:TPU:0, one launch (start us, length us, event | category | flops | bytes accessed | tf_op | source)
XLA Modules:
  0.0 206.4 jit_solution(9638638450463835953)
XLA Ops:
  0.6 0.0 copy-start.1
  0.6 0.0 copy-start
  1.4 1.2 convert_add_fusion.small_ref
  2.6 0.7 build.1.matrix_ref
  3.3 0.0 copy-done.1
  3.3 0.0 copy-done
  3.3 1.2 pack.1
  4.6 101.8 %all_to_all.10.in_ref = bf16[32,128,512]{2,1,0:T(8,128)(2,1)S(1)} all-to-all(bf16[32,128,512]{2,1,0:T(8,128)(2,1)S(1)} %pack.1), channel_id=1, replica_groups=mesh['grp'=2,'mom'=16] {'grp','mom'}, dimensions={0} | all-to-all | bytes 8388608 | tf_op jit(solution)/shard_map/all_to_all | solution.py:196
  106.4 1.3 mix.1
  107.6 96.4 %all_to_all.11.in_ref = bf16[32,128,512]{2,1,0:T(8,128)(2,1)S(1)} all-to-all(bf16[32,128,512]{2,1,0:T(8,128)(2,1)S(1)} %mix.1), channel_id=1, replica_groups=mesh['grp'=2,'mom'=16] {'grp','mom'}, dimensions={0} | all-to-all | bytes 8388608 | tf_op jit(solution)/shard_map/all_to_all | solution.py:196
  204.1 2.4 %unpack.1 = (bf16[2,1,4,256,512]{4,3,2,1,0:T(8,128)(2,1)}, bf16[2,1,4,256,512]{4,3,2,1,0:T(8,128)(2,1)}) custom-call(bf16[32,128,512]{2,1,0:T(8,128)(2,1)S(1)} %all_to_all.11.in_ref), custom_call_target="tpu_custom_call" | custom-call | tf_op jit(solution)/shard_map/unpack/pallas_call | solution.py:170
Async XLA Ops:
  0.6 2.7 %copy-start.1 = (bf16[2,1,4,256,512]{4,3,2,1,0:T(8,128)(2,1)S(1)}, bf16[2,1,4,256,512]{4,3,2,1,0:T(8,128)(2,1)}, u32[]{:S(2)}) copy-start(bf16[2,1,4,256,512]{4,3,2,1,0:T(8,128)(2,1)} %greater_ref.1) | copy-start | bytes 6291460
  0.6 2.7 %copy-start = (bf16[2,1,4,256,512]{4,3,2,1,0:T(8,128)(2,1)S(1)}, bf16[2,1,4,256,512]{4,3,2,1,0:T(8,128)(2,1)}, u32[]{:S(2)}) copy-start(bf16[2,1,4,256,512]{4,3,2,1,0:T(8,128)(2,1)} %lesser_ref.1) | copy-start | bytes 6291460

commit v17 on v15

--- a/solution.py
+++ b/solution.py
@@ -11,7 +11,7 @@
 SMAX = 2
 TILE = 16
 VMEM_BYTES = 32 * 1024 * 1024
-AXES = ("grp", "mom")
+AXES = ("grp", "near", "half")
 
 
 def turned(states, rows, back):
@@ -80,8 +80,7 @@
     occupation, shift, region = (
         small_ref[at : at + 1, :] for at in range(regions * modes, regions * modes + 3)
     )
-    place = lax.axis_index("grp") * shares + lax.axis_index("mom")
-    greater = lax.div(place, jnp.int32(groups * shares // 2)).astype(jnp.float32)
+    greater = lax.axis_index("grp").astype(jnp.float32)
     chosen = jnp.zeros((modes, points), jnp.float32)
     for at in range(regions):
         here = region[:, 0:1] == float(at)
@@ -109,7 +108,8 @@
     at = lax.broadcasted_iota(jnp.int32, (size, 1), 0)
     device, energy = at >> (states.bit_length() - 1), (at & (states - 1)) >> (momenta.bit_length() - 1)
     energy = (device >> (shares.bit_length() - 1)) * energies + energy
-    state = (energy * shares + (device & (shares - 1))) * momenta + (at & (momenta - 1))
+    share = ((device & 1) * (shares // 2)) + ((device & (shares - 1)) >> 1)
+    state = (energy * shares + share) * momenta + (at & (momenta - 1))
     pick = state == lax.broadcasted_iota(jnp.int32, (size, levels * points), 1)
     pick = jnp.where(pick, 1.0, 0.0).astype(jnp.bfloat16)
     half = jnp.dot(pick, plain, preferred_element_type=jnp.float32).astype(jnp.bfloat16)
@@ -285,10 +285,10 @@
     return (jnp.concatenate([real_part, imag_part], axis=-1) * (1.0 / points)).astype(jnp.bfloat16)
 
 
-def by_groups(lesser, greater, coupling, occupation, shift, region_map):
+def by_groups(lesser, greater, coupling, occupation, shift, region_map, momentum):
     stacked = jnp.stack([lesser, greater])
     widened = with_halo(stacked, (("grp", 1),), SMAX)
-    regrouped = lax.all_to_all(widened, "mom", split_axis=4, concat_axis=3, tiled=True)
+    regrouped = lax.all_to_all(widened, momentum, split_axis=4, concat_axis=3, tiled=True)
     points = regrouped.shape[3]
     basis = dft_basis(points)
     basis_low = basis.astype(jnp.bfloat16)
@@ -298,41 +298,38 @@
         hat_real, hat_imag, spec_real, spec_imag, occupation, shift, lesser.shape[0]
     )
     result = inverse(sigma_real, sigma_imag, basis_low)
-    returned = lax.all_to_all(result, "mom", split_axis=3, concat_axis=4, tiled=True)
+    returned = lax.all_to_all(result, momentum, split_axis=3, concat_axis=4, tiled=True)
     return (returned[0], returned[1])
 
 
-def on_device(groups, shares, lesser, greater, coupling, occupation, shift, region_map):
-    energies, blocks, momenta, height, columns = lesser.shape
-    devices = groups * shares
-    states = energies * momenta
-    whole_tiles = (
-        blocks == 1
-        and devices >= 4
-        and devices & (devices - 1) == 0
-        and height % (TILE * (devices // 2)) == 0
-        and TILE % states == 0
+def whole_tiles(shape, groups, shares):
+    energies, blocks, momenta, height, columns = shape
+    return (
+        groups == 2
+        and shares >= 8
+        and shares & (shares - 1) == 0
+        and blocks == 1
+        and height == TILE * shares
+        and TILE % (energies * momenta) == 0
         and columns % 128 == 0
     )
-    if whole_tiles:
-        return by_rows(
-            lesser, greater, coupling, occupation, shift, region_map, groups, shares
-        )
-    return by_groups(lesser, greater, coupling, occupation, shift, region_map)
 
 
 def solution(mesh):
+    groups, shares = mesh.shape["grp"], mesh.shape["mom"]
+    momentum = ("half", "near")
+    split = jax.sharding.Mesh(mesh.devices.reshape(groups, 2, shares // 2), ("grp",) + momentum)
+
+    def on_device(lesser, *rest):
+        if whole_tiles(lesser.shape, groups, shares):
+            return by_rows(lesser, *rest, groups, shares)
+        return by_groups(lesser, *rest, momentum)
+
+    slab = P("grp", None, momentum, None, None)
     return jax.shard_map(
-        functools.partial(on_device, mesh.shape["grp"], mesh.shape["mom"]),
-        mesh=mesh,
-        in_specs=(
-            P("grp", None, "mom", None, None),
-            P("grp", None, "mom", None, None),
-            P(),
-            P(),
-            P(),
-            P(),
-        ),
-        out_specs=(P("grp", None, "mom", None, None), P("grp", None, "mom", None, None)),
+        on_device,
+        mesh=split,
+        in_specs=(slab, slab, P(), P(), P(), P()),
+        out_specs=(slab, slab),
         check_vma=False,
     )

time: 207 us -> 207 us (level)
  no operation moved by 1% of the time
where the time goes in v17:
time: 207 us; the launch traced here: 205 us
  blocking collectives  197 us (95%)
  Pallas kernels  5.55 us (3%)
    all_to_all x2, blocking collectives, exchange(): return lax.all_to_all(array, AXES, split_axis=0, concat_axis=0, tiled=True)  197 us

profile of v17, /device:TPU:0, one launch (start us, length us, event | category | flops | bytes accessed | tf_op | source)
XLA Modules:
  0.0 205.3 jit_solution(13619980184805284668)
XLA Ops:
  0.6 0.0 copy-start.1
  0.6 0.0 copy-start
  1.4 1.2 convert_add_fusion.small_ref
  2.6 0.7 build.1.matrix_ref
  3.3 0.0 copy-done.1
  3.3 0.0 copy-done
  3.3 1.2 pack.1
  4.6 99.8 %all_to_all.10.in_ref = bf16[32,128,512]{2,1,0:T(8,128)(2,1)S(1)} all-to-all(bf16[32,128,512]{2,1,0:T(8,128)(2,1)S(1)} %pack.1), channel_id=1, replica_groups=mesh['grp'=2,'half'=2,'near'=8] {'grp','near','half'}, dimensions={0} | all-to-all | bytes 8388608 | tf_op jit(solution)/shard_map/all_to_all | solution.py:192
  104.4 1.3 mix.1
  105.7 97.2 %all_to_all.11.in_ref = bf16[32,128,512]{2,1,0:T(8,128)(2,1)S(1)} all-to-all(bf16[32,128,512]{2,1,0:T(8,128)(2,1)S(1)} %mix.1), channel_id=1, replica_groups=mesh['grp'=2,'half'=2,'near'=8] {'grp','near','half'}, dimensions={0} | all-to-all | bytes 8388608 | tf_op jit(solution)/shard_map/all_to_all | solution.py:192
  202.9 2.4 %unpack.1 = (bf16[2,1,4,256,512]{4,3,2,1,0:T(8,128)(2,1)}, bf16[2,1,4,256,512]{4,3,2,1,0:T(8,128)(2,1)}) custom-call(bf16[32,128,512]{2,1,0:T(8,128)(2,1)S(1)} %all_to_all.11.in_ref), custom_call_target="tpu_custom_call" | custom-call | tf_op jit(solution)/shard_map/unpack/pallas_call | solution.py:166
Async XLA Ops:
  0.6 2.7 %copy-start.1 = (bf16[2,1,4,256,512]{4,3,2,1,0:T(8,128)(2,1)S(1)}, bf16[2,1,4,256,512]{4,3,2,1,0:T(8,128)(2,1)}, u32[]{:S(2)}) copy-start(bf16[2,1,4,256,512]{4,3,2,1,0:T(8,128)(2,1)} %greater_ref.1) | copy-start | bytes 6291460
  0.6 2.7 %copy-start = (bf16[2,1,4,256,512]{4,3,2,1,0:T(8,128)(2,1)S(1)}, bf16[2,1,4,256,512]{4,3,2,1,0:T(8,128)(2,1)}, u32[]{:S(2)}) copy-start(bf16[2,1,4,256,512]{4,3,2,1,0:T(8,128)(2,1)} %lesser_ref.1) | copy-start | bytes 6291460

commit v18 on v15

--- a/solution.py
+++ b/solution.py
@@ -170,7 +170,7 @@
         out_specs=(SLABS, SLABS),
         scratch_shapes=[
             pltpu.VMEM((2, energies, momenta, pieces * rows, columns), packed.dtype),
-            pltpu.SemaphoreType.DMA((2, math.gcd(pieces, 4))),
+            pltpu.SemaphoreType.DMA((2, math.gcd(pieces, 8))),
         ],
         compiler_params=params(),
         name="unpack",

time: 207 us -> 207 us (level)
  no operation moved by 1% of the time
where the time goes in v18:
time: 207 us; the launch traced here: 206 us
  blocking collectives  198 us (96%)
  Pallas kernels  5.53 us (3%)
    all_to_all x2, blocking collectives, exchange(): return lax.all_to_all(array, AXES, split_axis=0, concat_axis=0, tiled=True)  198 us

profile of v18, /device:TPU:0, one launch (start us, length us, event | category | flops | bytes accessed | tf_op | source)
XLA Modules:
  0.0 206.4 jit_solution(2509949734131480879)
XLA Ops:
  0.6 0.0 copy-start.1
  0.6 0.0 copy-start
  1.4 1.2 convert_add_fusion.small_ref
  2.6 0.7 build.1.matrix_ref
  3.3 0.0 copy-done.1
  3.3 0.0 copy-done
  3.3 1.2 pack.1
  4.6 101.8 %all_to_all.10.in_ref = bf16[32,128,512]{2,1,0:T(8,128)(2,1)S(1)} all-to-all(bf16[32,128,512]{2,1,0:T(8,128)(2,1)S(1)} %pack.1), channel_id=1, replica_groups=mesh['grp'=2,'mom'=16] {'grp','mom'}, dimensions={0} | all-to-all | bytes 8388608 | tf_op jit(solution)/shard_map/all_to_all | solution.py:192
  106.4 1.3 mix.1
  107.6 96.4 %all_to_all.11.in_ref = bf16[32,128,512]{2,1,0:T(8,128)(2,1)S(1)} all-to-all(bf16[32,128,512]{2,1,0:T(8,128)(2,1)S(1)} %mix.1), channel_id=1, replica_groups=mesh['grp'=2,'mom'=16] {'grp','mom'}, dimensions={0} | all-to-all | bytes 8388608 | tf_op jit(solution)/shard_map/all_to_all | solution.py:192
  204.1 2.3 %unpack.1 = (bf16[2,1,4,256,512]{4,3,2,1,0:T(8,128)(2,1)}, bf16[2,1,4,256,512]{4,3,2,1,0:T(8,128)(2,1)}) custom-call(bf16[32,128,512]{2,1,0:T(8,128)(2,1)S(1)} %all_to_all.11.in_ref), custom_call_target="tpu_custom_call" | custom-call | tf_op jit(solution)/shard_map/unpack/pallas_call | solution.py:166
Async XLA Ops:
  0.6 2.7 %copy-start.1 = (bf16[2,1,4,256,512]{4,3,2,1,0:T(8,128)(2,1)S(1)}, bf16[2,1,4,256,512]{4,3,2,1,0:T(8,128)(2,1)}, u32[]{:S(2)}) copy-start(bf16[2,1,4,256,512]{4,3,2,1,0:T(8,128)(2,1)} %greater_ref.1) | copy-start | bytes 6291460
  0.6 2.7 %copy-start = (bf16[2,1,4,256,512]{4,3,2,1,0:T(8,128)(2,1)S(1)}, bf16[2,1,4,256,512]{4,3,2,1,0:T(8,128)(2,1)}, u32[]{:S(2)}) copy-start(bf16[2,1,4,256,512]{4,3,2,1,0:T(8,128)(2,1)} %lesser_ref.1) | copy-start | bytes 6291460
